TPU v7x, 128 devices: a whole 4x4x4 slice. The times are simulated.
128 devices in a mesh: row: 8 (over z, core), col: 16 (over x, y).
Axes of the slice: x: 4, y: 4, z: 4, core: 2. Of those that a mesh axis runs over, the one named last changes fastest.
Arguments:
- scans: float32 [16384, 4, 8, 128], P(('row', 'col')), may hold values from -6 to 6
- dest: int32 [16384, 1], P(('row', 'col')), may hold values from 0 to 127; in each aligned block of 128 rows (0 to 127, 128 to 255, ...) at most 2 rows name the same one
- offsets: int32 [16384], P(('row', 'col')), may hold values from 0 to 252
- profile_index: int32 [16384], P(('row', 'col')), may hold values from 0 to 15
- profiles: float32 [16, 4, 128], replicated, may hold values from 0.1 to 1.5
- embed_weight: bfloat16 [512, 1024], replicated, may hold values from -0.25 to 0.25
- attn_gain: float32 [2, 1024], replicated, may hold values from 0.1 to 1.9
- qkv_weight: bfloat16 [2, 1024, 3072], replicated, may hold values from -3 to 3
- out_weight: bfloat16 [2, 1024, 1024], replicated, may hold values from -0.1875 to 0.1875
Outputs:
- tokens: bfloat16 [256, 256, 1024], P('row', 'col')
Inputs may be any that keep to these rules, and one draw needn't show every extreme that they name: dest[b, 0] is the tile of block b, numbered 16 * tile row + tile column; of the 128 blocks of one device at most 2 go to any one tile.
All inputs are finite; a program needn't handle non-finite values.
Results may differ from a plain program's by a relative error of at most 0.012.
Values may be sent and summed in bfloat16 or wider, within the bound.
No kernel may reach another device: no remote copies, remote signals or barrier semaphores. Data moves between devices by JAX's collectives and lax.ppermute only.
A program may use at most 128 MiB of HBM per device.

v0:
```python
import functools

import jax
import jax.numpy as jnp
from jax import lax
from jax.experimental import pallas as pl
from jax.experimental.pallas import tpu as pltpu
from jax.sharding import PartitionSpec as P

HEADS = 16
RADIUS = 4
TOK_H = 32
TOK_W = 16
BR = 4
CH = 8
MODEL = 1024
PATCH = 512
GRP = 128
FULL = 160
HALO = 16
EDGE = 4 * HALO
META = 128
VMEM_BYTES = 50 * 1024 * 1024

f32 = jnp.float32
bf16 = jnp.bfloat16
i32 = jnp.int32


def dot(a, b):
    return lax.dot_general(a, b, (((1,), (0,)), ((), ())), preferred_element_type=f32)


def dot_nt(a, b):
    return lax.dot_general(a, b, (((1,), (1,)), ((), ())), preferred_element_type=f32)


def iota(shape, dim):
    return lax.broadcasted_iota(i32, shape, dim)


def onehot(cond):
    return jnp.where(cond, 1.0, 0.0).astype(bf16)


def halves(x):
    high = x.astype(bf16)
    return high, (x - high.astype(f32)).astype(bf16)


def pack_kernel(dest_ref, offs_ref, pidx_ref, prof_ref, scans_ref, out_ref, w_ref):
    count = dest_ref.shape[0]
    eye = iota((count, count), 0) == iota((count, count), 1)
    dest_col = dest_ref[...].astype(f32)
    dest_row = jnp.sum(jnp.where(eye, dest_col, 0.0), axis=0, keepdims=True)
    before = iota((count, count), 0) < iota((count, count), 1)
    same = (dest_col == dest_row) & before
    rank = jnp.sum(jnp.where(same, 1.0, 0.0), axis=0, keepdims=True)
    slot = dest_row * (2.0 * BR) + rank * float(BR)
    offs_col = jnp.sum(jnp.where(eye, offs_ref[...].astype(f32), 0.0), axis=1, keepdims=True)
    pidx_col = jnp.sum(jnp.where(eye, pidx_ref[...].astype(f32), 0.0), axis=1, keepdims=True)
    chosen = onehot(pidx_col == iota((count, prof_ref.shape[0]), 1).astype(f32))
    lane = iota((count, META), 1)
    meta = jnp.where(lane == 0, offs_col, jnp.where(lane == 1, pidx_col, 1.0)).astype(bf16)
    for k in range(BR):
        high, low = halves(prof_ref[:, k, :])
        weight = dot(chosen, high) + dot(chosen, low)
        for c in range(CH):
            block = scans_ref[pl.ds(k * CH + c, count, stride=BR * CH), :]
            w_ref[k * count : (k + 1) * count, c * 128 : (c + 1) * 128] = (block * weight).astype(
                bf16
            )
        w_ref[k * count : (k + 1) * count, CH * 128 :] = meta
    rows = out_ref.shape[0]
    slots = jnp.concatenate([slot + float(k) for k in range(BR)], axis=1)
    step = 256
    for r in range(0, rows, step):
        here = (iota((step, BR * count), 0) + r).astype(f32)
        placing = onehot(here == slots)
        out_ref[r : r + step, :] = dot(placing, w_ref[...]).astype(bf16)


def pack(dest, offsets, profile_index, profiles, scans):
    count = scans.shape[0]
    rows = count * 2 * BR
    return pl.pallas_call(
        pack_kernel,
        out_shape=jax.ShapeDtypeStruct((rows, CH * 128 + META), bf16),
        scratch_shapes=[pltpu.VMEM((BR * count, CH * 128 + META), bf16)],
        compiler_params=pltpu.CompilerParams(vmem_limit_bytes=VMEM_BYTES),
        name="pack",
    )(
        dest,
        offsets.reshape(1, count),
        profile_index.reshape(1, count),
        profiles,
        scans.reshape(count * BR * CH, 128),
    )


def merge_kernel(pay_ref, prof_ref, x_ref, top_ref, bot_ref, mg_ref, y_ref, xg_ref):
    rows = pay_ref.shape[0]
    pick = onehot(iota((8, META), 0) == iota((8, META), 1))
    fields = dot_nt(pick, pay_ref[:, CH * 128 :])
    offs = fields[0:1, :]
    pidx = fields[1:2, :]
    valid = fields[2:3, :]
    strip = (iota((1, rows), 1) % BR).astype(f32)
    land = jnp.where(valid > 0.5, offs + strip, 4096.0)
    kind = pidx + 16.0 * strip
    r = iota((TOK_H * 8, rows), 0)
    pixel = (r % TOK_H) * 8 + r // TOK_H
    placing = onehot(pixel.astype(f32) == land)
    kinds = onehot(iota((16 * BR, rows), 0).astype(f32) == kind)
    counts = dot_nt(placing, kinds).astype(bf16)
    table = jnp.concatenate([prof_ref[:, k, :] for k in range(BR)], axis=0)
    high, low = halves(table)
    scale = 1.0 / (1.0 + dot(counts, high) + dot(counts, low))
    for c in range(CH):
        part = dot(placing, pay_ref[:, c * 128 : (c + 1) * 128])
        mg_ref[:, c * 128 : (c + 1) * 128] = (part * scale).astype(bf16)
    width = CH * 128
    step = 256
    for n in range(0, width, step):
        source = iota((width, step), 0)
        to = iota((width, step), 1) + n
        wanted = (to // 8 % CH) * 128 + (to // 64) * 8 + to % 8
        y_ref[:, n : n + step] = dot(mg_ref[...], onehot(source == wanted))
    low_half = iota((TOK_H, 128), 1) < 64
    order = iota((GRP, GRP), 1)
    want = iota((GRP, GRP), 0)
    reorder = onehot(order == (want % 4) * TOK_H + want // 4)
    for g in range(4):
        for jj in range(4):
            j = 4 * g + jj
            tile = (j // 2) * 128
            for pp in range(4):
                a = y_ref[2 * pp * TOK_H : (2 * pp + 1) * TOK_H, tile : tile + 128]
                b = y_ref[(2 * pp + 1) * TOK_H : (2 * pp + 2) * TOK_H, tile : tile + 128]
                if j % 2 == 0:
                    piece = jnp.where(low_half, a, pltpu.roll(b, 64, 1))
                else:
                    piece = jnp.where(low_half, pltpu.roll(a, 64, 1), b)
                xg_ref[jj * TOK_H : (jj + 1) * TOK_H, pp * 128 : (pp + 1) * 128] = piece.astype(
                    bf16
                )
        tokens = dot(reorder, xg_ref[...]).astype(bf16)
        x_ref[g * GRP : (g + 1) * GRP, :] = tokens
        top_ref[g * HALO : (g + 1) * HALO, :] = tokens[:HALO, :]
        bot_ref[g * HALO : (g + 1) * HALO, :] = tokens[GRP - HALO :, :]


def merge(payload, profiles):
    return pl.pallas_call(
        merge_kernel,
        out_shape=[
            jax.ShapeDtypeStruct((4 * GRP, PATCH), bf16),
            jax.ShapeDtypeStruct((EDGE, PATCH), bf16),
            jax.ShapeDtypeStruct((EDGE, PATCH), bf16),
        ],
        scratch_shapes=[
            pltpu.VMEM((TOK_H * 8, CH * 128), bf16),
            pltpu.VMEM((TOK_H * 8, CH * 128), f32),
            pltpu.VMEM((GRP, PATCH), bf16),
        ],
        compiler_params=pltpu.CompilerParams(vmem_limit_bytes=VMEM_BYTES),
        name="merge",
    )(payload, profiles)


def normed(stream, gain):
    centre = jnp.mean(stream, -1, keepdims=True)
    moved = stream - centre
    spread = jnp.mean(jnp.square(moved), -1, keepdims=True)
    return (moved * lax.rsqrt(spread + 1e-05) * gain).astype(bf16)


def own_kernel(layer, *refs):
    if layer == 0:
        x_ref, embed_ref, gain_ref, w_ref, stream_ref, qkv_ref, w_vmem, sem, inp_ref = refs
    else:
        x_ref, w_ref, qkv_ref, w_vmem, sem = refs
        inp_ref = x_ref
    copies = [
        pltpu.make_async_copy(
            w_ref.at[layer, :, pl.ds(n * MODEL, MODEL)], w_vmem.at[n], sem.at[n]
        )
        for n in range(3)
    ]
    for copy in copies:
        copy.start()
    if layer == 0:
        for r in range(0, 4 * GRP, GRP):
            stream = dot(x_ref[r : r + GRP, :], embed_ref[...])
            stream_ref[r : r + GRP, :] = stream
            inp_ref[r : r + GRP, :] = normed(stream, gain_ref[0:1, :])
    step = 256
    for n in range(3):
        copies[n].wait()
        for m in range(0, MODEL, step):
            part = dot(inp_ref[...], w_vmem[n, :, m : m + step]).astype(bf16)
            if n == 0:
                part = part * jnp.asarray(0.125, bf16)
            qkv_ref[:, n * MODEL + m : n * MODEL + m + step] = part


def own_part(layer, x, embed, gain, qkv_weight):
    any_spec = pl.BlockSpec(memory_space=pl.ANY)
    vmem = pl.BlockSpec(memory_space=pltpu.VMEM)
    qkv = jax.ShapeDtypeStruct((4 * GRP, 3 * MODEL), bf16)
    scratch = [pltpu.VMEM((3, MODEL, MODEL), bf16), pltpu.SemaphoreType.DMA((3,))]
    params = pltpu.CompilerParams(vmem_limit_bytes=VMEM_BYTES)
    cost = pl.CostEstimate(
        flops=2 * 4 * GRP * MODEL * 3 * MODEL, bytes_accessed=12 << 20, transcendentals=0
    )
    if layer == 0:
        return pl.pallas_call(
            functools.partial(own_kernel, layer),
            out_shape=[jax.ShapeDtypeStruct((4 * GRP, MODEL), f32), qkv],
            in_specs=[vmem, vmem, vmem, any_spec],
            scratch_shapes=scratch + [pltpu.VMEM((4 * GRP, MODEL), bf16)],
            compiler_params=params,
            cost_estimate=cost,
            name="own0",
        )(x, embed, gain, qkv_weight)
    return pl.pallas_call(
        functools.partial(own_kernel, layer),
        out_shape=qkv,
        in_specs=[vmem, any_spec],
        scratch_shapes=scratch,
        compiler_params=params,
        cost_estimate=cost,
        name="own1",
    )(x, qkv_weight)


def attend_kernel(layer, *refs):
    if layer == 0:
        (place_ref, top_ref, bot_ref, left_ref, right_ref, stream_ref, qkv_ref, gain_ref, embed_ref,
         w_ref, o_ref, out_ref, x_ref, xt_ref, xb_ref,
         w_vmem, o_vmem, sem, halo_ref, kv_ref, att_ref) = refs
    else:
        (place_ref, top_ref, bot_ref, left_ref, right_ref, stream_ref, qkv_ref,
         w_ref, o_ref, out_ref,
         w_vmem, o_vmem, sem, halo_ref, kv_ref, att_ref) = refs
    copies = [
        pltpu.make_async_copy(
            w_ref.at[layer, :, pl.ds((n + 1) * MODEL, MODEL)], w_vmem.at[n], sem.at[n]
        )
        for n in range(2)
    ]
    copies.append(pltpu.make_async_copy(o_ref.at[layer], o_vmem, sem.at[2]))
    for copy in copies:
        copy.start()
    row = 0
    for ref in (top_ref, bot_ref, left_ref, right_ref):
        part = ref[...]
        if layer == 0:
            part = normed(dot(part, embed_ref[...]), gain_ref[0:1, :])
        halo_ref[row : row + ref.shape[0], :] = part
        row += ref.shape[0]
    for g in range(4):
        at = (g + 1) * FULL + HALO
        kv_ref[at : at + GRP, :] = qkv_ref[g * GRP : (g + 1) * GRP, MODEL:]
    step = 256
    for n in range(2):
        copies[n].wait()
        for m in range(0, MODEL, step):
            part = dot(halo_ref[...], w_vmem[n, :, m : m + step]).astype(bf16)
            lanes = slice(n * MODEL + m, n * MODEL + m + step)
            for g in range(4):
                at = (g + 1) * FULL
                kv_ref[at : at + HALO, lanes] = part[g * HALO : (g + 1) * HALO, :]
                kv_ref[at + HALO + GRP : at + FULL, lanes] = part[
                    EDGE + g * HALO : EDGE + (g + 1) * HALO, :
                ]
            kv_ref[0:FULL, lanes] = part[2 * EDGE : 2 * EDGE + FULL, :]
            kv_ref[5 * FULL : 6 * FULL, lanes] = part[2 * EDGE + FULL :, :]

    query = iota((64, 256), 0)
    key = iota((64, 256), 1)
    row_gap = (key % 64) // 4 - 4 - (query % 32) // 4
    col_gap = (key // 64 - 1) * 4 + key % 4 - (query // 32) * 4 - query % 4
    near = (jnp.abs(row_gap) <= RADIUS) & (jnp.abs(col_gap) <= RADIUS)
    near_bias = jnp.where(near, 0.0, -1e30)
    lane_key = iota((1, 256), 1)
    key_row = (lane_key % 64) // 4 - 4
    key_col = (lane_key // 64 - 1) * 4 + lane_key % 4
    low_half = iota((64, 128), 1) < 64
    zero = jnp.zeros((64, 128), bf16)
    ones = jnp.ones((256, 128), bf16)
    height, width = place_ref[2], place_ref[3]

    def block(b, carry):
        bi, bj = b // 2, b % 2
        at_row = key_row + bi * 8 + place_ref[0]
        at_col = key_col + bj * 8 + place_ref[1]
        inside = (at_row >= 0) & (at_row < height) & (at_col >= 0) & (at_col < width)
        bias = near_bias + jnp.where(inside, 0.0, -1e30)
        bias = jnp.concatenate([bias, bias], axis=0)
        q_rows = [pl.multiple_of((2 * bj + g) * GRP + bi * 32, 32) for g in range(2)]
        k_rows = [pl.multiple_of((2 * bj + g) * FULL + bi * 32, 32) for g in range(4)]
        for h in range(HEADS // 2):
            lanes = slice(h * 128, (h + 1) * 128)
            q = jnp.concatenate([qkv_ref[pl.ds(r, 32), lanes] for r in q_rows], axis=0)
            q = jnp.concatenate([jnp.where(low_half, q, zero), jnp.where(low_half, zero, q)], axis=0)
            k = jnp.concatenate([kv_ref[pl.ds(r, 64), lanes] for r in k_rows], axis=0)
            v_lanes = slice(MODEL + h * 128, MODEL + (h + 1) * 128)
            v = jnp.concatenate([kv_ref[pl.ds(r, 64), v_lanes] for r in k_rows], axis=0)
            logits = dot_nt(q, k) + bias
            top = jnp.max(logits, axis=-1, keepdims=True)
            share = jnp.exp(logits - top).astype(bf16)
            both = dot(share, jnp.concatenate([v, ones], axis=1))
            mixed = both[:, :128] / both[:, 128:]
            picked = jnp.where(low_half, mixed[:64, :], mixed[64:, :]).astype(bf16)
            for g in range(2):
                att_ref[pl.ds(q_rows[g], 32), lanes] = picked[g * 32 : (g + 1) * 32, :]
        return carry

    lax.fori_loop(0, 8, block, 0)

    copies[2].wait()
    if layer == 0:
        for g in range(4):
            rows = slice(g * GRP, (g + 1) * GRP)
            stream = stream_ref[rows, :] + dot(att_ref[rows, :], o_vmem[...])
            out_ref[rows, :] = stream
            inputs = normed(stream, gain_ref[1:2, :])
            x_ref[rows, :] = inputs
            xt_ref[g * HALO : (g + 1) * HALO, :] = inputs[:HALO, :]
            xb_ref[g * HALO : (g + 1) * HALO, :] = inputs[GRP - HALO :, :]
    else:
        for g in range(4):
            rows = slice(g * GRP, (g + 1) * GRP)
            stream = stream_ref[rows, :] + dot(att_ref[rows, :], o_vmem[...])
            att_ref[rows, :] = stream.astype(bf16)
        for r in range(0, 4 * GRP, GRP):
            to = iota((GRP, 4 * GRP), 0) + r
            source = iota((GRP, 4 * GRP), 1)
            wanted = (to // 4 % 4) * GRP + (to // 16) * 4 + to % 4
            out_ref[r : r + GRP, :] = dot(onehot(source == wanted), att_ref[...]).astype(bf16)


def attend(layer, place, halos, stream, qkv, gain, embed, qkv_weight, out_weight):
    any_spec = pl.BlockSpec(memory_space=pl.ANY)
    vmem = pl.BlockSpec(memory_space=pltpu.VMEM)
    smem = pl.BlockSpec(memory_space=pltpu.SMEM)
    operands = [place, *halos, stream, qkv]
    specs = [smem] + [vmem] * 6
    if layer == 0:
        operands += [gain, embed]
        specs += [vmem, vmem]
        out_shape = [
            jax.ShapeDtypeStruct((4 * GRP, MODEL), f32),
            jax.ShapeDtypeStruct((4 * GRP, MODEL), bf16),
            jax.ShapeDtypeStruct((EDGE, MODEL), bf16),
            jax.ShapeDtypeStruct((EDGE, MODEL), bf16),
        ]
    else:
        out_shape = jax.ShapeDtypeStruct((4 * GRP, MODEL), bf16)
    operands += [qkv_weight, out_weight]
    specs += [any_spec, any_spec]
    return pl.pallas_call(
        functools.partial(attend_kernel, layer),
        out_shape=out_shape,
        in_specs=specs,
        scratch_shapes=[
            pltpu.VMEM((2, MODEL, MODEL), bf16),
            pltpu.VMEM((MODEL, MODEL), bf16),
            pltpu.SemaphoreType.DMA((3,)),
            pltpu.VMEM((2 * EDGE + 2 * FULL, MODEL), bf16),
            pltpu.VMEM((6 * FULL, 2 * MODEL), bf16),
            pltpu.VMEM((4 * GRP, MODEL), bf16),
        ],
        compiler_params=pltpu.CompilerParams(vmem_limit_bytes=VMEM_BYTES),
        name="attend%d" % layer,
    )(*operands)


def shifted(cells, axis, by):
    count = lax.axis_size(axis)
    return lax.ppermute(cells, axis, [(i, (i + by) % count) for i in range(count)])


def around(x, first, last):
    top = shifted(last, "row", 1)
    bottom = shifted(first, "row", -1)
    right_edge = jnp.concatenate([top[3 * HALO :], x[3 * GRP :], bottom[3 * HALO :]], axis=0)
    left_edge = jnp.concatenate([top[:HALO], x[:GRP], bottom[:HALO]], axis=0)
    left = shifted(right_edge, "col", 1)
    right = shifted(left_edge, "col", -1)
    return top, bottom, left, right


def per_device(
    scans, dest, offsets, profile_index, profiles, embed_weight, attn_gain, qkv_weight, out_weight
):
    place = jnp.stack(
        [
            lax.axis_index("row") * TOK_H,
            lax.axis_index("col") * TOK_W,
            jnp.asarray(lax.axis_size("row") * TOK_H, i32),
            jnp.asarray(lax.axis_size("col") * TOK_W, i32),
        ]
    ).astype(i32)
    embed = embed_weight.reshape(CH, 8, 8, MODEL).transpose(1, 0, 2, 3).reshape(PATCH, MODEL)
    payload = pack(dest, offsets, profile_index, profiles, scans)
    payload = lax.all_to_all(payload, ("row", "col"), split_axis=0, concat_axis=0, tiled=True)
    x, first, last = merge(payload, profiles)
    halos = around(x, first, last)
    stream, qkv = own_part(0, x, embed, attn_gain, qkv_weight)
    stream, x, first, last = attend(
        0, place, halos, stream, qkv, attn_gain, embed, qkv_weight, out_weight
    )
    halos = around(x, first, last)
    qkv = own_part(1, x, None, None, qkv_weight)
    tokens = attend(1, place, halos, stream, qkv, None, None, qkv_weight, out_weight)
    return tokens.reshape(TOK_H, TOK_W, MODEL)


def solution(mesh):
    placed = (
        P(("row", "col"), None, None, None),
        P(("row", "col"), None),
        P(("row", "col")),
        P(("row", "col")),
        P(),
        P(),
        P(),
        P(),
        P(),
    )
    return jax.shard_map(
        per_device, mesh=mesh, in_specs=placed, out_specs=P("row", "col", None), check_vma=False
    )
```

profile of v0, /device:TPU:0, one launch (start us, length us, event | category | flops | bytes accessed | tf_op | source)
XLA Modules:
  0.0 121.5 jit_solution(9275811473598121547)
XLA Ops:
  0.0 0.8 copy.10.dest_ref
  0.8 0.0 copy-start.1
  0.8 1.6 %copy-done.1 = f32[128,4,8,128]{3,2,1,0:T(8,128)S(1)} copy-done((f32[128,4,8,128]{3,2,1,0:T(8,128)S(1)}, f32[128,4,8,128]{3,2,1,0:T(8,128)}, u32[]{:S(2)}) %copy-start.1) | copy-done | bytes 2097176
  2.4 0.0 copy-start.3
  2.4 0.8 copy-done.3
  3.1 0.0 copy-start.6
  3.1 0.7 copy-done.6
  3.8 0.0 copy-start.7
  3.8 0.7 copy-done.7
  4.4 4.4 %pack.1 = bf16[1024,1152]{1,0:T(8,128)(2,1)} custom-call(s32[128,1]{1,0:T(8,128)S(1)} %copy.10.dest_ref, s32[1,128]{1,0:T(1,128)S(1)} %bitcast.16, s32[1,128]{1,0:T(1,128)S(1)} %bitcast.17, f32[16,4,128]{2,1,0:T(4,128)S(1)} %copy-done.3, f32[4096,128]{1,0:T(8,128)S(1)} %bitcast.15), custom_call_target="tpu_custom_call" | custom-call | tf_op jit(solution)/shard_map/pack/pallas_call | solution.py:86
  8.8 0.0 copy-start.4
  8.8 11.1 %all-to-all-start = ((bf16[128,8,1152]{2,1,0:T(8,128)(2,1)}), bf16[128,8,1152]{2,1,0:T(8,128)(2,1)S(1)}, u32[]{:S(2)}, u32[]{:S(2)}) async-start(bf16[128,8,1152]{2,1,0:T(8,128)(2,1)} %bitcast.18), calls=%async_computation | async-start | bytes 4718592 | tf_op jit(solution)/shard_map/all_to_all | solution.py:408
  20.0 1.3 %copy.11 = bf16[8,8,8,1024]{3,2,0,1:T(8,128)(2,1)S(1)} copy(bf16[8,8,8,1024]{3,2,1,0:T(8,128)(2,1)} %bitcast.19) | data formatting | bytes 2097152 | tf_op jit(solution)/shard_map/reshape | solution.py:406
  21.3 0.0 copy-start.5
  21.3 0.1 pad_add_fusion.refs_0_
  21.4 31.1 %all-to-all-done = bf16[128,8,1152]{2,1,0:T(8,128)(2,1)S(1)} async-done(((bf16[128,8,1152]{2,1,0:T(8,128)(2,1)}), bf16[128,8,1152]{2,1,0:T(8,128)(2,1)S(1)}, u32[]{:S(2)}, u32[]{:S(2)}) %all-to-all-start) | async-done | bytes 2359328 | tf_op jit(solution)/shard_map/all_to_all | solution.py:408
  52.5 0.0 copy-done.4
  52.5 2.9 %merge.1 = (bf16[512,512]{1,0:T(8,128)(2,1)S(1)}, bf16[64,512]{1,0:T(8,128)(2,1)S(1)}, bf16[64,512]{1,0:T(8,128)(2,1)S(1)}) custom-call(bf16[1024,1152]{1,0:T(8,128)(2,1)S(1)} %bitcast.14, f32[16,4,128]{2,1,0:T(4,128)S(1)} %copy-done.4), custom_call_target="tpu_custom_call" | custom-call | tf_op jit(solution)/shard_map/merge/pallas_call | solution.py:154
  55.4 0.0 collective-permute-start
  55.4 2.9 %collective-permute-start.1 = (bf16[64,512]{1,0:T(8,128)(2,1)S(1)}, bf16[64,512]{1,0:T(8,128)(2,1)S(1)}, u32[]{:S(2)}, u32[]{:S(2)}) collective-permute-start(bf16[64,512]{1,0:T(8,128)(2,1)S(1)} %get-tuple-element.15), channel_id=1, source_target_pairs={{0,112},{16,0},{32,16},{48,32},{64,48},{80,64},{96,80},{112,96},{1... | collective-permute-start | bytes 196616 | tf_op jit(solution)/shard_map/ppermute | solution.py:382
  58.4 1.9 %collective-permute-done.refs_1_ = bf16[64,512]{1,0:T(8,128)(2,1)S(1)} collective-permute-done((bf16[64,512]{1,0:T(8,128)(2,1)S(1)}, bf16[64,512]{1,0:T(8,128)(2,1)S(1)}, u32[]{:S(2)}, u32[]{:S(2)}) %collective-permute-start) | collective-permute-done | bytes 65568 | tf_op jit(solution)/shard_map/ppermute | solution.py:382
  60.3 0.0 collective-permute-done.1.refs_2_
  60.3 0.9 collective-permute-start.2
  61.3 4.7 %collective-permute-start.3 = (bf16[160,512]{1,0:T(8,128)(2,1)S(1)}, bf16[160,512]{1,0:T(8,128)(2,1)S(1)}, u32[]{:S(2)}, u32[]{:S(2)}) collective-permute-start(bf16[160,512]{1,0:T(8,128)(2,1)S(1)} %pad_maximum_fusion.3), channel_id=1, source_target_pairs={{0,15},{1,0},{2,1},{3,2},{4,3},{5,4},{6,5},{7,6},{8,7},{9,8},{10,9... | collective-permute-start | bytes 491528 | tf_op jit(solution)/shard_map/ppermute | solution.py:382
  66.0 0.0 copy-done.5
  66.0 7.1 %own0.1 = (f32[512,1024]{1,0:T(8,128)S(1)}, bf16[512,3072]{1,0:T(8,128)(2,1)}) custom-call(bf16[512,512]{1,0:T(8,128)(2,1)S(1)} %get-tuple-element.16.refs_0_, bf16[512,1024]{1,0:T(8,128)(2,1)S(1)} %bitcast.12, f32[2,1024]{1,0:T(2,128)S(1)} %copy-done.5, bf16[2,1024,3072]{2,1,0:T(8,128)(2,1)} %refs_7_.3), custom_call_target="tpu_custom_call" | custom-call | flops 3221225472 | bytes 12582912 | tf_op jit(solution)/shard_map/own0/pallas_call | solution.py:217
  73.1 0.0 copy-start
  73.1 1.3 %copy-done = f32[512,1024]{1,0:T(8,128)} copy-done((f32[512,1024]{1,0:T(8,128)}, f32[512,1024]{1,0:T(8,128)S(1)}, u32[]{:S(2)}) %copy-start) | copy-done | bytes 2097176
  74.5 0.0 collective-permute-done.2.refs_3_
  74.5 0.0 collective-permute-done.3.refs_4_
  74.5 14.4 %attend0.1 = (f32[512,1024]{1,0:T(8,128)}, bf16[512,1024]{1,0:T(8,128)(2,1)S(1)}, bf16[64,1024]{1,0:T(8,128)(2,1)S(1)}, bf16[64,1024]{1,0:T(8,128)(2,1)S(1)}) custom-call(s32[4]{0:T(128)S(1)} %pad_add_fusion.refs_0_, bf16[64,512]{1,0:T(8,128)(2,1)S(1)} %collective-permute-done.refs_1_, bf16[64,512]{1,0:T(8,128)(2,1)S(1)} %collective-permute-done.1.refs_2_, ...), custom_call_target="tpu_custom_call" | custom-call | tf_op jit(solution)/shard_map/attend0/pallas_call | solution.py:363
  88.8 0.0 collective-permute-start.4
  88.9 2.9 %collective-permute-start.5 = (bf16[64,1024]{1,0:T(8,128)(2,1)S(1)}, bf16[64,1024]{1,0:T(8,128)(2,1)S(1)}, u32[]{:S(2)}, u32[]{:S(2)}) collective-permute-start(bf16[64,1024]{1,0:T(8,128)(2,1)S(1)} %get-tuple-element.20), channel_id=1, source_target_pairs={{0,112},{16,0},{32,16},{48,32},{64,48},{80,64},{96,80},{112,96},{1... | collective-permute-start | bytes 393224 | tf_op jit(solution)/shard_map/ppermute | solution.py:382
  91.8 2.6 %collective-permute-done.4.refs_1_ = bf16[64,1024]{1,0:T(8,128)(2,1)S(1)} collective-permute-done((bf16[64,1024]{1,0:T(8,128)(2,1)S(1)}, bf16[64,1024]{1,0:T(8,128)(2,1)S(1)}, u32[]{:S(2)}, u32[]{:S(2)}) %collective-permute-start.4) | collective-permute-done | bytes 131104 | tf_op jit(solution)/shard_map/ppermute | solution.py:382
  94.5 0.0 collective-permute-done.5.refs_2_
  94.5 0.1 collective-permute-start.6
  94.6 0.0 copy-start.2
  94.6 5.6 %collective-permute-start.7 = (bf16[160,1024]{1,0:T(8,128)(2,1)S(1)}, bf16[160,1024]{1,0:T(8,128)(2,1)S(1)}, u32[]{:S(2)}, u32[]{:S(2)}) collective-permute-start(bf16[160,1024]{1,0:T(8,128)(2,1)S(1)} %pad_maximum_fusion.1), channel_id=1, source_target_pairs={{0,15},{1,0},{2,1},{3,2},{4,3},{5,4},{6,5},{7,6},{8,7},{9,8},{10,9... | collective-permute-start | bytes 983048 | tf_op jit(solution)/shard_map/ppermute | solution.py:382
  100.3 7.1 %own1.1.refs_6_ = bf16[512,3072]{1,0:T(8,128)(2,1)} custom-call(bf16[512,1024]{1,0:T(8,128)(2,1)S(1)} %get-tuple-element.21.refs_0_, bf16[2,1024,3072]{2,1,0:T(8,128)(2,1)} %refs_7_.3), custom_call_target="tpu_custom_call" | custom-call | flops 3221225472 | bytes 12582912 | tf_op jit(solution)/shard_map/own1/pallas_call | solution.py:226
  107.4 0.0 collective-permute-done.6.refs_3_
  107.4 0.0 collective-permute-done.7.refs_4_
  107.4 0.0 copy-done.2
  107.4 14.0 %attend1.1 = bf16[512,1024]{1,0:T(8,128)(2,1)} custom-call(s32[4]{0:T(128)S(1)} %pad_add_fusion.refs_0_, bf16[64,1024]{1,0:T(8,128)(2,1)S(1)} %collective-permute-done.4.refs_1_, bf16[64,1024]{1,0:T(8,128)(2,1)S(1)} %collective-permute-done.5.refs_2_, bf16[160,1024]{1,0:T(8,128)(2,1)S(1)} %collective-permute-done.6.refs_3_, ...), custom_call_target="tpu_custom_call" | custom-call | tf_op jit(solution)/shard_map/attend1/pallas_call | solution.py:363
  (11 shorter events, 0.1 us)
Async XLA Ops:
  0.8 1.6 %copy-start.1 = (f32[128,4,8,128]{3,2,1,0:T(8,128)S(1)}, f32[128,4,8,128]{3,2,1,0:T(8,128)}, u32[]{:S(2)}) copy-start(f32[128,4,8,128]{3,2,1,0:T(8,128)} %param.9) | copy-start | bytes 6291460
  2.4 0.8 copy-start.3
  3.1 0.7 copy-start.6
  3.8 0.7 copy-start.7
  8.8 43.6 %copy-start.4 = (f32[16,4,128]{2,1,0:T(4,128)S(1)}, f32[16,4,128]{2,1,0:T(4,128)}, u32[]{:S(2)}) copy-start(f32[16,4,128]{2,1,0:T(4,128)} %prof_ref.3) | copy-start | bytes 98308
  8.8 43.6 %all-to-all-start = ((bf16[128,8,1152]{2,1,0:T(8,128)(2,1)}), bf16[128,8,1152]{2,1,0:T(8,128)(2,1)S(1)}, u32[]{:S(2)}, u32[]{:S(2)}) async-start(bf16[128,8,1152]{2,1,0:T(8,128)(2,1)} %bitcast.18), calls=%async_computation | async-start | bytes 4718592 | tf_op jit(solution)/shard_map/all_to_all | solution.py:408
  21.3 44.7 %copy-start.5 = (f32[2,1024]{1,0:T(2,128)S(1)}, f32[2,1024]{1,0:T(2,128)}, u32[]{:S(2)}) copy-start(f32[2,1024]{1,0:T(2,128)} %refs_7_.2) | copy-start | bytes 24580
  55.4 4.9 %collective-permute-start = (bf16[64,512]{1,0:T(8,128)(2,1)S(1)}, bf16[64,512]{1,0:T(8,128)(2,1)S(1)}, u32[]{:S(2)}, u32[]{:S(2)}) collective-permute-start(bf16[64,512]{1,0:T(8,128)(2,1)S(1)} %get-tuple-element.14), channel_id=1, source_target_pairs={{0,16},{16,32},{32,48},{48,64},{64,80},{80,96},{96,112},{112,0},{1... | collective-permute-start | bytes 196616 | tf_op jit(solution)/shard_map/ppermute | solution.py:382
  55.4 4.9 %collective-permute-start.1 = (bf16[64,512]{1,0:T(8,128)(2,1)S(1)}, bf16[64,512]{1,0:T(8,128)(2,1)S(1)}, u32[]{:S(2)}, u32[]{:S(2)}) collective-permute-start(bf16[64,512]{1,0:T(8,128)(2,1)S(1)} %get-tuple-element.15), channel_id=1, source_target_pairs={{0,112},{16,0},{32,16},{48,32},{64,48},{80,64},{96,80},{112,96},{1... | collective-permute-start | bytes 196616 | tf_op jit(solution)/shard_map/ppermute | solution.py:382
  60.3 14.1 %collective-permute-start.2 = (bf16[160,512]{1,0:T(8,128)(2,1)S(1)}, bf16[160,512]{1,0:T(8,128)(2,1)S(1)}, u32[]{:S(2)}, u32[]{:S(2)}) collective-permute-start(bf16[160,512]{1,0:T(8,128)(2,1)S(1)} %pad_maximum_fusion.2), channel_id=1, source_target_pairs={{0,1},{1,2},{2,3},{3,4},{4,5},{5,6},{6,7},{7,8},{8,9},{9,10},{10,1... | collective-permute-start | bytes 491528 | tf_op jit(solution)/shard_map/ppermute | solution.py:382
  61.3 13.2 %collective-permute-start.3 = (bf16[160,512]{1,0:T(8,128)(2,1)S(1)}, bf16[160,512]{1,0:T(8,128)(2,1)S(1)}, u32[]{:S(2)}, u32[]{:S(2)}) collective-permute-start(bf16[160,512]{1,0:T(8,128)(2,1)S(1)} %pad_maximum_fusion.3), channel_id=1, source_target_pairs={{0,15},{1,0},{2,1},{3,2},{4,3},{5,4},{6,5},{7,6},{8,7},{9,8},{10,9... | collective-permute-start | bytes 491528 | tf_op jit(solution)/shard_map/ppermute | solution.py:382
  73.1 1.3 %copy-start = (f32[512,1024]{1,0:T(8,128)}, f32[512,1024]{1,0:T(8,128)S(1)}, u32[]{:S(2)}) copy-start(f32[512,1024]{1,0:T(8,128)S(1)} %get-tuple-element.17.refs_5_) | copy-start | bytes 6291460
  88.8 5.6 %collective-permute-start.4 = (bf16[64,1024]{1,0:T(8,128)(2,1)S(1)}, bf16[64,1024]{1,0:T(8,128)(2,1)S(1)}, u32[]{:S(2)}, u32[]{:S(2)}) collective-permute-start(bf16[64,1024]{1,0:T(8,128)(2,1)S(1)} %get-tuple-element.19), channel_id=1, source_target_pairs={{0,16},{16,32},{32,48},{48,64},{64,80},{80,96},{96,112},{112,0},{1... | collective-permute-start | bytes 393224 | tf_op jit(solution)/shard_map/ppermute | solution.py:382
  88.9 5.6 %collective-permute-start.5 = (bf16[64,1024]{1,0:T(8,128)(2,1)S(1)}, bf16[64,1024]{1,0:T(8,128)(2,1)S(1)}, u32[]{:S(2)}, u32[]{:S(2)}) collective-permute-start(bf16[64,1024]{1,0:T(8,128)(2,1)S(1)} %get-tuple-element.20), channel_id=1, source_target_pairs={{0,112},{16,0},{32,16},{48,32},{64,48},{80,64},{96,80},{112,96},{1... | collective-permute-start | bytes 393224 | tf_op jit(solution)/shard_map/ppermute | solution.py:382
  94.5 12.8 %collective-permute-start.6 = (bf16[160,1024]{1,0:T(8,128)(2,1)S(1)}, bf16[160,1024]{1,0:T(8,128)(2,1)S(1)}, u32[]{:S(2)}, u32[]{:S(2)}) collective-permute-start(bf16[160,1024]{1,0:T(8,128)(2,1)S(1)} %pad_maximum_fusion), channel_id=1, source_target_pairs={{0,1},{1,2},{2,3},{3,4},{4,5},{5,6},{6,7},{7,8},{8,9},{9,10},{10,1... | collective-permute-start | bytes 983048 | tf_op jit(solution)/shard_map/ppermute | solution.py:382
  94.6 12.8 %copy-start.2 = (f32[512,1024]{1,0:T(8,128)S(1)}, f32[512,1024]{1,0:T(8,128)}, u32[]{:S(2)}) copy-start(f32[512,1024]{1,0:T(8,128)} %get-tuple-element.22.refs_5_) | copy-start | bytes 6291460
  94.6 12.7 %collective-permute-start.7 = (bf16[160,1024]{1,0:T(8,128)(2,1)S(1)}, bf16[160,1024]{1,0:T(8,128)(2,1)S(1)}, u32[]{:S(2)}, u32[]{:S(2)}) collective-permute-start(bf16[160,1024]{1,0:T(8,128)(2,1)S(1)} %pad_maximum_fusion.1), channel_id=1, source_target_pairs={{0,15},{1,0},{2,1},{3,2},{4,3},{5,4},{6,5},{7,6},{8,7},{9,8},{10,9... | collective-permute-start | bytes 983048 | tf_op jit(solution)/shard_map/ppermute | solution.py:382
where the time goes:
time: 122 us
  Pallas kernels  49.8 us (41%)
  waiting for transfers between devices  35.6 us (29%)
  starting transfers between devices  28.4 us (23%)
  local copies, waits for them, and re-layouts  7.13 us (6%)
    all_to_all x1, waiting for transfers between devices, per_device(): lax.all_to_all(payload, ('row', 'col'), split_axis=0, concat_axis=0, tile...  31.1 us
    pallas_call x2, Pallas kernels, attend(): pl.pallas_call(functools.partial(attend_kernel, layer), out_shape=out_sha...  28.3 us
    ppermute x8, starting transfers between devices, shifted(): lax.ppermute(cells, axis, [(i, (i + by) % count) for i in range(count)])  17.3 us
    all_to_all x1, starting transfers between devices, per_device(): lax.all_to_all(payload, ('row', 'col'), split_axis=0, concat_axis=0, tile...  11.1 us
    pallas_call x1, Pallas kernels, own_part(): pl.pallas_call(functools.partial(own_kernel, layer), out_shape=[jax.Shape...  7.13 us
    pallas_call x1, Pallas kernels, own_part(): pl.pallas_call(functools.partial(own_kernel, layer), out_shape=qkv, in_sp...  7.09 us
    unnamed x17, local copies, waits for them, and re-layouts  5.75 us
    ppermute x8, waiting for transfers between devices, shifted(): lax.ppermute(cells, axis, [(i, (i + by) % count) for i in range(count)])  4.55 us
  transfers between devices with their start and end apart: 9, of which 3 were waited for; matrix products, arithmetic and copies ran while one was open for 1% of the time, Pallas kernels for 12%

commit v1 on v0

--- a/solution.py
+++ b/solution.py
@@ -20,7 +20,8 @@
 HALO = 16
 EDGE = 4 * HALO
 META = 128
-VMEM_BYTES = 50 * 1024 * 1024
+CHUNKS = 4
+VMEM_BYTES = 20 * 1024 * 1024
 
 f32 = jnp.float32
 bf16 = jnp.bfloat16
@@ -48,11 +49,31 @@
     return high, (x - high.astype(f32)).astype(bf16)
 
 
-def pack_kernel(dest_ref, offs_ref, pidx_ref, prof_ref, scans_ref, out_ref, w_ref):
-    count = dest_ref.shape[0]
+def pack_kernel(
+    dest_hbm, offs_hbm, pidx_hbm, prof_hbm, scans_hbm, out_ref,
+    dest_ref, offs_ref, pidx_ref, prof_ref, scans_ref, w_ref, sem,
+):
+    count = dest_ref.shape[1]
+    chunk = scans_ref.shape[0] // CHUNKS
+    small = [
+        pltpu.make_async_copy(a, b, sem.at[n])
+        for n, (a, b) in enumerate(
+            [(dest_hbm, dest_ref), (offs_hbm, offs_ref), (pidx_hbm, pidx_ref), (prof_hbm, prof_ref)]
+        )
+    ]
+    large = [
+        pltpu.make_async_copy(
+            scans_hbm.at[pl.ds(n * chunk, chunk)], scans_ref.at[pl.ds(n * chunk, chunk)], sem.at[4 + n]
+        )
+        for n in range(CHUNKS)
+    ]
+    for copy in small + large:
+        copy.start()
+    for copy in small:
+        copy.wait()
     eye = iota((count, count), 0) == iota((count, count), 1)
-    dest_col = dest_ref[...].astype(f32)
-    dest_row = jnp.sum(jnp.where(eye, dest_col, 0.0), axis=0, keepdims=True)
+    dest_row = dest_ref[...].astype(f32)
+    dest_col = jnp.sum(jnp.where(eye, dest_row, 0.0), axis=1, keepdims=True)
     before = iota((count, count), 0) < iota((count, count), 1)
     same = (dest_col == dest_row) & before
     rank = jnp.sum(jnp.where(same, 1.0, 0.0), axis=0, keepdims=True)
@@ -62,15 +83,21 @@
     chosen = onehot(pidx_col == iota((count, prof_ref.shape[0]), 1).astype(f32))
     lane = iota((count, META), 1)
     meta = jnp.where(lane == 0, offs_col, jnp.where(lane == 1, pidx_col, 1.0)).astype(bf16)
+    weights = []
     for k in range(BR):
         high, low = halves(prof_ref[:, k, :])
-        weight = dot(chosen, high) + dot(chosen, low)
-        for c in range(CH):
-            block = scans_ref[pl.ds(k * CH + c, count, stride=BR * CH), :]
-            w_ref[k * count : (k + 1) * count, c * 128 : (c + 1) * 128] = (block * weight).astype(
-                bf16
-            )
+        weights.append(dot(chosen, high) + dot(chosen, low))
         w_ref[k * count : (k + 1) * count, CH * 128 :] = meta
+    some = count // CHUNKS
+    for n in range(CHUNKS):
+        large[n].wait()
+        for k in range(BR):
+            for c in range(CH):
+                block = scans_ref[pl.ds(n * chunk + k * CH + c, some, stride=BR * CH), :]
+                at = k * count + n * some
+                w_ref[at : at + some, c * 128 : (c + 1) * 128] = (
+                    block * weights[k][n * some : (n + 1) * some, :]
+                ).astype(bf16)
     rows = out_ref.shape[0]
     slots = jnp.concatenate([slot + float(k) for k in range(BR)], axis=1)
     step = 256
@@ -86,20 +113,46 @@
     return pl.pallas_call(
         pack_kernel,
         out_shape=jax.ShapeDtypeStruct((rows, CH * 128 + META), bf16),
-        scratch_shapes=[pltpu.VMEM((BR * count, CH * 128 + META), bf16)],
+        in_specs=[pl.BlockSpec(memory_space=pltpu.HBM)] * 5,
+        scratch_shapes=[
+            pltpu.VMEM((1, count), i32),
+            pltpu.VMEM((1, count), i32),
+            pltpu.VMEM((1, count), i32),
+            pltpu.VMEM(profiles.shape, f32),
+            pltpu.VMEM((count * BR * CH, 128), f32),
+            pltpu.VMEM((BR * count, CH * 128 + META), bf16),
+            pltpu.SemaphoreType.DMA((4 + CHUNKS,)),
+        ],
         compiler_params=pltpu.CompilerParams(vmem_limit_bytes=VMEM_BYTES),
         name="pack",
     )(
-        dest,
-        offsets.reshape(1, count),
-        profile_index.reshape(1, count),
-        profiles,
-        scans.reshape(count * BR * CH, 128),
+        in_hbm(dest.reshape(1, count)),
+        in_hbm(offsets.reshape(1, count)),
+        in_hbm(profile_index.reshape(1, count)),
+        in_hbm(profiles),
+        in_hbm(scans.reshape(count * BR * CH, 128)),
     )
 
 
-def merge_kernel(pay_ref, prof_ref, x_ref, top_ref, bot_ref, mg_ref, y_ref, xg_ref):
+def in_hbm(x):
+    return pltpu.with_memory_space_constraint(x, pltpu.HBM)
+
+
+def in_vmem(x):
+    return pltpu.with_memory_space_constraint(x, pltpu.VMEM)
+
+
+def merge_kernel(
+    pay_ref, prof_ref, embed_hbm, w_hbm, x_ref, top_ref, bot_ref, embed_ref, w_ref,
+    mg_ref, y_ref, xg_ref, sem,
+):
     rows = pay_ref.shape[0]
+    copies = [
+        pltpu.make_async_copy(embed_hbm, embed_ref, sem.at[0]),
+        pltpu.make_async_copy(w_hbm.at[0], w_ref, sem.at[1]),
+    ]
+    for copy in copies:
+        copy.start()
     pick = onehot(iota((8, META), 0) == iota((8, META), 1))
     fields = dot_nt(pick, pay_ref[:, CH * 128 :])
     offs = fields[0:1, :]
@@ -148,24 +201,32 @@
         x_ref[g * GRP : (g + 1) * GRP, :] = tokens
         top_ref[g * HALO : (g + 1) * HALO, :] = tokens[:HALO, :]
         bot_ref[g * HALO : (g + 1) * HALO, :] = tokens[GRP - HALO :, :]
-
-
-def merge(payload, profiles):
+    for copy in copies:
+        copy.wait()
+
+
+def merge(payload, profiles, embed, qkv_weight):
+    vmem = pl.BlockSpec(memory_space=pltpu.VMEM)
+    hbm = pl.BlockSpec(memory_space=pltpu.HBM)
     return pl.pallas_call(
         merge_kernel,
         out_shape=[
             jax.ShapeDtypeStruct((4 * GRP, PATCH), bf16),
             jax.ShapeDtypeStruct((EDGE, PATCH), bf16),
             jax.ShapeDtypeStruct((EDGE, PATCH), bf16),
+            pltpu.VMEM((PATCH, MODEL), bf16),
+            pltpu.VMEM((MODEL, 3 * MODEL), bf16),
         ],
+        in_specs=[vmem, vmem, hbm, hbm],
         scratch_shapes=[
             pltpu.VMEM((TOK_H * 8, CH * 128), bf16),
             pltpu.VMEM((TOK_H * 8, CH * 128), f32),
             pltpu.VMEM((GRP, PATCH), bf16),
+            pltpu.SemaphoreType.DMA((2,)),
         ],
         compiler_params=pltpu.CompilerParams(vmem_limit_bytes=VMEM_BYTES),
         name="merge",
-    )(payload, profiles)
+    )(payload, profiles, in_hbm(embed), in_hbm(qkv_weight))
 
 
 def normed(stream, gain):
@@ -177,38 +238,24 @@
 
 def own_kernel(layer, *refs):
     if layer == 0:
-        x_ref, embed_ref, gain_ref, w_ref, stream_ref, qkv_ref, w_vmem, sem, inp_ref = refs
-    else:
-        x_ref, w_ref, qkv_ref, w_vmem, sem = refs
-        inp_ref = x_ref
-    copies = [
-        pltpu.make_async_copy(
-            w_ref.at[layer, :, pl.ds(n * MODEL, MODEL)], w_vmem.at[n], sem.at[n]
-        )
-        for n in range(3)
-    ]
-    for copy in copies:
-        copy.start()
-    if layer == 0:
+        x_ref, embed_ref, gain_ref, w_ref, stream_ref, qkv_ref, inp_ref = refs
         for r in range(0, 4 * GRP, GRP):
             stream = dot(x_ref[r : r + GRP, :], embed_ref[...])
             stream_ref[r : r + GRP, :] = stream
             inp_ref[r : r + GRP, :] = normed(stream, gain_ref[0:1, :])
+    else:
+        inp_ref, w_ref, qkv_ref = refs
     step = 256
-    for n in range(3):
-        copies[n].wait()
-        for m in range(0, MODEL, step):
-            part = dot(inp_ref[...], w_vmem[n, :, m : m + step]).astype(bf16)
-            if n == 0:
-                part = part * jnp.asarray(0.125, bf16)
-            qkv_ref[:, n * MODEL + m : n * MODEL + m + step] = part
-
-
-def own_part(layer, x, embed, gain, qkv_weight):
-    any_spec = pl.BlockSpec(memory_space=pl.ANY)
+    for m in range(0, 3 * MODEL, step):
+        part = dot(inp_ref[...], w_ref[:, m : m + step]).astype(bf16)
+        if m < MODEL:
+            part = part * jnp.asarray(0.125, bf16)
+        qkv_ref[:, m : m + step] = part
+
+
+def own_part(layer, x, embed, gain, w):
     vmem = pl.BlockSpec(memory_space=pltpu.VMEM)
     qkv = jax.ShapeDtypeStruct((4 * GRP, 3 * MODEL), bf16)
-    scratch = [pltpu.VMEM((3, MODEL, MODEL), bf16), pltpu.SemaphoreType.DMA((3,))]
     params = pltpu.CompilerParams(vmem_limit_bytes=VMEM_BYTES)
     cost = pl.CostEstimate(
         flops=2 * 4 * GRP * MODEL * 3 * MODEL, bytes_accessed=12 << 20, transcendentals=0
@@ -217,39 +264,34 @@
         return pl.pallas_call(
             functools.partial(own_kernel, layer),
             out_shape=[jax.ShapeDtypeStruct((4 * GRP, MODEL), f32), qkv],
-            in_specs=[vmem, vmem, vmem, any_spec],
-            scratch_shapes=scratch + [pltpu.VMEM((4 * GRP, MODEL), bf16)],
+            in_specs=[vmem] * 4,
+            scratch_shapes=[pltpu.VMEM((4 * GRP, MODEL), bf16)],
             compiler_params=params,
             cost_estimate=cost,
             name="own0",
-        )(x, embed, gain, qkv_weight)
+        )(x, in_vmem(embed), gain, in_vmem(w))
     return pl.pallas_call(
         functools.partial(own_kernel, layer),
         out_shape=qkv,
-        in_specs=[vmem, any_spec],
-        scratch_shapes=scratch,
+        in_specs=[vmem] * 2,
         compiler_params=params,
         cost_estimate=cost,
         name="own1",
-    )(x, qkv_weight)
+    )(x, in_vmem(w))
 
 
 def attend_kernel(layer, *refs):
     if layer == 0:
         (place_ref, top_ref, bot_ref, left_ref, right_ref, stream_ref, qkv_ref, gain_ref, embed_ref,
-         w_ref, o_ref, out_ref, x_ref, xt_ref, xb_ref,
-         w_vmem, o_vmem, sem, halo_ref, kv_ref, att_ref) = refs
+         w_ref, o_hbm, next_hbm, out_ref, x_ref, xt_ref, xb_ref, next_ref,
+         halo_ref, kv_ref, att_ref, o_ref, sem) = refs
     else:
         (place_ref, top_ref, bot_ref, left_ref, right_ref, stream_ref, qkv_ref,
-         w_ref, o_ref, out_ref,
-         w_vmem, o_vmem, sem, halo_ref, kv_ref, att_ref) = refs
-    copies = [
-        pltpu.make_async_copy(
-            w_ref.at[layer, :, pl.ds((n + 1) * MODEL, MODEL)], w_vmem.at[n], sem.at[n]
-        )
-        for n in range(2)
-    ]
-    copies.append(pltpu.make_async_copy(o_ref.at[layer], o_vmem, sem.at[2]))
+         w_ref, o_hbm, out_ref,
+         halo_ref, kv_ref, att_ref, o_ref, sem) = refs
+    copies = [pltpu.make_async_copy(o_hbm.at[layer], o_ref, sem.at[0])]
+    if layer == 0:
+        copies.append(pltpu.make_async_copy(next_hbm.at[1], next_ref, sem.at[1]))
     for copy in copies:
         copy.start()
     row = 0
@@ -264,10 +306,11 @@
         kv_ref[at : at + GRP, :] = qkv_ref[g * GRP : (g + 1) * GRP, MODEL:]
     step = 256
     for n in range(2):
-        copies[n].wait()
         for m in range(0, MODEL, step):
-            part = dot(halo_ref[...], w_vmem[n, :, m : m + step]).astype(bf16)
             lanes = slice(n * MODEL + m, n * MODEL + m + step)
+            part = dot(
+                halo_ref[...], w_ref[:, MODEL + lanes.start : MODEL + lanes.stop]
+            ).astype(bf16)
             for g in range(4):
                 at = (g + 1) * FULL
                 kv_ref[at : at + HALO, lanes] = part[g * HALO : (g + 1) * HALO, :]
@@ -318,12 +361,13 @@
         return carry
 
     lax.fori_loop(0, 8, block, 0)
-
-    copies[2].wait()
+    for copy in copies:
+        copy.wait()
+
     if layer == 0:
         for g in range(4):
             rows = slice(g * GRP, (g + 1) * GRP)
-            stream = stream_ref[rows, :] + dot(att_ref[rows, :], o_vmem[...])
+            stream = stream_ref[rows, :] + dot(att_ref[rows, :], o_ref[...])
             out_ref[rows, :] = stream
             inputs = normed(stream, gain_ref[1:2, :])
             x_ref[rows, :] = inputs
@@ -332,7 +376,7 @@
     else:
         for g in range(4):
             rows = slice(g * GRP, (g + 1) * GRP)
-            stream = stream_ref[rows, :] + dot(att_ref[rows, :], o_vmem[...])
+            stream = stream_ref[rows, :] + dot(att_ref[rows, :], o_ref[...])
             att_ref[rows, :] = stream.astype(bf16)
         for r in range(0, 4 * GRP, GRP):
             to = iota((GRP, 4 * GRP), 0) + r
@@ -341,14 +385,14 @@
             out_ref[r : r + GRP, :] = dot(onehot(source == wanted), att_ref[...]).astype(bf16)
 
 
-def attend(layer, place, halos, stream, qkv, gain, embed, qkv_weight, out_weight):
-    any_spec = pl.BlockSpec(memory_space=pl.ANY)
+def attend(layer, place, halos, stream, qkv, gain, embed, w, out_weight, qkv_weight):
+    hbm = pl.BlockSpec(memory_space=pltpu.HBM)
     vmem = pl.BlockSpec(memory_space=pltpu.VMEM)
     smem = pl.BlockSpec(memory_space=pltpu.SMEM)
     operands = [place, *halos, stream, qkv]
     specs = [smem] + [vmem] * 6
     if layer == 0:
-        operands += [gain, embed]
+        operands += [gain, in_vmem(embed)]
         specs += [vmem, vmem]
         out_shape = [
             jax.ShapeDtypeStruct((4 * GRP, MODEL), f32),
@@ -358,19 +402,22 @@
         ]
     else:
         out_shape = jax.ShapeDtypeStruct((4 * GRP, MODEL), bf16)
-    operands += [qkv_weight, out_weight]
-    specs += [any_spec, any_spec]
+    operands += [in_vmem(w), in_hbm(out_weight)]
+    specs += [vmem, hbm]
+    if layer == 0:
+        operands.append(in_hbm(qkv_weight))
+        specs.append(hbm)
+        out_shape.append(pltpu.VMEM((MODEL, 3 * MODEL), bf16))
     return pl.pallas_call(
         functools.partial(attend_kernel, layer),
         out_shape=out_shape,
         in_specs=specs,
         scratch_shapes=[
-            pltpu.VMEM((2, MODEL, MODEL), bf16),
-            pltpu.VMEM((MODEL, MODEL), bf16),
-            pltpu.SemaphoreType.DMA((3,)),
             pltpu.VMEM((2 * EDGE + 2 * FULL, MODEL), bf16),
             pltpu.VMEM((6 * FULL, 2 * MODEL), bf16),
             pltpu.VMEM((4 * GRP, MODEL), bf16),
+            pltpu.VMEM((MODEL, MODEL), bf16),
+            pltpu.SemaphoreType.DMA((2,)),
         ],
         compiler_params=pltpu.CompilerParams(vmem_limit_bytes=VMEM_BYTES),
         name="attend%d" % layer,
@@ -406,15 +453,15 @@
     embed = embed_weight.reshape(CH, 8, 8, MODEL).transpose(1, 0, 2, 3).reshape(PATCH, MODEL)
     payload = pack(dest, offsets, profile_index, profiles, scans)
     payload = lax.all_to_all(payload, ("row", "col"), split_axis=0, concat_axis=0, tiled=True)
-    x, first, last = merge(payload, profiles)
+    x, first, last, embed, w = merge(payload, profiles, embed, qkv_weight)
     halos = around(x, first, last)
-    stream, qkv = own_part(0, x, embed, attn_gain, qkv_weight)
-    stream, x, first, last = attend(
-        0, place, halos, stream, qkv, attn_gain, embed, qkv_weight, out_weight
+    stream, qkv = own_part(0, x, embed, attn_gain, w)
+    stream, x, first, last, w = attend(
+        0, place, halos, stream, qkv, attn_gain, embed, w, out_weight, qkv_weight
     )
     halos = around(x, first, last)
-    qkv = own_part(1, x, None, None, qkv_weight)
-    tokens = attend(1, place, halos, stream, qkv, None, None, qkv_weight, out_weight)
+    qkv = own_part(1, x, None, None, w)
+    tokens = attend(1, place, halos, stream, qkv, None, None, w, out_weight, None)
     return tokens.reshape(TOK_H, TOK_W, MODEL)
 
 

time: 122 us -> 107 us (0.88)
  Pallas kernels: 49.8 us -> 37.8 us
  local copies, waits for them, and re-layouts: 7.13 us -> 1.15 us
  waiting for transfers between devices: 35.6 us -> 38.7 us
    pallas_call x2, Pallas kernels: 28.3 us -> 21.4 us  [attend(): pl.pallas_call(functools.partial(attend_kernel, layer), out_shape=out_sha...]
    unnamed x17 -> x6, local copies, waits for them, and re-layouts: 5.75 us -> 0.02 us
    pallas_call x1, Pallas kernels: 7.09 us -> 3.47 us  [own_part(): pl.pallas_call(functools.partial(own_kernel, layer), out_shape=qkv, in_sp...]
    ppermute x8, waiting for transfers between devices: 4.55 us -> 7.36 us  [shifted(): lax.ppermute(cells, axis, [(i, (i + by) % count) for i in range(count)])]
    pallas_call x1, Pallas kernels: 7.13 us -> 4.38 us  [own_part(): pl.pallas_call(functools.partial(own_kernel, layer), out_shape=[jax.Shape...]
  transfers between devices with their start and end apart: 9 -> 9, of which waited for: 3 -> 4; matrix products, arithmetic and copies ran while one was open for 1% -> 1% of each run, Pallas kernels for 12% -> 7%
where the time goes in v1:
time: 107 us
  waiting for transfers between devices  38.7 us (36%)
  Pallas kernels  37.8 us (35%)
  starting transfers between devices  28.4 us (27%)
  local copies, waits for them, and re-layouts  1.15 us (1%)
    all_to_all x1, waiting for transfers between devices, per_device(): lax.all_to_all(payload, ('row', 'col'), split_axis=0, concat_axis=0, tile...  31.3 us
    pallas_call x2, Pallas kernels, attend(): pl.pallas_call(functools.partial(attend_kernel, layer), out_shape=out_sha...  21.4 us
    ppermute x8, starting transfers between devices, shifted(): lax.ppermute(cells, axis, [(i, (i + by) % count) for i in range(count)])  17.3 us
    all_to_all x1, starting transfers between devices, per_device(): lax.all_to_all(payload, ('row', 'col'), split_axis=0, concat_axis=0, tile...  11.1 us
    ppermute x8, waiting for transfers between devices, shifted(): lax.ppermute(cells, axis, [(i, (i + by) % count) for i in range(count)])  7.36 us
    pallas_call x1, Pallas kernels, pack(): pl.pallas_call(pack_kernel, out_shape=jax.ShapeDtypeStruct((rows, CH * 12...  5.34 us
    pallas_call x1, Pallas kernels, own_part(): pl.pallas_call(functools.partial(own_kernel, layer), out_shape=[jax.Shape...  4.38 us
    pallas_call x1, Pallas kernels, own_part(): pl.pallas_call(functools.partial(own_kernel, layer), out_shape=qkv, in_sp...  3.47 us
  transfers between devices with their start and end apart: 9, of which 4 were waited for; matrix products, arithmetic and copies ran while one was open for 1% of the time, Pallas kernels for 7%

profile of v1, /device:TPU:0, one launch (start us, length us, event | category | flops | bytes accessed | tf_op | source)
XLA Modules:
  0.0 106.5 jit_solution(5918333216570433052)
XLA Ops:
  0.0 5.3 %pack.1 = bf16[1024,1152]{1,0:T(8,128)(2,1)} custom-call(s32[1,128]{1,0:T(1,128)} %bitcast.17, s32[1,128]{1,0:T(1,128)} %bitcast.18, s32[1,128]{1,0:T(1,128)} %bitcast.19, f32[16,4,128]{2,1,0:T(4,128)} %prof_ref.1, f32[4096,128]{1,0:T(8,128)} %bitcast.15), custom_call_target="tpu_custom_call" | custom-call | tf_op jit(solution)/shard_map/pack/pallas_call | solution.py:113
  5.3 0.0 copy-start.2
  5.4 0.0 copy-start
  5.4 11.1 %all-to-all-start = ((bf16[128,8,1152]{2,1,0:T(8,128)(2,1)}), bf16[128,8,1152]{2,1,0:T(8,128)(2,1)S(1)}, u32[]{:S(2)}, u32[]{:S(2)}) async-start(bf16[128,8,1152]{2,1,0:T(8,128)(2,1)} %bitcast.6), calls=%async_computation | async-start | bytes 4718592 | tf_op jit(solution)/shard_map/all_to_all | solution.py:455
  16.5 0.0 copy-done.2
  16.5 1.1 copy.10
  17.6 0.1 pad_add_fusion.refs_0_
  17.7 31.3 %all-to-all-done = bf16[128,8,1152]{2,1,0:T(8,128)(2,1)S(1)} async-done(((bf16[128,8,1152]{2,1,0:T(8,128)(2,1)}), bf16[128,8,1152]{2,1,0:T(8,128)(2,1)S(1)}, u32[]{:S(2)}, u32[]{:S(2)}) %all-to-all-start) | async-done | bytes 2359328 | tf_op jit(solution)/shard_map/all_to_all | solution.py:455
  49.0 0.0 copy-done
  49.0 0.0 copy-start.1
  49.0 3.2 %merge.1 = (bf16[512,512]{1,0:T(8,128)(2,1)S(1)}, bf16[64,512]{1,0:T(8,128)(2,1)S(1)}, bf16[64,512]{1,0:T(8,128)(2,1)S(1)}, bf16[512,1024]{1,0:T(8,128)(2,1)S(1)}, bf16[1024,3072]{1,0:T(8,128)(2,1)S(1)}) custom-call(bf16[1024,1152]{1,0:T(8,128)(2,1)S(1)} %bitcast.13, f32[16,4,128]{2,1,0:T(4,128)S(1)} %copy-done, bf16[512,1024]{1,0:T(8,128)(2,1)} %bitcast.14, ...), custom_call_target="tpu_custom_call" | custom-call | tf_op jit(solution)/shard_map/merge/pallas_call | solution.py:211
  52.2 0.0 collective-permute-start
  52.2 2.9 %collective-permute-start.1 = (bf16[64,512]{1,0:T(8,128)(2,1)S(1)}, bf16[64,512]{1,0:T(8,128)(2,1)S(1)}, u32[]{:S(2)}, u32[]{:S(2)}) collective-permute-start(bf16[64,512]{1,0:T(8,128)(2,1)S(1)} %get-tuple-element.18), channel_id=1, source_target_pairs={{0,112},{16,0},{32,16},{48,32},{64,48},{80,64},{96,80},{112,96},{1... | collective-permute-start | bytes 196616 | tf_op jit(solution)/shard_map/ppermute | solution.py:429
  55.2 1.9 %collective-permute-done.refs_1_ = bf16[64,512]{1,0:T(8,128)(2,1)S(1)} collective-permute-done((bf16[64,512]{1,0:T(8,128)(2,1)S(1)}, bf16[64,512]{1,0:T(8,128)(2,1)S(1)}, u32[]{:S(2)}, u32[]{:S(2)}) %collective-permute-start) | collective-permute-done | bytes 65568 | tf_op jit(solution)/shard_map/ppermute | solution.py:429
  57.1 0.0 collective-permute-done.1.refs_2_
  57.1 0.9 collective-permute-start.2
  58.1 4.7 %collective-permute-start.3 = (bf16[160,512]{1,0:T(8,128)(2,1)S(1)}, bf16[160,512]{1,0:T(8,128)(2,1)S(1)}, u32[]{:S(2)}, u32[]{:S(2)}) collective-permute-start(bf16[160,512]{1,0:T(8,128)(2,1)S(1)} %pad_maximum_fusion.3), channel_id=1, source_target_pairs={{0,15},{1,0},{2,1},{3,2},{4,3},{5,4},{6,5},{7,6},{8,7},{9,8},{10,9... | collective-permute-start | bytes 491528 | tf_op jit(solution)/shard_map/ppermute | solution.py:429
  62.8 0.0 copy-done.1
  62.8 4.4 %own0.1 = (f32[512,1024]{1,0:T(8,128)S(1)}, bf16[512,3072]{1,0:T(8,128)(2,1)S(1)}) custom-call(bf16[512,512]{1,0:T(8,128)(2,1)S(1)} %get-tuple-element.19.refs_0_, bf16[512,1024]{1,0:T(8,128)(2,1)S(1)} %get-tuple-element.20.refs_1_.refs_8_, f32[2,1024]{1,0:T(2,128)S(1)} %copy-done.1, bf16[1024,3072]{1,0:T(8,128)(2,1)S(1)} %get-tuple-element.21.refs_3_.refs_9_), custom_call_target="tpu_custom_call" | custom-call | flops 3221225472 | bytes 12582912 | tf_op jit(solution)/shard_map/own0/pallas_call | solution.py:264
  67.2 0.0 collective-permute-done.2.refs_3_
  67.2 0.0 collective-permute-done.3.refs_4_
  67.2 10.6 %attend0.1 = (f32[512,1024]{1,0:T(8,128)S(1)}, bf16[512,1024]{1,0:T(8,128)(2,1)S(1)}, bf16[64,1024]{1,0:T(8,128)(2,1)S(1)}, bf16[64,1024]{1,0:T(8,128)(2,1)S(1)}, bf16[1024,3072]{1,0:T(8,128)(2,1)S(1)}) custom-call(s32[4]{0:T(128)S(1)} %pad_add_fusion.refs_0_, bf16[64,512]{1,0:T(8,128)(2,1)S(1)} %collective-permute-done.refs_1_, ...), custom_call_target="tpu_custom_call" | custom-call | tf_op jit(solution)/shard_map/attend0/pallas_call | solution.py:411
  77.8 0.0 collective-permute-start.4
  77.9 2.9 %collective-permute-start.5 = (bf16[64,1024]{1,0:T(8,128)(2,1)S(1)}, bf16[64,1024]{1,0:T(8,128)(2,1)S(1)}, u32[]{:S(2)}, u32[]{:S(2)}) collective-permute-start(bf16[64,1024]{1,0:T(8,128)(2,1)S(1)} %get-tuple-element.25), channel_id=1, source_target_pairs={{0,112},{16,0},{32,16},{48,32},{64,48},{80,64},{96,80},{112,96},{1... | collective-permute-start | bytes 393224 | tf_op jit(solution)/shard_map/ppermute | solution.py:429
  80.9 2.6 %collective-permute-done.4.refs_1_ = bf16[64,1024]{1,0:T(8,128)(2,1)S(1)} collective-permute-done((bf16[64,1024]{1,0:T(8,128)(2,1)S(1)}, bf16[64,1024]{1,0:T(8,128)(2,1)S(1)}, u32[]{:S(2)}, u32[]{:S(2)}) %collective-permute-start.4) | collective-permute-done | bytes 131104 | tf_op jit(solution)/shard_map/ppermute | solution.py:429
  83.5 0.0 collective-permute-done.5.refs_2_
  83.5 0.1 collective-permute-start.6
  83.6 5.6 %collective-permute-start.7 = (bf16[160,1024]{1,0:T(8,128)(2,1)S(1)}, bf16[160,1024]{1,0:T(8,128)(2,1)S(1)}, u32[]{:S(2)}, u32[]{:S(2)}) collective-permute-start(bf16[160,1024]{1,0:T(8,128)(2,1)S(1)} %pad_maximum_fusion.1), channel_id=1, source_target_pairs={{0,15},{1,0},{2,1},{3,2},{4,3},{5,4},{6,5},{7,6},{8,7},{9,8},{10,9... | collective-permute-start | bytes 983048 | tf_op jit(solution)/shard_map/ppermute | solution.py:429
  89.3 3.5 %own1.1.refs_6_ = bf16[512,3072]{1,0:T(8,128)(2,1)S(1)} custom-call(bf16[512,1024]{1,0:T(8,128)(2,1)S(1)} %get-tuple-element.26.refs_0_, bf16[1024,3072]{1,0:T(8,128)(2,1)S(1)} %get-tuple-element.28.refs_1_.refs_7_), custom_call_target="tpu_custom_call" | custom-call | flops 3221225472 | bytes 12582912 | tf_op jit(solution)/shard_map/own1/pallas_call | solution.py:273
  92.7 2.8 %collective-permute-done.6.refs_3_ = bf16[160,1024]{1,0:T(8,128)(2,1)S(1)} collective-permute-done((bf16[160,1024]{1,0:T(8,128)(2,1)S(1)}, bf16[160,1024]{1,0:T(8,128)(2,1)S(1)}, u32[]{:S(2)}, u32[]{:S(2)}) %collective-permute-start.6) | collective-permute-done | bytes 327712 | tf_op jit(solution)/shard_map/ppermute | solution.py:429
  95.5 0.0 collective-permute-done.7.refs_4_
  95.5 10.8 %attend1.1 = bf16[512,1024]{1,0:T(8,128)(2,1)} custom-call(s32[4]{0:T(128)S(1)} %pad_add_fusion.refs_0_, bf16[64,1024]{1,0:T(8,128)(2,1)S(1)} %collective-permute-done.4.refs_1_, bf16[64,1024]{1,0:T(8,128)(2,1)S(1)} %collective-permute-done.5.refs_2_, bf16[160,1024]{1,0:T(8,128)(2,1)S(1)} %collective-permute-done.6.refs_3_, ...), custom_call_target="tpu_custom_call" | custom-call | tf_op jit(solution)/shard_map/attend1/pallas_call | solution.py:411
  (11 shorter events, 0.1 us)
Async XLA Ops:
  5.3 11.2 %copy-start.2 = (bf16[512,1024]{1,0:T(8,128)(2,1)S(1)}, bf16[512,1024]{1,0:T(8,128)(2,1)}, u32[]{:S(2)}) copy-start(bf16[512,1024]{1,0:T(8,128)(2,1)} %param.14) | copy-start | bytes 3145732
  5.4 43.7 %copy-start = (f32[16,4,128]{2,1,0:T(4,128)S(1)}, f32[16,4,128]{2,1,0:T(4,128)}, u32[]{:S(2)}) copy-start(f32[16,4,128]{2,1,0:T(4,128)} %prof_ref.1) | copy-start | bytes 98308
  5.4 43.6 %all-to-all-start = ((bf16[128,8,1152]{2,1,0:T(8,128)(2,1)}), bf16[128,8,1152]{2,1,0:T(8,128)(2,1)S(1)}, u32[]{:S(2)}, u32[]{:S(2)}) async-start(bf16[128,8,1152]{2,1,0:T(8,128)(2,1)} %bitcast.6), calls=%async_computation | async-start | bytes 4718592 | tf_op jit(solution)/shard_map/all_to_all | solution.py:455
  49.0 13.8 %copy-start.1 = (f32[2,1024]{1,0:T(2,128)S(1)}, f32[2,1024]{1,0:T(2,128)}, u32[]{:S(2)}) copy-start(f32[2,1024]{1,0:T(2,128)} %refs_7_.1) | copy-start | bytes 24580
  52.2 4.9 %collective-permute-start = (bf16[64,512]{1,0:T(8,128)(2,1)S(1)}, bf16[64,512]{1,0:T(8,128)(2,1)S(1)}, u32[]{:S(2)}, u32[]{:S(2)}) collective-permute-start(bf16[64,512]{1,0:T(8,128)(2,1)S(1)} %get-tuple-element.17), channel_id=1, source_target_pairs={{0,16},{16,32},{32,48},{48,64},{64,80},{80,96},{96,112},{112,0},{1... | collective-permute-start | bytes 196616 | tf_op jit(solution)/shard_map/ppermute | solution.py:429
  52.2 4.9 %collective-permute-start.1 = (bf16[64,512]{1,0:T(8,128)(2,1)S(1)}, bf16[64,512]{1,0:T(8,128)(2,1)S(1)}, u32[]{:S(2)}, u32[]{:S(2)}) collective-permute-start(bf16[64,512]{1,0:T(8,128)(2,1)S(1)} %get-tuple-element.18), channel_id=1, source_target_pairs={{0,112},{16,0},{32,16},{48,32},{64,48},{80,64},{96,80},{112,96},{1... | collective-permute-start | bytes 196616 | tf_op jit(solution)/shard_map/ppermute | solution.py:429
  57.1 10.1 %collective-permute-start.2 = (bf16[160,512]{1,0:T(8,128)(2,1)S(1)}, bf16[160,512]{1,0:T(8,128)(2,1)S(1)}, u32[]{:S(2)}, u32[]{:S(2)}) collective-permute-start(bf16[160,512]{1,0:T(8,128)(2,1)S(1)} %pad_maximum_fusion.2), channel_id=1, source_target_pairs={{0,1},{1,2},{2,3},{3,4},{4,5},{5,6},{6,7},{7,8},{8,9},{9,10},{10,1... | collective-permute-start | bytes 491528 | tf_op jit(solution)/shard_map/ppermute | solution.py:429
  58.1 9.1 %collective-permute-start.3 = (bf16[160,512]{1,0:T(8,128)(2,1)S(1)}, bf16[160,512]{1,0:T(8,128)(2,1)S(1)}, u32[]{:S(2)}, u32[]{:S(2)}) collective-permute-start(bf16[160,512]{1,0:T(8,128)(2,1)S(1)} %pad_maximum_fusion.3), channel_id=1, source_target_pairs={{0,15},{1,0},{2,1},{3,2},{4,3},{5,4},{6,5},{7,6},{8,7},{9,8},{10,9... | collective-permute-start | bytes 491528 | tf_op jit(solution)/shard_map/ppermute | solution.py:429
  77.8 5.6 %collective-permute-start.4 = (bf16[64,1024]{1,0:T(8,128)(2,1)S(1)}, bf16[64,1024]{1,0:T(8,128)(2,1)S(1)}, u32[]{:S(2)}, u32[]{:S(2)}) collective-permute-start(bf16[64,1024]{1,0:T(8,128)(2,1)S(1)} %get-tuple-element.24), channel_id=1, source_target_pairs={{0,16},{16,32},{32,48},{48,64},{64,80},{80,96},{96,112},{112,0},{1... | collective-permute-start | bytes 393224 | tf_op jit(solution)/shard_map/ppermute | solution.py:429
  77.9 5.6 %collective-permute-start.5 = (bf16[64,1024]{1,0:T(8,128)(2,1)S(1)}, bf16[64,1024]{1,0:T(8,128)(2,1)S(1)}, u32[]{:S(2)}, u32[]{:S(2)}) collective-permute-start(bf16[64,1024]{1,0:T(8,128)(2,1)S(1)} %get-tuple-element.25), channel_id=1, source_target_pairs={{0,112},{16,0},{32,16},{48,32},{64,48},{80,64},{96,80},{112,96},{1... | collective-permute-start | bytes 393224 | tf_op jit(solution)/shard_map/ppermute | solution.py:429
  83.5 12.0 %collective-permute-start.6 = (bf16[160,1024]{1,0:T(8,128)(2,1)S(1)}, bf16[160,1024]{1,0:T(8,128)(2,1)S(1)}, u32[]{:S(2)}, u32[]{:S(2)}) collective-permute-start(bf16[160,1024]{1,0:T(8,128)(2,1)S(1)} %pad_maximum_fusion), channel_id=1, source_target_pairs={{0,1},{1,2},{2,3},{3,4},{4,5},{5,6},{6,7},{7,8},{8,9},{9,10},{10,1... | collective-permute-start | bytes 983048 | tf_op jit(solution)/shard_map/ppermute | solution.py:429
  83.6 11.9 %collective-permute-start.7 = (bf16[160,1024]{1,0:T(8,128)(2,1)S(1)}, bf16[160,1024]{1,0:T(8,128)(2,1)S(1)}, u32[]{:S(2)}, u32[]{:S(2)}) collective-permute-start(bf16[160,1024]{1,0:T(8,128)(2,1)S(1)} %pad_maximum_fusion.1), channel_id=1, source_target_pairs={{0,15},{1,0},{2,1},{3,2},{4,3},{5,4},{6,5},{7,6},{8,7},{9,8},{10,9... | collective-permute-start | bytes 983048 | tf_op jit(solution)/shard_map/ppermute | solution.py:429

commit v2 on v1

--- a/solution.py
+++ b/solution.py
@@ -16,12 +16,15 @@
 MODEL = 1024
 PATCH = 512
 GRP = 128
-FULL = 160
-HALO = 16
+MID = 160
+WIDE = 192
+HALO = 32
 EDGE = 4 * HALO
+SIDE = 2 * WIDE
 META = 128
 CHUNKS = 4
 VMEM_BYTES = 20 * 1024 * 1024
+LARGE_BYTES = 40 * 1024 * 1024
 
 f32 = jnp.float32
 bf16 = jnp.bfloat16
@@ -236,15 +239,11 @@
     return (moved * lax.rsqrt(spread + 1e-05) * gain).astype(bf16)
 
 
-def own_kernel(layer, *refs):
-    if layer == 0:
-        x_ref, embed_ref, gain_ref, w_ref, stream_ref, qkv_ref, inp_ref = refs
-        for r in range(0, 4 * GRP, GRP):
-            stream = dot(x_ref[r : r + GRP, :], embed_ref[...])
-            stream_ref[r : r + GRP, :] = stream
-            inp_ref[r : r + GRP, :] = normed(stream, gain_ref[0:1, :])
-    else:
-        inp_ref, w_ref, qkv_ref = refs
+def own_kernel(x_ref, embed_ref, gain_ref, w_ref, stream_ref, qkv_ref, inp_ref):
+    for r in range(0, 4 * GRP, GRP):
+        stream = dot(x_ref[r : r + GRP, :], embed_ref[...])
+        stream_ref[r : r + GRP, :] = stream
+        inp_ref[r : r + GRP, :] = normed(stream, gain_ref[0:1, :])
     step = 256
     for m in range(0, 3 * MODEL, step):
         part = dot(inp_ref[...], w_ref[:, m : m + step]).astype(bf16)
@@ -253,73 +252,23 @@
         qkv_ref[:, m : m + step] = part
 
 
-def own_part(layer, x, embed, gain, w):
-    vmem = pl.BlockSpec(memory_space=pltpu.VMEM)
-    qkv = jax.ShapeDtypeStruct((4 * GRP, 3 * MODEL), bf16)
-    params = pltpu.CompilerParams(vmem_limit_bytes=VMEM_BYTES)
-    cost = pl.CostEstimate(
-        flops=2 * 4 * GRP * MODEL * 3 * MODEL, bytes_accessed=12 << 20, transcendentals=0
-    )
-    if layer == 0:
-        return pl.pallas_call(
-            functools.partial(own_kernel, layer),
-            out_shape=[jax.ShapeDtypeStruct((4 * GRP, MODEL), f32), qkv],
-            in_specs=[vmem] * 4,
-            scratch_shapes=[pltpu.VMEM((4 * GRP, MODEL), bf16)],
-            compiler_params=params,
-            cost_estimate=cost,
-            name="own0",
-        )(x, in_vmem(embed), gain, in_vmem(w))
+def own_part(x, embed, gain, w):
     return pl.pallas_call(
-        functools.partial(own_kernel, layer),
-        out_shape=qkv,
-        in_specs=[vmem] * 2,
-        compiler_params=params,
-        cost_estimate=cost,
-        name="own1",
-    )(x, in_vmem(w))
-
-
-def attend_kernel(layer, *refs):
-    if layer == 0:
-        (place_ref, top_ref, bot_ref, left_ref, right_ref, stream_ref, qkv_ref, gain_ref, embed_ref,
-         w_ref, o_hbm, next_hbm, out_ref, x_ref, xt_ref, xb_ref, next_ref,
-         halo_ref, kv_ref, att_ref, o_ref, sem) = refs
-    else:
-        (place_ref, top_ref, bot_ref, left_ref, right_ref, stream_ref, qkv_ref,
-         w_ref, o_hbm, out_ref,
-         halo_ref, kv_ref, att_ref, o_ref, sem) = refs
-    copies = [pltpu.make_async_copy(o_hbm.at[layer], o_ref, sem.at[0])]
-    if layer == 0:
-        copies.append(pltpu.make_async_copy(next_hbm.at[1], next_ref, sem.at[1]))
-    for copy in copies:
-        copy.start()
-    row = 0
-    for ref in (top_ref, bot_ref, left_ref, right_ref):
-        part = ref[...]
-        if layer == 0:
-            part = normed(dot(part, embed_ref[...]), gain_ref[0:1, :])
-        halo_ref[row : row + ref.shape[0], :] = part
-        row += ref.shape[0]
-    for g in range(4):
-        at = (g + 1) * FULL + HALO
-        kv_ref[at : at + GRP, :] = qkv_ref[g * GRP : (g + 1) * GRP, MODEL:]
-    step = 256
-    for n in range(2):
-        for m in range(0, MODEL, step):
-            lanes = slice(n * MODEL + m, n * MODEL + m + step)
-            part = dot(
-                halo_ref[...], w_ref[:, MODEL + lanes.start : MODEL + lanes.stop]
-            ).astype(bf16)
-            for g in range(4):
-                at = (g + 1) * FULL
-                kv_ref[at : at + HALO, lanes] = part[g * HALO : (g + 1) * HALO, :]
-                kv_ref[at + HALO + GRP : at + FULL, lanes] = part[
-                    EDGE + g * HALO : EDGE + (g + 1) * HALO, :
-                ]
-            kv_ref[0:FULL, lanes] = part[2 * EDGE : 2 * EDGE + FULL, :]
-            kv_ref[5 * FULL : 6 * FULL, lanes] = part[2 * EDGE + FULL :, :]
-
+        own_kernel,
+        out_shape=[
+            jax.ShapeDtypeStruct((4 * GRP, MODEL), f32),
+            jax.ShapeDtypeStruct((4 * GRP, 3 * MODEL), bf16),
+        ],
+        scratch_shapes=[pltpu.VMEM((4 * GRP, MODEL), bf16)],
+        compiler_params=pltpu.CompilerParams(vmem_limit_bytes=VMEM_BYTES),
+        cost_estimate=pl.CostEstimate(
+            flops=2 * 4 * GRP * MODEL * 3 * MODEL, bytes_accessed=12 << 20, transcendentals=0
+        ),
+        name="own",
+    )(x, in_vmem(embed), gain, in_vmem(w))
+
+
+def attention(q_ref, q_at, q_pitch, kv_ref, k_pitch, a_ref, a_pitch, tall, broad, row, col, ends):
     query = iota((64, 256), 0)
     key = iota((64, 256), 1)
     row_gap = (key % 64) // 4 - 4 - (query % 32) // 4
@@ -327,101 +276,192 @@
     near = (jnp.abs(row_gap) <= RADIUS) & (jnp.abs(col_gap) <= RADIUS)
     near_bias = jnp.where(near, 0.0, -1e30)
     lane_key = iota((1, 256), 1)
-    key_row = (lane_key % 64) // 4 - 4
-    key_col = (lane_key // 64 - 1) * 4 + lane_key % 4
+    key_row = (lane_key % 64) // 4 + row
+    key_col = (lane_key // 64) * 4 + lane_key % 4 + col
     low_half = iota((64, 128), 1) < 64
     zero = jnp.zeros((64, 128), bf16)
     ones = jnp.ones((256, 128), bf16)
-    height, width = place_ref[2], place_ref[3]
-
-    def block(b, carry):
-        bi, bj = b // 2, b % 2
-        at_row = key_row + bi * 8 + place_ref[0]
-        at_col = key_col + bj * 8 + place_ref[1]
-        inside = (at_row >= 0) & (at_row < height) & (at_col >= 0) & (at_col < width)
-        bias = near_bias + jnp.where(inside, 0.0, -1e30)
-        bias = jnp.concatenate([bias, bias], axis=0)
-        q_rows = [pl.multiple_of((2 * bj + g) * GRP + bi * 32, 32) for g in range(2)]
-        k_rows = [pl.multiple_of((2 * bj + g) * FULL + bi * 32, 32) for g in range(4)]
-        for h in range(HEADS // 2):
-            lanes = slice(h * 128, (h + 1) * 128)
-            q = jnp.concatenate([qkv_ref[pl.ds(r, 32), lanes] for r in q_rows], axis=0)
-            q = jnp.concatenate([jnp.where(low_half, q, zero), jnp.where(low_half, zero, q)], axis=0)
-            k = jnp.concatenate([kv_ref[pl.ds(r, 64), lanes] for r in k_rows], axis=0)
-            v_lanes = slice(MODEL + h * 128, MODEL + (h + 1) * 128)
-            v = jnp.concatenate([kv_ref[pl.ds(r, 64), v_lanes] for r in k_rows], axis=0)
-            logits = dot_nt(q, k) + bias
-            top = jnp.max(logits, axis=-1, keepdims=True)
-            share = jnp.exp(logits - top).astype(bf16)
-            both = dot(share, jnp.concatenate([v, ones], axis=1))
-            mixed = both[:, :128] / both[:, 128:]
-            picked = jnp.where(low_half, mixed[:64, :], mixed[64:, :]).astype(bf16)
-            for g in range(2):
-                att_ref[pl.ds(q_rows[g], 32), lanes] = picked[g * 32 : (g + 1) * 32, :]
+
+    def strip(bi, carry):
+        at_row = key_row + bi * 8
+        row_inside = (at_row >= 0) & (at_row < ends[0])
+        for bj in range(broad):
+            at_col = key_col + bj * 8
+            inside = row_inside & (at_col >= 0) & (at_col < ends[1])
+            bias = near_bias + jnp.where(inside, 0.0, -1e30)
+            bias = jnp.concatenate([bias, bias], axis=0)
+            q_rows = [
+                pl.ds(pl.multiple_of((2 * bj + g) * q_pitch + q_at + bi * 32, 16), 32)
+                for g in range(2)
+            ]
+            a_rows = [
+                pl.ds(pl.multiple_of((2 * bj + g) * a_pitch + bi * 32, 32), 32) for g in range(2)
+            ]
+            k_rows = [
+                pl.ds(pl.multiple_of((2 * bj + g) * k_pitch + bi * 32, 32), 64) for g in range(4)
+            ]
+            for h in range(HEADS // 2):
+                lanes = slice(h * 128, (h + 1) * 128)
+                q = jnp.concatenate([q_ref[r, lanes] for r in q_rows], axis=0)
+                q = jnp.concatenate(
+                    [jnp.where(low_half, q, zero), jnp.where(low_half, zero, q)], axis=0
+                )
+                k = jnp.concatenate([kv_ref[r, lanes] for r in k_rows], axis=0)
+                v_lanes = slice(MODEL + h * 128, MODEL + (h + 1) * 128)
+                v = jnp.concatenate([kv_ref[r, v_lanes] for r in k_rows], axis=0)
+                logits = dot_nt(q, k) + bias
+                top = jnp.max(logits, axis=-1, keepdims=True)
+                share = jnp.exp(logits - top).astype(bf16)
+                both = dot(share, jnp.concatenate([v, ones], axis=1))
+                mixed = jnp.where(low_half, both[:64, :128], both[64:, :128])
+                total = jnp.where(low_half, both[:64, 128:], both[64:, 128:])
+                picked = (mixed / total).astype(bf16)
+                for g in range(2):
+                    a_ref[a_rows[g], lanes] = picked[g * 32 : (g + 1) * 32, :]
         return carry
 
-    lax.fori_loop(0, 8, block, 0)
+    lax.fori_loop(0, tall, strip, 0, unroll=True)
+
+
+def rest_kernel(
+    place_ref, top_ref, bot_ref, left_ref, right_ref, stream_ref, qkv_ref, gain_ref, embed_ref,
+    w_ref, w_hbm, o_hbm, out_ref,
+    next_ref, o_ref, halo_ref, kv_ref, q_ref, mid_ref, att_ref, inp_ref, sem,
+):
+    copies = [
+        pltpu.make_async_copy(o_hbm.at[0], o_ref.at[0], sem.at[0]),
+        pltpu.make_async_copy(w_hbm.at[1], next_ref, sem.at[1]),
+        pltpu.make_async_copy(o_hbm.at[1], o_ref.at[1], sem.at[2]),
+    ]
     for copy in copies:
-        copy.wait()
-
-    if layer == 0:
-        for g in range(4):
-            rows = slice(g * GRP, (g + 1) * GRP)
-            stream = stream_ref[rows, :] + dot(att_ref[rows, :], o_ref[...])
-            out_ref[rows, :] = stream
-            inputs = normed(stream, gain_ref[1:2, :])
-            x_ref[rows, :] = inputs
-            xt_ref[g * HALO : (g + 1) * HALO, :] = inputs[:HALO, :]
-            xb_ref[g * HALO : (g + 1) * HALO, :] = inputs[GRP - HALO :, :]
-    else:
-        for g in range(4):
-            rows = slice(g * GRP, (g + 1) * GRP)
-            stream = stream_ref[rows, :] + dot(att_ref[rows, :], o_ref[...])
-            att_ref[rows, :] = stream.astype(bf16)
-        for r in range(0, 4 * GRP, GRP):
-            to = iota((GRP, 4 * GRP), 0) + r
-            source = iota((GRP, 4 * GRP), 1)
-            wanted = (to // 4 % 4) * GRP + (to // 16) * 4 + to % 4
-            out_ref[r : r + GRP, :] = dot(onehot(source == wanted), att_ref[...]).astype(bf16)
-
-
-def attend(layer, place, halos, stream, qkv, gain, embed, w, out_weight, qkv_weight):
+        copy.start()
+    step = 256
+    scale = jnp.asarray(0.125, bf16)
+
+    for g in range(4):
+        own = slice(g * GRP, (g + 1) * GRP)
+        at = (g + 1) * MID + 16
+        mid_ref[at : at + GRP, :] = stream_ref[own, :]
+        q_ref[at : at + GRP, :] = qkv_ref[own, :MODEL]
+        at = (g + 2) * WIDE + HALO
+        kv_ref[at : at + GRP, :] = qkv_ref[own, MODEL:]
+
+    def enter(piece, row):
+        stream = dot(piece, embed_ref[...])
+        halo_ref[row : row + piece.shape[0], :] = normed(stream, gain_ref[0:1, :])
+        return stream
+
+    def side(ref, g):
+        return jnp.concatenate(
+            [
+                ref[g * HALO : (g + 1) * HALO, :],
+                ref[2 * HALO + g * GRP : 2 * HALO + (g + 1) * GRP, :],
+                ref[2 * HALO + 2 * GRP + g * HALO : 2 * HALO + 2 * GRP + (g + 1) * HALO, :],
+            ],
+            axis=0,
+        )
+
+    first_q = WIDE
+    left_q = WIDE + 2 * EDGE
+    right_q = left_q + WIDE
+    last = right_q + WIDE
+    enter(side(left_ref, 0), 0)
+    top = enter(top_ref[...], first_q)
+    bottom = enter(bot_ref[...], first_q + EDGE)
+    for g in range(4):
+        at = (g + 1) * MID
+        mid_ref[at : at + 16, :] = top[g * HALO + 16 : (g + 1) * HALO, :]
+        mid_ref[at + 16 + GRP : at + MID, :] = bottom[g * HALO : g * HALO + 16, :]
+    mid_ref[:MID, :] = enter(side(left_ref, 1), left_q)[16 : 16 + MID, :]
+    mid_ref[5 * MID :, :] = enter(side(right_ref, 0), right_q)[16 : 16 + MID, :]
+    enter(side(right_ref, 1), last)
+    for m in range(0, 3 * MODEL, step):
+        if m < MODEL:
+            lanes = slice(m, m + step)
+            part = dot(halo_ref[first_q:last, :], w_ref[:, lanes]).astype(bf16) * scale
+            for g in range(4):
+                at = (g + 1) * MID
+                q_ref[at : at + 16, lanes] = part[g * HALO + 16 : (g + 1) * HALO, :]
+                q_ref[at + 16 + GRP : at + MID, lanes] = part[
+                    EDGE + g * HALO : EDGE + g * HALO + 16, :
+                ]
+            at = left_q - first_q + 16
+            q_ref[:MID, lanes] = part[at : at + MID, :]
+            at = right_q - first_q + 16
+            q_ref[5 * MID :, lanes] = part[at : at + MID, :]
+        else:
+            lanes = slice(m - MODEL, m - MODEL + step)
+            part = dot(halo_ref[...], w_ref[:, m : m + step]).astype(bf16)
+            kv_ref[:WIDE, lanes] = part[:WIDE, :]
+            kv_ref[WIDE : 2 * WIDE, lanes] = part[left_q:right_q, :]
+            kv_ref[6 * WIDE :, lanes] = part[right_q:, :]
+            for g in range(4):
+                at = (g + 2) * WIDE
+                kv_ref[at : at + HALO, lanes] = part[first_q + g * HALO : first_q + (g + 1) * HALO, :]
+                kv_ref[at + HALO + GRP : at + WIDE, lanes] = part[
+                    first_q + EDGE + g * HALO : first_q + EDGE + (g + 1) * HALO, :
+                ]
+
+    ends = (place_ref[2], place_ref[3])
+    attention(
+        q_ref, 0, MID, kv_ref, WIDE, att_ref, MID, 5, 3, place_ref[0] - 8, place_ref[1] - 8, ends
+    )
+    copies[0].wait()
+    for g in range(6):
+        rows = slice(g * MID, (g + 1) * MID)
+        stream = mid_ref[rows, :] + dot(att_ref[rows, :], o_ref[0])
+        mid_ref[rows, :] = stream
+        inp_ref[rows, :] = normed(stream, gain_ref[1:2, :])
+
+    copies[1].wait()
+    for m in range(0, 3 * MODEL, step):
+        if m < MODEL:
+            part = dot(inp_ref[MID : 5 * MID, :], next_ref[:, m : m + step]).astype(bf16) * scale
+            q_ref[: 4 * MID, m : m + step] = part
+        else:
+            part = dot(inp_ref[...], next_ref[:, m : m + step]).astype(bf16)
+            kv_ref[: 6 * MID, m - MODEL : m - MODEL + step] = part
+    attention(
+        q_ref, 16, MID, kv_ref, MID, att_ref, GRP, 4, 2, place_ref[0] - 4, place_ref[1] - 4, ends
+    )
+    copies[2].wait()
+    for g in range(4):
+        rows = slice(g * GRP, (g + 1) * GRP)
+        at = (g + 1) * MID + 16
+        stream = mid_ref[at : at + GRP, :] + dot(att_ref[rows, :], o_ref[1])
+        inp_ref[rows, :] = stream.astype(bf16)
+    for r in range(0, 4 * GRP, GRP):
+        to = iota((GRP, 4 * GRP), 0) + r
+        source = iota((GRP, 4 * GRP), 1)
+        wanted = (to // 4 % 4) * GRP + (to // 16) * 4 + to % 4
+        out_ref[r : r + GRP, :] = dot(onehot(source == wanted), inp_ref[: 4 * GRP, :]).astype(bf16)
+
+
+def rest(place, halos, stream, qkv, gain, embed, w, qkv_weight, out_weight):
     hbm = pl.BlockSpec(memory_space=pltpu.HBM)
     vmem = pl.BlockSpec(memory_space=pltpu.VMEM)
     smem = pl.BlockSpec(memory_space=pltpu.SMEM)
-    operands = [place, *halos, stream, qkv]
-    specs = [smem] + [vmem] * 6
-    if layer == 0:
-        operands += [gain, in_vmem(embed)]
-        specs += [vmem, vmem]
-        out_shape = [
-            jax.ShapeDtypeStruct((4 * GRP, MODEL), f32),
-            jax.ShapeDtypeStruct((4 * GRP, MODEL), bf16),
-            jax.ShapeDtypeStruct((EDGE, MODEL), bf16),
-            jax.ShapeDtypeStruct((EDGE, MODEL), bf16),
-        ]
-    else:
-        out_shape = jax.ShapeDtypeStruct((4 * GRP, MODEL), bf16)
-    operands += [in_vmem(w), in_hbm(out_weight)]
-    specs += [vmem, hbm]
-    if layer == 0:
-        operands.append(in_hbm(qkv_weight))
-        specs.append(hbm)
-        out_shape.append(pltpu.VMEM((MODEL, 3 * MODEL), bf16))
     return pl.pallas_call(
-        functools.partial(attend_kernel, layer),
-        out_shape=out_shape,
-        in_specs=specs,
+        rest_kernel,
+        out_shape=jax.ShapeDtypeStruct((4 * GRP, MODEL), bf16),
+        in_specs=[smem] + [vmem] * 9 + [hbm] * 2,
         scratch_shapes=[
-            pltpu.VMEM((2 * EDGE + 2 * FULL, MODEL), bf16),
-            pltpu.VMEM((6 * FULL, 2 * MODEL), bf16),
-            pltpu.VMEM((4 * GRP, MODEL), bf16),
-            pltpu.VMEM((MODEL, MODEL), bf16),
-            pltpu.SemaphoreType.DMA((2,)),
+            pltpu.VMEM((MODEL, 3 * MODEL), bf16),
+            pltpu.VMEM((2, MODEL, MODEL), bf16),
+            pltpu.VMEM((2 * EDGE + 2 * SIDE, MODEL), bf16),
+            pltpu.VMEM((8 * WIDE, 2 * MODEL), bf16),
+            pltpu.VMEM((6 * MID, MODEL), bf16),
+            pltpu.VMEM((6 * MID, MODEL), f32),
+            pltpu.VMEM((6 * MID, MODEL), bf16),
+            pltpu.VMEM((6 * MID, MODEL), bf16),
+            pltpu.SemaphoreType.DMA((3,)),
         ],
-        compiler_params=pltpu.CompilerParams(vmem_limit_bytes=VMEM_BYTES),
-        name="attend%d" % layer,
-    )(*operands)
+        compiler_params=pltpu.CompilerParams(vmem_limit_bytes=LARGE_BYTES),
+        name="rest",
+    )(
+        place, *halos, stream, qkv, gain, in_vmem(embed), in_vmem(w),
+        in_hbm(qkv_weight), in_hbm(out_weight),
+    )
 
 
 def shifted(cells, axis, by):
@@ -432,8 +472,9 @@
 def around(x, first, last):
     top = shifted(last, "row", 1)
     bottom = shifted(first, "row", -1)
-    right_edge = jnp.concatenate([top[3 * HALO :], x[3 * GRP :], bottom[3 * HALO :]], axis=0)
-    left_edge = jnp.concatenate([top[:HALO], x[:GRP], bottom[:HALO]], axis=0)
+    two = 2 * HALO
+    right_edge = jnp.concatenate([top[two:], x[2 * GRP :], bottom[two:]], axis=0)
+    left_edge = jnp.concatenate([top[:two], x[: 2 * GRP], bottom[:two]], axis=0)
     left = shifted(right_edge, "col", 1)
     right = shifted(left_edge, "col", -1)
     return top, bottom, left, right
@@ -453,15 +494,11 @@
     embed = embed_weight.reshape(CH, 8, 8, MODEL).transpose(1, 0, 2, 3).reshape(PATCH, MODEL)
     payload = pack(dest, offsets, profile_index, profiles, scans)
     payload = lax.all_to_all(payload, ("row", "col"), split_axis=0, concat_axis=0, tiled=True)
+    payload, place = lax.optimization_barrier((payload, place))
     x, first, last, embed, w = merge(payload, profiles, embed, qkv_weight)
     halos = around(x, first, last)
-    stream, qkv = own_part(0, x, embed, attn_gain, w)
-    stream, x, first, last, w = attend(
-        0, place, halos, stream, qkv, attn_gain, embed, w, out_weight, qkv_weight
-    )
-    halos = around(x, first, last)
-    qkv = own_part(1, x, None, None, w)
-    tokens = attend(1, place, halos, stream, qkv, None, None, w, out_weight, None)
+    stream, qkv = own_part(x, embed, attn_gain, w)
+    tokens = rest(place, halos, stream, qkv, attn_gain, embed, w, qkv_weight, out_weight)
     return tokens.reshape(TOK_H, TOK_W, MODEL)
 
 

time: 107 us -> 99.4 us (0.929)
  starting transfers between devices: 28.4 us -> 19.8 us
  Pallas kernels: 37.8 us -> 39.5 us
    ppermute x8 -> x4, starting transfers between devices: 17.3 us -> 8.63 us  [shifted(): lax.ppermute(cells, axis, [(i, (i + by) % count) for i in range(count)])]
    pallas_call x4 -> x2, Pallas kernels: 29.3 us -> 31.1 us  [the longest x1 26.7 us: rest(): pl.pallas_call(rest_kernel, out_shape=jax.ShapeDtypeStruct((4 * GRP, MODE...]
    ppermute x8 -> x4, waiting for transfers between devices: 7.36 us -> 6.93 us  [shifted(): lax.ppermute(cells, axis, [(i, (i + by) % count) for i in range(count)])]
  transfers between devices with their start and end apart: 9 -> 5, of which waited for: 4 -> 3; matrix products, arithmetic and copies ran while one was open for 1% -> 1% of each run, Pallas kernels for 7% -> 4%
where the time goes in v2:
time: 99.4 us; the launch traced here: 99.1 us
  Pallas kernels  39.5 us (40%)
  waiting for transfers between devices  38.3 us (39%)
  starting transfers between devices  19.8 us (20%)
  local copies, waits for them, and re-layouts  1.14 us (1%)
    all_to_all x1, waiting for transfers between devices, per_device(): lax.all_to_all(payload, ('row', 'col'), split_axis=0, concat_axis=0, tile...  31.3 us
    pallas_call x1, Pallas kernels, rest(): pl.pallas_call(rest_kernel, out_shape=jax.ShapeDtypeStruct((4 * GRP, MODE...  26.7 us
    all_to_all x1, starting transfers between devices, per_device(): lax.all_to_all(payload, ('row', 'col'), split_axis=0, concat_axis=0, tile...  11.1 us
    ppermute x4, starting transfers between devices, shifted(): lax.ppermute(cells, axis, [(i, (i + by) % count) for i in range(count)])  8.63 us
    ppermute x4, waiting for transfers between devices, shifted(): lax.ppermute(cells, axis, [(i, (i + by) % count) for i in range(count)])  6.93 us
    pallas_call x1, Pallas kernels, pack(): pl.pallas_call(pack_kernel, out_shape=jax.ShapeDtypeStruct((rows, CH * 12...  5.32 us
    pallas_call x1, Pallas kernels, own_part(): pl.pallas_call(own_kernel, out_shape=[jax.ShapeDtypeStruct((4 * GRP, MODE...  4.39 us
    pallas_call x1, Pallas kernels, merge(): pl.pallas_call(merge_kernel, out_shape=[jax.ShapeDtypeStruct((4 * GRP, PA...  3.15 us
  transfers between devices with their start and end apart: 5, of which 3 were waited for; matrix products, arithmetic and copies ran while one was open for 1% of the time, Pallas kernels for 4%

profile of v2, /device:TPU:0, one launch (start us, length us, event | category | flops | bytes accessed | tf_op | source)
XLA Modules:
  0.0 99.1 jit_solution(10497068331295683484)
XLA Ops:
  0.0 5.3 %pack.1 = bf16[1024,1152]{1,0:T(8,128)(2,1)} custom-call(s32[1,128]{1,0:T(1,128)} %bitcast.17, s32[1,128]{1,0:T(1,128)} %bitcast.18, s32[1,128]{1,0:T(1,128)} %bitcast.19, f32[16,4,128]{2,1,0:T(4,128)} %prof_ref.1, f32[4096,128]{1,0:T(8,128)} %bitcast.15), custom_call_target="tpu_custom_call" | custom-call | tf_op jit(solution)/shard_map/pack/pallas_call | solution.py:116
  5.3 0.0 copy-start.2
  5.3 0.0 copy-start
  5.4 11.1 %all-to-all-start = ((bf16[128,8,1152]{2,1,0:T(8,128)(2,1)}), bf16[128,8,1152]{2,1,0:T(8,128)(2,1)S(1)}, u32[]{:S(2)}, u32[]{:S(2)}) async-start(bf16[128,8,1152]{2,1,0:T(8,128)(2,1)} %bitcast.4), calls=%async_computation | async-start | bytes 4718592 | tf_op jit(solution)/shard_map/all_to_all | solution.py:496
  16.5 0.0 copy-done.2
  16.5 1.1 %copy.10 = bf16[8,8,8,1024]{3,2,0,1:T(8,128)(2,1)} copy(bf16[8,8,8,1024]{3,2,1,0:T(8,128)(2,1)S(1)} %bitcast.16) | data formatting | bytes 2097152 | tf_op jit(solution)/shard_map/reshape | solution.py:494
  17.6 0.1 pad_add_fusion.place_ref
  17.7 31.3 %all-to-all-done = bf16[128,8,1152]{2,1,0:T(8,128)(2,1)S(1)} async-done(((bf16[128,8,1152]{2,1,0:T(8,128)(2,1)}), bf16[128,8,1152]{2,1,0:T(8,128)(2,1)S(1)}, u32[]{:S(2)}, u32[]{:S(2)}) %all-to-all-start) | async-done | bytes 2359328 | tf_op jit(solution)/shard_map/all_to_all | solution.py:496
  49.0 0.0 copy-done
  49.0 3.2 %merge.1 = (bf16[512,512]{1,0:T(8,128)(2,1)S(1)}, bf16[128,512]{1,0:T(8,128)(2,1)S(1)}, bf16[128,512]{1,0:T(8,128)(2,1)S(1)}, bf16[512,1024]{1,0:T(8,128)(2,1)S(1)}, bf16[1024,3072]{1,0:T(8,128)(2,1)S(1)}) custom-call(bf16[1024,1152]{1,0:T(8,128)(2,1)S(1)} %bitcast.13, f32[16,4,128]{2,1,0:T(4,128)S(1)} %copy-done, bf16[512,1024]{1,0:T(8,128)(2,1)} %bitcast.14, ...), custom_call_target="tpu_custom_call" | custom-call | tf_op jit(solution)/shard_map/merge/pallas_call | solution.py:214
  52.2 0.0 copy-start.1
  52.2 0.0 collective-permute-start
  52.2 2.9 %collective-permute-start.1 = (bf16[128,512]{1,0:T(8,128)(2,1)S(1)}, bf16[128,512]{1,0:T(8,128)(2,1)S(1)}, u32[]{:S(2)}, u32[]{:S(2)}) collective-permute-start(bf16[128,512]{1,0:T(8,128)(2,1)S(1)} %get-tuple-element.17), channel_id=1, source_target_pairs={{0,112},{16,0},{32,16},{48,32},{64,48},{80,64},{96,80},{112,96},{1... | collective-permute-start | bytes 393224 | tf_op jit(solution)/shard_map/ppermute | solution.py:469
  55.2 2.6 %collective-permute-done.top_ref = bf16[128,512]{1,0:T(8,128)(2,1)S(1)} collective-permute-done((bf16[128,512]{1,0:T(8,128)(2,1)S(1)}, bf16[128,512]{1,0:T(8,128)(2,1)S(1)}, u32[]{:S(2)}, u32[]{:S(2)}) %collective-permute-start) | collective-permute-done | bytes 131104 | tf_op jit(solution)/shard_map/ppermute | solution.py:469
  57.8 0.0 collective-permute-done.1.bot_ref
  57.9 0.9 collective-permute-start.2
  58.8 4.7 %collective-permute-start.3 = (bf16[384,512]{1,0:T(8,128)(2,1)S(1)}, bf16[384,512]{1,0:T(8,128)(2,1)S(1)}, u32[]{:S(2)}, u32[]{:S(2)}) collective-permute-start(bf16[384,512]{1,0:T(8,128)(2,1)S(1)} %pad_maximum_fusion.1), channel_id=1, source_target_pairs={{0,15},{1,0},{2,1},{3,2},{4,3},{5,4},{6,5},{7,6},{8,7},{9,8},{10,9... | collective-permute-start | bytes 1179656 | tf_op jit(solution)/shard_map/ppermute | solution.py:469
  63.6 0.0 copy-done.1
  63.6 4.4 %own.1 = (f32[512,1024]{1,0:T(8,128)S(1)}, bf16[512,3072]{1,0:T(8,128)(2,1)S(1)}) custom-call(bf16[512,512]{1,0:T(8,128)(2,1)S(1)} %get-tuple-element.18.x_ref, bf16[512,1024]{1,0:T(8,128)(2,1)S(1)} %get-tuple-element.19.embed_ref, f32[2,1024]{1,0:T(2,128)S(1)} %copy-done.1, bf16[1024,3072]{1,0:T(8,128)(2,1)S(1)} %get-tuple-element.20.w_ref), custom_call_target="tpu_custom_call" | custom-call | flops 3221225472 | bytes 12582912 | tf_op jit(solution)/shard_map/own/pallas_call | solution.py:256
  68.0 4.3 %collective-permute-done.2.left_ref = bf16[384,512]{1,0:T(8,128)(2,1)S(1)} collective-permute-done((bf16[384,512]{1,0:T(8,128)(2,1)S(1)}, bf16[384,512]{1,0:T(8,128)(2,1)S(1)}, u32[]{:S(2)}, u32[]{:S(2)}) %collective-permute-start.2) | collective-permute-done | bytes 393248 | tf_op jit(solution)/shard_map/ppermute | solution.py:469
  72.3 0.0 collective-permute-done.3.right_ref
  72.3 26.7 %rest.1 = bf16[512,1024]{1,0:T(8,128)(2,1)} custom-call(s32[4]{0:T(128)S(1)} %pad_add_fusion.place_ref, bf16[128,512]{1,0:T(8,128)(2,1)S(1)} %collective-permute-done.top_ref, bf16[128,512]{1,0:T(8,128)(2,1)S(1)} %collective-permute-done.1.bot_ref, bf16[384,512]{1,0:T(8,128)(2,1)S(1)} %collective-permute-done.2.left_ref, ...), custom_call_target="tpu_custom_call" | custom-call | tf_op jit(solution)/shard_map/rest/pallas_call | solution.py:444
  (6 shorter events, 0.1 us)
Async XLA Ops:
  5.3 11.2 %copy-start.2 = (bf16[512,1024]{1,0:T(8,128)(2,1)S(1)}, bf16[512,1024]{1,0:T(8,128)(2,1)}, u32[]{:S(2)}) copy-start(bf16[512,1024]{1,0:T(8,128)(2,1)} %param.14) | copy-start | bytes 3145732
  5.3 43.7 %copy-start = (f32[16,4,128]{2,1,0:T(4,128)S(1)}, f32[16,4,128]{2,1,0:T(4,128)}, u32[]{:S(2)}) copy-start(f32[16,4,128]{2,1,0:T(4,128)} %prof_ref.1) | copy-start | bytes 98308
  5.4 43.6 %all-to-all-start = ((bf16[128,8,1152]{2,1,0:T(8,128)(2,1)}), bf16[128,8,1152]{2,1,0:T(8,128)(2,1)S(1)}, u32[]{:S(2)}, u32[]{:S(2)}) async-start(bf16[128,8,1152]{2,1,0:T(8,128)(2,1)} %bitcast.4), calls=%async_computation | async-start | bytes 4718592 | tf_op jit(solution)/shard_map/all_to_all | solution.py:496
  52.2 11.4 %copy-start.1 = (f32[2,1024]{1,0:T(2,128)S(1)}, f32[2,1024]{1,0:T(2,128)}, u32[]{:S(2)}) copy-start(f32[2,1024]{1,0:T(2,128)} %gain_ref.3) | copy-start | bytes 24580
  52.2 5.6 %collective-permute-start = (bf16[128,512]{1,0:T(8,128)(2,1)S(1)}, bf16[128,512]{1,0:T(8,128)(2,1)S(1)}, u32[]{:S(2)}, u32[]{:S(2)}) collective-permute-start(bf16[128,512]{1,0:T(8,128)(2,1)S(1)} %get-tuple-element.16), channel_id=1, source_target_pairs={{0,16},{16,32},{32,48},{48,64},{64,80},{80,96},{96,112},{112,0},{1... | collective-permute-start | bytes 393224 | tf_op jit(solution)/shard_map/ppermute | solution.py:469
  52.2 5.6 %collective-permute-start.1 = (bf16[128,512]{1,0:T(8,128)(2,1)S(1)}, bf16[128,512]{1,0:T(8,128)(2,1)S(1)}, u32[]{:S(2)}, u32[]{:S(2)}) collective-permute-start(bf16[128,512]{1,0:T(8,128)(2,1)S(1)} %get-tuple-element.17), channel_id=1, source_target_pairs={{0,112},{16,0},{32,16},{48,32},{64,48},{80,64},{96,80},{112,96},{1... | collective-permute-start | bytes 393224 | tf_op jit(solution)/shard_map/ppermute | solution.py:469
  57.9 14.4 %collective-permute-start.2 = (bf16[384,512]{1,0:T(8,128)(2,1)S(1)}, bf16[384,512]{1,0:T(8,128)(2,1)S(1)}, u32[]{:S(2)}, u32[]{:S(2)}) collective-permute-start(bf16[384,512]{1,0:T(8,128)(2,1)S(1)} %pad_maximum_fusion), channel_id=1, source_target_pairs={{0,1},{1,2},{2,3},{3,4},{4,5},{5,6},{6,7},{7,8},{8,9},{9,10},{10,1... | collective-permute-start | bytes 1179656 | tf_op jit(solution)/shard_map/ppermute | solution.py:469
  58.8 13.4 %collective-permute-start.3 = (bf16[384,512]{1,0:T(8,128)(2,1)S(1)}, bf16[384,512]{1,0:T(8,128)(2,1)S(1)}, u32[]{:S(2)}, u32[]{:S(2)}) collective-permute-start(bf16[384,512]{1,0:T(8,128)(2,1)S(1)} %pad_maximum_fusion.1), channel_id=1, source_target_pairs={{0,15},{1,0},{2,1},{3,2},{4,3},{5,4},{6,5},{7,6},{8,7},{9,8},{10,9... | collective-permute-start | bytes 1179656 | tf_op jit(solution)/shard_map/ppermute | solution.py:469

commit v3 on v2

--- a/solution.py
+++ b/solution.py
@@ -20,11 +20,10 @@
 WIDE = 192
 HALO = 32
 EDGE = 4 * HALO
-SIDE = 2 * WIDE
 META = 128
 CHUNKS = 4
 VMEM_BYTES = 20 * 1024 * 1024
-LARGE_BYTES = 40 * 1024 * 1024
+LARGE_BYTES = 30 * 1024 * 1024
 
 f32 = jnp.float32
 bf16 = jnp.bfloat16
@@ -239,36 +238,64 @@
     return (moved * lax.rsqrt(spread + 1e-05) * gain).astype(bf16)
 
 
-def own_kernel(x_ref, embed_ref, gain_ref, w_ref, stream_ref, qkv_ref, inp_ref):
-    for r in range(0, 4 * GRP, GRP):
-        stream = dot(x_ref[r : r + GRP, :], embed_ref[...])
-        stream_ref[r : r + GRP, :] = stream
-        inp_ref[r : r + GRP, :] = normed(stream, gain_ref[0:1, :])
+def own_kernel(
+    place_ref, x_ref, top_ref, bot_ref, embed_ref, gain_ref, w_ref,
+    stream_ref, q_ref, kv_ref, att_ref, inp_ref,
+):
+    for g in range(4):
+        edge = slice(g * HALO, (g + 1) * HALO)
+        tokens = jnp.concatenate(
+            [top_ref[edge, :], x_ref[g * GRP : (g + 1) * GRP, :], bot_ref[edge, :]], axis=0
+        )
+        stream = dot(tokens, embed_ref[...])
+        rows = slice(g * WIDE, (g + 1) * WIDE)
+        stream_ref[rows, :] = stream
+        inp_ref[rows, :] = normed(stream, gain_ref[0:1, :])
+    project(inp_ref[...], inp_ref[...], w_ref, q_ref, kv_ref)
+    attention(
+        [1],
+        5,
+        lambda g: (q_ref, (g - 1) * WIDE + 16),
+        lambda g: (kv_ref, (g - 2) * WIDE),
+        lambda g: (att_ref, (g - 2) * MID),
+        place_ref[0] - 8,
+        place_ref[1] - 8,
+        (place_ref[2], place_ref[3]),
+    )
+
+
+def project(query_inputs, inputs, w_ref, q_ref, kv_ref):
     step = 256
-    for m in range(0, 3 * MODEL, step):
-        part = dot(inp_ref[...], w_ref[:, m : m + step]).astype(bf16)
-        if m < MODEL:
-            part = part * jnp.asarray(0.125, bf16)
-        qkv_ref[:, m : m + step] = part
-
-
-def own_part(x, embed, gain, w):
+    for m in range(0, MODEL, step):
+        part = dot(query_inputs, w_ref[:, m : m + step]).astype(bf16)
+        q_ref[: part.shape[0], m : m + step] = part * jnp.asarray(0.125, bf16)
+    for m in range(0, 2 * MODEL, step):
+        part = dot(inputs, w_ref[:, MODEL + m : MODEL + m + step]).astype(bf16)
+        kv_ref[: part.shape[0], m : m + step] = part
+
+
+def own_part(place, x, top, bottom, embed, gain, w):
+    vmem = pl.BlockSpec(memory_space=pltpu.VMEM)
+    smem = pl.BlockSpec(memory_space=pltpu.SMEM)
     return pl.pallas_call(
         own_kernel,
         out_shape=[
-            jax.ShapeDtypeStruct((4 * GRP, MODEL), f32),
-            jax.ShapeDtypeStruct((4 * GRP, 3 * MODEL), bf16),
+            jax.ShapeDtypeStruct((4 * WIDE, MODEL), f32),
+            jax.ShapeDtypeStruct((4 * WIDE, MODEL), bf16),
+            jax.ShapeDtypeStruct((4 * WIDE, 2 * MODEL), bf16),
+            jax.ShapeDtypeStruct((2 * MID, MODEL), bf16),
         ],
-        scratch_shapes=[pltpu.VMEM((4 * GRP, MODEL), bf16)],
+        in_specs=[smem] + [vmem] * 6,
+        scratch_shapes=[pltpu.VMEM((4 * WIDE, MODEL), bf16)],
         compiler_params=pltpu.CompilerParams(vmem_limit_bytes=VMEM_BYTES),
         cost_estimate=pl.CostEstimate(
-            flops=2 * 4 * GRP * MODEL * 3 * MODEL, bytes_accessed=12 << 20, transcendentals=0
+            flops=2 * 4 * WIDE * MODEL * 3 * MODEL, bytes_accessed=12 << 20, transcendentals=0
         ),
         name="own",
-    )(x, in_vmem(embed), gain, in_vmem(w))
-
-
-def attention(q_ref, q_at, q_pitch, kv_ref, k_pitch, a_ref, a_pitch, tall, broad, row, col, ends):
+    )(place, x, top, bottom, in_vmem(embed), gain, in_vmem(w))
+
+
+def attention(broad, tall, q_of, kv_of, a_of, row, col, ends):
     query = iota((64, 256), 0)
     key = iota((64, 256), 1)
     row_gap = (key % 64) // 4 - 4 - (query % 32) // 4
@@ -282,33 +309,27 @@
     zero = jnp.zeros((64, 128), bf16)
     ones = jnp.ones((256, 128), bf16)
 
-    def strip(bi, carry):
+    for bi in range(tall):
         at_row = key_row + bi * 8
         row_inside = (at_row >= 0) & (at_row < ends[0])
-        for bj in range(broad):
+        for bj in broad:
             at_col = key_col + bj * 8
             inside = row_inside & (at_col >= 0) & (at_col < ends[1])
             bias = near_bias + jnp.where(inside, 0.0, -1e30)
             bias = jnp.concatenate([bias, bias], axis=0)
-            q_rows = [
-                pl.ds(pl.multiple_of((2 * bj + g) * q_pitch + q_at + bi * 32, 16), 32)
-                for g in range(2)
-            ]
-            a_rows = [
-                pl.ds(pl.multiple_of((2 * bj + g) * a_pitch + bi * 32, 32), 32) for g in range(2)
-            ]
-            k_rows = [
-                pl.ds(pl.multiple_of((2 * bj + g) * k_pitch + bi * 32, 32), 64) for g in range(4)
-            ]
+            q_from = [q_of(2 * bj + g) for g in range(2)]
+            k_from = [kv_of(2 * bj + g) for g in range(4)]
+            a_to = [a_of(2 * bj + g) for g in range(2)]
+            at = bi * 32
             for h in range(HEADS // 2):
                 lanes = slice(h * 128, (h + 1) * 128)
-                q = jnp.concatenate([q_ref[r, lanes] for r in q_rows], axis=0)
+                q = jnp.concatenate([r[b + at : b + at + 32, lanes] for r, b in q_from], axis=0)
                 q = jnp.concatenate(
                     [jnp.where(low_half, q, zero), jnp.where(low_half, zero, q)], axis=0
                 )
-                k = jnp.concatenate([kv_ref[r, lanes] for r in k_rows], axis=0)
+                k = jnp.concatenate([r[b + at : b + at + 64, lanes] for r, b in k_from], axis=0)
                 v_lanes = slice(MODEL + h * 128, MODEL + (h + 1) * 128)
-                v = jnp.concatenate([kv_ref[r, v_lanes] for r in k_rows], axis=0)
+                v = jnp.concatenate([r[b + at : b + at + 64, v_lanes] for r, b in k_from], axis=0)
                 logits = dot_nt(q, k) + bias
                 top = jnp.max(logits, axis=-1, keepdims=True)
                 share = jnp.exp(logits - top).astype(bf16)
@@ -316,17 +337,14 @@
                 mixed = jnp.where(low_half, both[:64, :128], both[64:, :128])
                 total = jnp.where(low_half, both[:64, 128:], both[64:, 128:])
                 picked = (mixed / total).astype(bf16)
-                for g in range(2):
-                    a_ref[a_rows[g], lanes] = picked[g * 32 : (g + 1) * 32, :]
-        return carry
-
-    lax.fori_loop(0, tall, strip, 0, unroll=True)
+                for g, (r, b) in enumerate(a_to):
+                    r[b + at : b + at + 32, lanes] = picked[g * 32 : (g + 1) * 32, :]
 
 
 def rest_kernel(
-    place_ref, top_ref, bot_ref, left_ref, right_ref, stream_ref, qkv_ref, gain_ref, embed_ref,
+    place_ref, left_ref, right_ref, stream_ref, oq_ref, okv_ref, oatt_ref, gain_ref, embed_ref,
     w_ref, w_hbm, o_hbm, out_ref,
-    next_ref, o_ref, halo_ref, kv_ref, q_ref, mid_ref, att_ref, inp_ref, sem,
+    next_ref, o_ref, side_ref, sq_ref, skv_ref, q_ref, kv_ref, mid_ref, att_ref, inp_ref, sem,
 ):
     copies = [
         pltpu.make_async_copy(o_hbm.at[0], o_ref.at[0], sem.at[0]),
@@ -335,100 +353,67 @@
     ]
     for copy in copies:
         copy.start()
-    step = 256
-    scale = jnp.asarray(0.125, bf16)
-
-    for g in range(4):
-        own = slice(g * GRP, (g + 1) * GRP)
-        at = (g + 1) * MID + 16
-        mid_ref[at : at + GRP, :] = stream_ref[own, :]
-        q_ref[at : at + GRP, :] = qkv_ref[own, :MODEL]
-        at = (g + 2) * WIDE + HALO
-        kv_ref[at : at + GRP, :] = qkv_ref[own, MODEL:]
-
-    def enter(piece, row):
-        stream = dot(piece, embed_ref[...])
-        halo_ref[row : row + piece.shape[0], :] = normed(stream, gain_ref[0:1, :])
-        return stream
-
-    def side(ref, g):
-        return jnp.concatenate(
+
+    for n in range(4):
+        ref, g = (left_ref, right_ref)[n // 2], n % 2
+        below = 2 * HALO + 2 * GRP
+        tokens = jnp.concatenate(
             [
                 ref[g * HALO : (g + 1) * HALO, :],
                 ref[2 * HALO + g * GRP : 2 * HALO + (g + 1) * GRP, :],
-                ref[2 * HALO + 2 * GRP + g * HALO : 2 * HALO + 2 * GRP + (g + 1) * HALO, :],
+                ref[below + g * HALO : below + (g + 1) * HALO, :],
             ],
             axis=0,
         )
-
-    first_q = WIDE
-    left_q = WIDE + 2 * EDGE
-    right_q = left_q + WIDE
-    last = right_q + WIDE
-    enter(side(left_ref, 0), 0)
-    top = enter(top_ref[...], first_q)
-    bottom = enter(bot_ref[...], first_q + EDGE)
-    for g in range(4):
-        at = (g + 1) * MID
-        mid_ref[at : at + 16, :] = top[g * HALO + 16 : (g + 1) * HALO, :]
-        mid_ref[at + 16 + GRP : at + MID, :] = bottom[g * HALO : g * HALO + 16, :]
-    mid_ref[:MID, :] = enter(side(left_ref, 1), left_q)[16 : 16 + MID, :]
-    mid_ref[5 * MID :, :] = enter(side(right_ref, 0), right_q)[16 : 16 + MID, :]
-    enter(side(right_ref, 1), last)
-    for m in range(0, 3 * MODEL, step):
-        if m < MODEL:
-            lanes = slice(m, m + step)
-            part = dot(halo_ref[first_q:last, :], w_ref[:, lanes]).astype(bf16) * scale
-            for g in range(4):
-                at = (g + 1) * MID
-                q_ref[at : at + 16, lanes] = part[g * HALO + 16 : (g + 1) * HALO, :]
-                q_ref[at + 16 + GRP : at + MID, lanes] = part[
-                    EDGE + g * HALO : EDGE + g * HALO + 16, :
-                ]
-            at = left_q - first_q + 16
-            q_ref[:MID, lanes] = part[at : at + MID, :]
-            at = right_q - first_q + 16
-            q_ref[5 * MID :, lanes] = part[at : at + MID, :]
-        else:
-            lanes = slice(m - MODEL, m - MODEL + step)
-            part = dot(halo_ref[...], w_ref[:, m : m + step]).astype(bf16)
-            kv_ref[:WIDE, lanes] = part[:WIDE, :]
-            kv_ref[WIDE : 2 * WIDE, lanes] = part[left_q:right_q, :]
-            kv_ref[6 * WIDE :, lanes] = part[right_q:, :]
-            for g in range(4):
-                at = (g + 2) * WIDE
-                kv_ref[at : at + HALO, lanes] = part[first_q + g * HALO : first_q + (g + 1) * HALO, :]
-                kv_ref[at + HALO + GRP : at + WIDE, lanes] = part[
-                    first_q + EDGE + g * HALO : first_q + EDGE + (g + 1) * HALO, :
-                ]
+        stream = dot(tokens, embed_ref[...])
+        inp_ref[n * WIDE : (n + 1) * WIDE, :] = normed(stream, gain_ref[0:1, :])
+        if n in (1, 2):
+            side_ref[(n - 1) * WIDE : n * WIDE, :] = stream
+    project(inp_ref[WIDE : 3 * WIDE, :], inp_ref[: 4 * WIDE, :], w_ref, sq_ref, skv_ref)
+
+    def q_of(g):
+        if g in (0, 5):
+            return sq_ref, (g // 5) * WIDE + 16
+        return oq_ref, (g - 1) * WIDE + 16
+
+    def kv_of(g):
+        if g in (0, 1, 6, 7):
+            return skv_ref, (g if g < 2 else g - 4) * WIDE
+        return okv_ref, (g - 2) * WIDE
 
     ends = (place_ref[2], place_ref[3])
     attention(
-        q_ref, 0, MID, kv_ref, WIDE, att_ref, MID, 5, 3, place_ref[0] - 8, place_ref[1] - 8, ends
+        [0, 2], 5, q_of, kv_of, lambda g: (att_ref, g * MID), place_ref[0] - 8, place_ref[1] - 8, ends
     )
     copies[0].wait()
     for g in range(6):
         rows = slice(g * MID, (g + 1) * MID)
-        stream = mid_ref[rows, :] + dot(att_ref[rows, :], o_ref[0])
-        mid_ref[rows, :] = stream
+        if g in (0, 5):
+            before = side_ref[(g // 5) * WIDE + 16 : (g // 5) * WIDE + 16 + MID, :]
+        else:
+            before = stream_ref[(g - 1) * WIDE + 16 : (g - 1) * WIDE + 16 + MID, :]
+        mixed = oatt_ref[(g - 2) * MID : (g - 1) * MID, :] if g in (2, 3) else att_ref[rows, :]
+        stream = before + dot(mixed, o_ref[0])
+        if g not in (0, 5):
+            mid_ref[(g - 1) * GRP : g * GRP, :] = stream[16 : 16 + GRP, :]
         inp_ref[rows, :] = normed(stream, gain_ref[1:2, :])
 
     copies[1].wait()
-    for m in range(0, 3 * MODEL, step):
-        if m < MODEL:
-            part = dot(inp_ref[MID : 5 * MID, :], next_ref[:, m : m + step]).astype(bf16) * scale
-            q_ref[: 4 * MID, m : m + step] = part
-        else:
-            part = dot(inp_ref[...], next_ref[:, m : m + step]).astype(bf16)
-            kv_ref[: 6 * MID, m - MODEL : m - MODEL + step] = part
+    project(inp_ref[MID : 5 * MID, :], inp_ref[...], next_ref, q_ref, kv_ref)
     attention(
-        q_ref, 16, MID, kv_ref, MID, att_ref, GRP, 4, 2, place_ref[0] - 4, place_ref[1] - 4, ends
+        [0, 1],
+        4,
+        lambda g: (q_ref, g * MID + 16),
+        lambda g: (kv_ref, g * MID),
+        lambda g: (att_ref, g * GRP),
+        place_ref[0] - 4,
+        place_ref[1] - 4,
+        ends,
     )
     copies[2].wait()
     for g in range(4):
         rows = slice(g * GRP, (g + 1) * GRP)
-        at = (g + 1) * MID + 16
-        stream = mid_ref[at : at + GRP, :] + dot(att_ref[rows, :], o_ref[1])
+        stream = mid_ref[rows, :] + dot(att_ref[rows, :], o_ref[1])
         inp_ref[rows, :] = stream.astype(bf16)
     for r in range(0, 4 * GRP, GRP):
         to = iota((GRP, 4 * GRP), 0) + r
@@ -437,7 +422,7 @@
         out_ref[r : r + GRP, :] = dot(onehot(source == wanted), inp_ref[: 4 * GRP, :]).astype(bf16)
 
 
-def rest(place, halos, stream, qkv, gain, embed, w, qkv_weight, out_weight):
+def rest(place, left, right, own, gain, embed, w, qkv_weight, out_weight):
     hbm = pl.BlockSpec(memory_space=pltpu.HBM)
     vmem = pl.BlockSpec(memory_space=pltpu.VMEM)
     smem = pl.BlockSpec(memory_space=pltpu.SMEM)
@@ -448,10 +433,12 @@
         scratch_shapes=[
             pltpu.VMEM((MODEL, 3 * MODEL), bf16),
             pltpu.VMEM((2, MODEL, MODEL), bf16),
-            pltpu.VMEM((2 * EDGE + 2 * SIDE, MODEL), bf16),
-            pltpu.VMEM((8 * WIDE, 2 * MODEL), bf16),
-            pltpu.VMEM((6 * MID, MODEL), bf16),
-            pltpu.VMEM((6 * MID, MODEL), f32),
+            pltpu.VMEM((2 * WIDE, MODEL), f32),
+            pltpu.VMEM((2 * WIDE, MODEL), bf16),
+            pltpu.VMEM((4 * WIDE, 2 * MODEL), bf16),
+            pltpu.VMEM((4 * MID, MODEL), bf16),
+            pltpu.VMEM((6 * MID, 2 * MODEL), bf16),
+            pltpu.VMEM((4 * GRP, MODEL), f32),
             pltpu.VMEM((6 * MID, MODEL), bf16),
             pltpu.VMEM((6 * MID, MODEL), bf16),
             pltpu.SemaphoreType.DMA((3,)),
@@ -459,7 +446,7 @@
         compiler_params=pltpu.CompilerParams(vmem_limit_bytes=LARGE_BYTES),
         name="rest",
     )(
-        place, *halos, stream, qkv, gain, in_vmem(embed), in_vmem(w),
+        place, left, right, *own, gain, in_vmem(embed), in_vmem(w),
         in_hbm(qkv_weight), in_hbm(out_weight),
     )
 
@@ -496,9 +483,9 @@
     payload = lax.all_to_all(payload, ("row", "col"), split_axis=0, concat_axis=0, tiled=True)
     payload, place = lax.optimization_barrier((payload, place))
     x, first, last, embed, w = merge(payload, profiles, embed, qkv_weight)
-    halos = around(x, first, last)
-    stream, qkv = own_part(x, embed, attn_gain, w)
-    tokens = rest(place, halos, stream, qkv, attn_gain, embed, w, qkv_weight, out_weight)
+    top, bottom, left, right = around(x, first, last)
+    own = own_part(place, x, top, bottom, embed, attn_gain, w)
+    tokens = rest(place, left, right, own, attn_gain, embed, w, qkv_weight, out_weight)
     return tokens.reshape(TOK_H, TOK_W, MODEL)
 
 

time: 99.4 us -> 96.4 us (0.970)
  waiting for transfers between devices: 38.3 us -> 34 us
  Pallas kernels: 39.5 us -> 40.5 us
    pallas_call x1, Pallas kernels: 4.39 us -> 8.64 us  [own_part(): pl.pallas_call(own_kernel, out_shape=[jax.ShapeDtypeStruct((4 * WIDE, MOD...]
    ppermute x4, waiting for transfers between devices: 6.93 us -> 2.68 us  [shifted(): lax.ppermute(cells, axis, [(i, (i + by) % count) for i in range(count)])]
    pallas_call x1, Pallas kernels: 26.7 us -> 23.4 us  [rest(): pl.pallas_call(rest_kernel, out_shape=jax.ShapeDtypeStruct((4 * GRP, MODE...]
  transfers between devices with their start and end apart: 5 -> 5, of which waited for: 3 -> 3; matrix products, arithmetic and copies ran while one was open for 1% -> 1% of each run, Pallas kernels for 4% -> 9%
where the time goes in v3:
time: 96.4 us; the launch traced here: 95.9 us
  Pallas kernels  40.5 us (42%)
  waiting for transfers between devices  34 us (35%)
  starting transfers between devices  19.8 us (21%)
  local copies, waits for them, and re-layouts  1.14 us (1%)
    all_to_all x1, waiting for transfers between devices, per_device(): lax.all_to_all(payload, ('row', 'col'), split_axis=0, concat_axis=0, tile...  31.3 us
    pallas_call x1, Pallas kernels, rest(): pl.pallas_call(rest_kernel, out_shape=jax.ShapeDtypeStruct((4 * GRP, MODE...  23.4 us
    all_to_all x1, starting transfers between devices, per_device(): lax.all_to_all(payload, ('row', 'col'), split_axis=0, concat_axis=0, tile...  11.1 us
    pallas_call x1, Pallas kernels, own_part(): pl.pallas_call(own_kernel, out_shape=[jax.ShapeDtypeStruct((4 * WIDE, MOD...  8.64 us
    ppermute x4, starting transfers between devices, shifted(): lax.ppermute(cells, axis, [(i, (i + by) % count) for i in range(count)])  8.63 us
    pallas_call x1, Pallas kernels, pack(): pl.pallas_call(pack_kernel, out_shape=jax.ShapeDtypeStruct((rows, CH * 12...  5.32 us
    pallas_call x1, Pallas kernels, merge(): pl.pallas_call(merge_kernel, out_shape=[jax.ShapeDtypeStruct((4 * GRP, PA...  3.15 us
    ppermute x4, waiting for transfers between devices, shifted(): lax.ppermute(cells, axis, [(i, (i + by) % count) for i in range(count)])  2.68 us
  transfers between devices with their start and end apart: 5, of which 3 were waited for; matrix products, arithmetic and copies ran while one was open for 1% of the time, Pallas kernels for 9%

profile of v3, /device:TPU:0, one launch (start us, length us, event | category | flops | bytes accessed | tf_op | source)
XLA Modules:
  0.0 95.9 jit_solution(1384423288161334660)
XLA Ops:
  0.0 5.3 %pack.1 = bf16[1024,1152]{1,0:T(8,128)(2,1)} custom-call(s32[1,128]{1,0:T(1,128)} %bitcast.17, s32[1,128]{1,0:T(1,128)} %bitcast.18, s32[1,128]{1,0:T(1,128)} %bitcast.19, f32[16,4,128]{2,1,0:T(4,128)} %prof_ref.1, f32[4096,128]{1,0:T(8,128)} %bitcast.15), custom_call_target="tpu_custom_call" | custom-call | tf_op jit(solution)/shard_map/pack/pallas_call | solution.py:115
  5.3 0.0 copy-start.2
  5.3 0.0 copy-start
  5.4 11.1 %all-to-all-start = ((bf16[128,8,1152]{2,1,0:T(8,128)(2,1)}), bf16[128,8,1152]{2,1,0:T(8,128)(2,1)S(1)}, u32[]{:S(2)}, u32[]{:S(2)}) async-start(bf16[128,8,1152]{2,1,0:T(8,128)(2,1)} %bitcast.4), calls=%async_computation | async-start | bytes 4718592 | tf_op jit(solution)/shard_map/all_to_all | solution.py:483
  16.5 0.0 copy-done.2
  16.5 1.1 %copy.10 = bf16[8,8,8,1024]{3,2,0,1:T(8,128)(2,1)} copy(bf16[8,8,8,1024]{3,2,1,0:T(8,128)(2,1)S(1)} %bitcast.16) | data formatting | bytes 2097152 | tf_op jit(solution)/shard_map/reshape | solution.py:481
  17.6 0.1 pad_add_fusion.place_ref
  17.7 31.3 %all-to-all-done = bf16[128,8,1152]{2,1,0:T(8,128)(2,1)S(1)} async-done(((bf16[128,8,1152]{2,1,0:T(8,128)(2,1)}), bf16[128,8,1152]{2,1,0:T(8,128)(2,1)S(1)}, u32[]{:S(2)}, u32[]{:S(2)}) %all-to-all-start) | async-done | bytes 2359328 | tf_op jit(solution)/shard_map/all_to_all | solution.py:483
  49.0 0.0 copy-done
  49.0 3.2 %merge.1 = (bf16[512,512]{1,0:T(8,128)(2,1)S(1)}, bf16[128,512]{1,0:T(8,128)(2,1)S(1)}, bf16[128,512]{1,0:T(8,128)(2,1)S(1)}, bf16[512,1024]{1,0:T(8,128)(2,1)S(1)}, bf16[1024,3072]{1,0:T(8,128)(2,1)S(1)}) custom-call(bf16[1024,1152]{1,0:T(8,128)(2,1)S(1)} %bitcast.13, f32[16,4,128]{2,1,0:T(4,128)S(1)} %copy-done, bf16[512,1024]{1,0:T(8,128)(2,1)} %bitcast.14, ...), custom_call_target="tpu_custom_call" | custom-call | tf_op jit(solution)/shard_map/merge/pallas_call | solution.py:213
  52.2 0.0 copy-start.1
  52.2 0.0 collective-permute-start
  52.2 2.9 %collective-permute-start.1 = (bf16[128,512]{1,0:T(8,128)(2,1)S(1)}, bf16[128,512]{1,0:T(8,128)(2,1)S(1)}, u32[]{:S(2)}, u32[]{:S(2)}) collective-permute-start(bf16[128,512]{1,0:T(8,128)(2,1)S(1)} %get-tuple-element.20), channel_id=1, source_target_pairs={{0,112},{16,0},{32,16},{48,32},{64,48},{80,64},{96,80},{112,96},{1... | collective-permute-start | bytes 393224 | tf_op jit(solution)/shard_map/ppermute | solution.py:456
  55.2 2.6 %collective-permute-done.top_ref = bf16[128,512]{1,0:T(8,128)(2,1)S(1)} collective-permute-done((bf16[128,512]{1,0:T(8,128)(2,1)S(1)}, bf16[128,512]{1,0:T(8,128)(2,1)S(1)}, u32[]{:S(2)}, u32[]{:S(2)}) %collective-permute-start) | collective-permute-done | bytes 131104 | tf_op jit(solution)/shard_map/ppermute | solution.py:456
  57.8 0.0 collective-permute-done.1.bot_ref
  57.9 0.9 collective-permute-start.2
  58.8 4.7 %collective-permute-start.3 = (bf16[384,512]{1,0:T(8,128)(2,1)S(1)}, bf16[384,512]{1,0:T(8,128)(2,1)S(1)}, u32[]{:S(2)}, u32[]{:S(2)}) collective-permute-start(bf16[384,512]{1,0:T(8,128)(2,1)S(1)} %pad_maximum_fusion.1), channel_id=1, source_target_pairs={{0,15},{1,0},{2,1},{3,2},{4,3},{5,4},{6,5},{7,6},{8,7},{9,8},{10,9... | collective-permute-start | bytes 1179656 | tf_op jit(solution)/shard_map/ppermute | solution.py:456
  63.6 0.0 copy-done.1
  63.6 8.6 %own.1 = (f32[768,1024]{1,0:T(8,128)S(1)}, bf16[768,1024]{1,0:T(8,128)(2,1)S(1)}, bf16[768,2048]{1,0:T(8,128)(2,1)S(1)}, bf16[320,1024]{1,0:T(8,128)(2,1)S(1)}) custom-call(s32[4]{0:T(128)S(1)} %pad_add_fusion.place_ref, bf16[512,512]{1,0:T(8,128)(2,1)S(1)} %get-tuple-element.19.x_ref, bf16[128,512]{1,0:T(8,128)(2,1)S(1)} %collective-permute-done.top_ref, ...), custom_call_target="tpu_custom_call" | custom-call | flops 4831838208 | bytes 12582912 | tf_op jit(solution)/shard_map/own/pallas_call | solution.py:280
  72.2 0.1 collective-permute-done.2.left_ref
  72.3 0.0 collective-permute-done.3.right_ref
  72.3 23.4 %rest.1 = bf16[512,1024]{1,0:T(8,128)(2,1)} custom-call(s32[4]{0:T(128)S(1)} %pad_add_fusion.place_ref, bf16[384,512]{1,0:T(8,128)(2,1)S(1)} %collective-permute-done.2.left_ref, bf16[384,512]{1,0:T(8,128)(2,1)S(1)} %collective-permute-done.3.right_ref, f32[768,1024]{1,0:T(8,128)S(1)} %get-tuple-element.23.stream_ref, ...), custom_call_target="tpu_custom_call" | custom-call | tf_op jit(solution)/shard_map/rest/pallas_call | solution.py:429
  (6 shorter events, 0.1 us)
Async XLA Ops:
  5.3 11.2 %copy-start.2 = (bf16[512,1024]{1,0:T(8,128)(2,1)S(1)}, bf16[512,1024]{1,0:T(8,128)(2,1)}, u32[]{:S(2)}) copy-start(bf16[512,1024]{1,0:T(8,128)(2,1)} %param.14) | copy-start | bytes 3145732
  5.3 43.7 %copy-start = (f32[16,4,128]{2,1,0:T(4,128)S(1)}, f32[16,4,128]{2,1,0:T(4,128)}, u32[]{:S(2)}) copy-start(f32[16,4,128]{2,1,0:T(4,128)} %prof_ref.1) | copy-start | bytes 98308
  5.4 43.6 %all-to-all-start = ((bf16[128,8,1152]{2,1,0:T(8,128)(2,1)}), bf16[128,8,1152]{2,1,0:T(8,128)(2,1)S(1)}, u32[]{:S(2)}, u32[]{:S(2)}) async-start(bf16[128,8,1152]{2,1,0:T(8,128)(2,1)} %bitcast.4), calls=%async_computation | async-start | bytes 4718592 | tf_op jit(solution)/shard_map/all_to_all | solution.py:483
  52.2 11.4 %copy-start.1 = (f32[2,1024]{1,0:T(2,128)S(1)}, f32[2,1024]{1,0:T(2,128)}, u32[]{:S(2)}) copy-start(f32[2,1024]{1,0:T(2,128)} %gain_ref.3) | copy-start | bytes 24580
  52.2 5.6 %collective-permute-start = (bf16[128,512]{1,0:T(8,128)(2,1)S(1)}, bf16[128,512]{1,0:T(8,128)(2,1)S(1)}, u32[]{:S(2)}, u32[]{:S(2)}) collective-permute-start(bf16[128,512]{1,0:T(8,128)(2,1)S(1)} %get-tuple-element.18), channel_id=1, source_target_pairs={{0,16},{16,32},{32,48},{48,64},{64,80},{80,96},{96,112},{112,0},{1... | collective-permute-start | bytes 393224 | tf_op jit(solution)/shard_map/ppermute | solution.py:456
  52.2 5.6 %collective-permute-start.1 = (bf16[128,512]{1,0:T(8,128)(2,1)S(1)}, bf16[128,512]{1,0:T(8,128)(2,1)S(1)}, u32[]{:S(2)}, u32[]{:S(2)}) collective-permute-start(bf16[128,512]{1,0:T(8,128)(2,1)S(1)} %get-tuple-element.20), channel_id=1, source_target_pairs={{0,112},{16,0},{32,16},{48,32},{64,48},{80,64},{96,80},{112,96},{1... | collective-permute-start | bytes 393224 | tf_op jit(solution)/shard_map/ppermute | solution.py:456
  57.9 14.4 %collective-permute-start.2 = (bf16[384,512]{1,0:T(8,128)(2,1)S(1)}, bf16[384,512]{1,0:T(8,128)(2,1)S(1)}, u32[]{:S(2)}, u32[]{:S(2)}) collective-permute-start(bf16[384,512]{1,0:T(8,128)(2,1)S(1)} %pad_maximum_fusion), channel_id=1, source_target_pairs={{0,1},{1,2},{2,3},{3,4},{4,5},{5,6},{6,7},{7,8},{8,9},{9,10},{10,1... | collective-permute-start | bytes 1179656 | tf_op jit(solution)/shard_map/ppermute | solution.py:456
  58.8 13.4 %collective-permute-start.3 = (bf16[384,512]{1,0:T(8,128)(2,1)S(1)}, bf16[384,512]{1,0:T(8,128)(2,1)S(1)}, u32[]{:S(2)}, u32[]{:S(2)}) collective-permute-start(bf16[384,512]{1,0:T(8,128)(2,1)S(1)} %pad_maximum_fusion.1), channel_id=1, source_target_pairs={{0,15},{1,0},{2,1},{3,2},{4,3},{5,4},{6,5},{7,6},{8,7},{9,8},{10,9... | collective-permute-start | bytes 1179656 | tf_op jit(solution)/shard_map/ppermute | solution.py:456

commit v4 on v3

--- a/solution.py
+++ b/solution.py
@@ -52,8 +52,8 @@
 
 
 def pack_kernel(
-    dest_hbm, offs_hbm, pidx_hbm, prof_hbm, scans_hbm, out_ref,
-    dest_ref, offs_ref, pidx_ref, prof_ref, scans_ref, w_ref, sem,
+    dest_hbm, offs_hbm, pidx_hbm, prof_hbm, scans_hbm, out_hbm,
+    dest_ref, offs_ref, pidx_ref, prof_ref, scans_ref, w_ref, packed_ref, sem, out_sem,
 ):
     count = dest_ref.shape[1]
     chunk = scans_ref.shape[0] // CHUNKS
@@ -100,13 +100,19 @@
                 w_ref[at : at + some, c * 128 : (c + 1) * 128] = (
                     block * weights[k][n * some : (n + 1) * some, :]
                 ).astype(bf16)
-    rows = out_ref.shape[0]
     slots = jnp.concatenate([slot + float(k) for k in range(BR)], axis=1)
-    step = 256
-    for r in range(0, rows, step):
-        here = (iota((step, BR * count), 0) + r).astype(f32)
-        placing = onehot(here == slots)
-        out_ref[r : r + step, :] = dot(placing, w_ref[...]).astype(bf16)
+    step = packed_ref.shape[0] // CHUNKS
+    outs = []
+    for n in range(CHUNKS):
+        here = (iota((step, BR * count), 0) + n * step).astype(f32)
+        rows = pl.ds(n * step, step)
+        packed_ref[rows, :] = dot(onehot(here == slots), w_ref[...]).astype(bf16)
+        outs.append(
+            pltpu.make_async_copy(packed_ref.at[rows, :], out_hbm.at[rows, :], out_sem.at[n])
+        )
+        outs[-1].start()
+    for copy in outs:
+        copy.wait()
 
 
 def pack(dest, offsets, profile_index, profiles, scans):
@@ -116,6 +122,7 @@
         pack_kernel,
         out_shape=jax.ShapeDtypeStruct((rows, CH * 128 + META), bf16),
         in_specs=[pl.BlockSpec(memory_space=pltpu.HBM)] * 5,
+        out_specs=pl.BlockSpec(memory_space=pltpu.HBM),
         scratch_shapes=[
             pltpu.VMEM((1, count), i32),
             pltpu.VMEM((1, count), i32),
@@ -123,7 +130,9 @@
             pltpu.VMEM(profiles.shape, f32),
             pltpu.VMEM((count * BR * CH, 128), f32),
             pltpu.VMEM((BR * count, CH * 128 + META), bf16),
+            pltpu.VMEM((rows, CH * 128 + META), bf16),
             pltpu.SemaphoreType.DMA((4 + CHUNKS,)),
+            pltpu.SemaphoreType.DMA((CHUNKS,)),
         ],
         compiler_params=pltpu.CompilerParams(vmem_limit_bytes=VMEM_BYTES),
         name="pack",
@@ -342,7 +351,7 @@
 
 
 def rest_kernel(
-    place_ref, left_ref, right_ref, stream_ref, oq_ref, okv_ref, oatt_ref, gain_ref, embed_ref,
+    place_ref, right_ref, left_ref, stream_ref, oq_ref, okv_ref, oatt_ref, gain_ref, embed_ref,
     w_ref, w_hbm, o_hbm, out_ref,
     next_ref, o_ref, side_ref, sq_ref, skv_ref, q_ref, kv_ref, mid_ref, att_ref, inp_ref, sem,
 ):
@@ -446,7 +455,7 @@
         compiler_params=pltpu.CompilerParams(vmem_limit_bytes=LARGE_BYTES),
         name="rest",
     )(
-        place, left, right, *own, gain, in_vmem(embed), in_vmem(w),
+        place, right, left, *own, gain, in_vmem(embed), in_vmem(w),
         in_hbm(qkv_weight), in_hbm(out_weight),
     )
 
@@ -462,8 +471,8 @@
     two = 2 * HALO
     right_edge = jnp.concatenate([top[two:], x[2 * GRP :], bottom[two:]], axis=0)
     left_edge = jnp.concatenate([top[:two], x[: 2 * GRP], bottom[:two]], axis=0)
+    right = shifted(left_edge, "col", -1)
     left = shifted(right_edge, "col", 1)
-    right = shifted(left_edge, "col", -1)
     return top, bottom, left, right
 
 

time: 96.4 us -> 96.2 us (level)
  waiting for transfers between devices: 34 us -> 37.5 us
  starting transfers between devices: 19.8 us -> 17.1 us
    ppermute x4, waiting for transfers between devices: 2.68 us -> 6.13 us  [shifted(): lax.ppermute(cells, axis, [(i, (i + by) % count) for i in range(count)])]
    ppermute x4, starting transfers between devices: 8.63 us -> 5.91 us  [shifted(): lax.ppermute(cells, axis, [(i, (i + by) % count) for i in range(count)])]
where the time goes in v4:
time: 96.2 us; the launch traced here: 96.1 us
  Pallas kernels  40 us (42%)
  waiting for transfers between devices  37.5 us (39%)
  starting transfers between devices  17.1 us (18%)
  local copies, waits for them, and re-layouts  1.14 us (1%)
    all_to_all x1, waiting for transfers between devices, per_device(): lax.all_to_all(payload, ('row', 'col'), split_axis=0, concat_axis=0, tile...  31.3 us
    pallas_call x1, Pallas kernels, rest(): pl.pallas_call(rest_kernel, out_shape=jax.ShapeDtypeStruct((4 * GRP, MODE...  23.4 us
    all_to_all x1, starting transfers between devices, per_device(): lax.all_to_all(payload, ('row', 'col'), split_axis=0, concat_axis=0, tile...  11.1 us
    pallas_call x1, Pallas kernels, own_part(): pl.pallas_call(own_kernel, out_shape=[jax.ShapeDtypeStruct((4 * WIDE, MOD...  8.64 us
    ppermute x4, waiting for transfers between devices, shifted(): lax.ppermute(cells, axis, [(i, (i + by) % count) for i in range(count)])  6.13 us
    ppermute x4, starting transfers between devices, shifted(): lax.ppermute(cells, axis, [(i, (i + by) % count) for i in range(count)])  5.91 us
    pallas_call x1, Pallas kernels, pack(): pl.pallas_call(pack_kernel, out_shape=jax.ShapeDtypeStruct((rows, CH * 12...  4.75 us
    pallas_call x1, Pallas kernels, merge(): pl.pallas_call(merge_kernel, out_shape=[jax.ShapeDtypeStruct((4 * GRP, PA...  3.15 us
  transfers between devices with their start and end apart: 5, of which 3 were waited for; matrix products, arithmetic and copies ran while one was open for 1% of the time, Pallas kernels for 9%

profile of v4, /device:TPU:0, one launch (start us, length us, event | category | flops | bytes accessed | tf_op | source)
XLA Modules:
  0.0 96.1 jit_solution(13588791013215058241)
XLA Ops:
  0.0 4.8 %pack.1 = bf16[1024,1152]{1,0:T(8,128)(2,1)} custom-call(s32[1,128]{1,0:T(1,128)} %bitcast.17, s32[1,128]{1,0:T(1,128)} %bitcast.18, s32[1,128]{1,0:T(1,128)} %bitcast.19, f32[16,4,128]{2,1,0:T(4,128)} %prof_ref.1, f32[4096,128]{1,0:T(8,128)} %bitcast.15), custom_call_target="tpu_custom_call" | custom-call | tf_op jit(solution)/shard_map/pack/pallas_call | solution.py:121
  4.8 0.0 copy-start.2
  4.8 0.0 copy-start
  4.8 11.1 %all-to-all-start = ((bf16[128,8,1152]{2,1,0:T(8,128)(2,1)}), bf16[128,8,1152]{2,1,0:T(8,128)(2,1)S(1)}, u32[]{:S(2)}, u32[]{:S(2)}) async-start(bf16[128,8,1152]{2,1,0:T(8,128)(2,1)} %bitcast.4), calls=%async_computation | async-start | bytes 4718592 | tf_op jit(solution)/shard_map/all_to_all | solution.py:492
  15.9 0.0 copy-done.2
  16.0 1.1 %copy.10 = bf16[8,8,8,1024]{3,2,0,1:T(8,128)(2,1)} copy(bf16[8,8,8,1024]{3,2,1,0:T(8,128)(2,1)S(1)} %bitcast.16) | data formatting | bytes 2097152 | tf_op jit(solution)/shard_map/reshape | solution.py:490
  17.0 0.1 pad_add_fusion.place_ref
  17.1 31.3 %all-to-all-done = bf16[128,8,1152]{2,1,0:T(8,128)(2,1)S(1)} async-done(((bf16[128,8,1152]{2,1,0:T(8,128)(2,1)}), bf16[128,8,1152]{2,1,0:T(8,128)(2,1)S(1)}, u32[]{:S(2)}, u32[]{:S(2)}) %all-to-all-start) | async-done | bytes 2359328 | tf_op jit(solution)/shard_map/all_to_all | solution.py:492
  48.4 0.0 copy-done
  48.4 3.2 %merge.1 = (bf16[512,512]{1,0:T(8,128)(2,1)S(1)}, bf16[128,512]{1,0:T(8,128)(2,1)S(1)}, bf16[128,512]{1,0:T(8,128)(2,1)S(1)}, bf16[512,1024]{1,0:T(8,128)(2,1)S(1)}, bf16[1024,3072]{1,0:T(8,128)(2,1)S(1)}) custom-call(bf16[1024,1152]{1,0:T(8,128)(2,1)S(1)} %bitcast.13, f32[16,4,128]{2,1,0:T(4,128)S(1)} %copy-done, bf16[512,1024]{1,0:T(8,128)(2,1)} %bitcast.14, ...), custom_call_target="tpu_custom_call" | custom-call | tf_op jit(solution)/shard_map/merge/pallas_call | solution.py:222
  51.6 0.0 copy-start.1
  51.6 0.0 collective-permute-start
  51.6 2.9 %collective-permute-start.1 = (bf16[128,512]{1,0:T(8,128)(2,1)S(1)}, bf16[128,512]{1,0:T(8,128)(2,1)S(1)}, u32[]{:S(2)}, u32[]{:S(2)}) collective-permute-start(bf16[128,512]{1,0:T(8,128)(2,1)S(1)} %get-tuple-element.20), channel_id=1, source_target_pairs={{0,112},{16,0},{32,16},{48,32},{64,48},{80,64},{96,80},{112,96},{1... | collective-permute-start | bytes 393224 | tf_op jit(solution)/shard_map/ppermute | solution.py:465
  54.6 2.6 %collective-permute-done.top_ref = bf16[128,512]{1,0:T(8,128)(2,1)S(1)} collective-permute-done((bf16[128,512]{1,0:T(8,128)(2,1)S(1)}, bf16[128,512]{1,0:T(8,128)(2,1)S(1)}, u32[]{:S(2)}, u32[]{:S(2)}) %collective-permute-start) | collective-permute-done | bytes 131104 | tf_op jit(solution)/shard_map/ppermute | solution.py:465
  57.2 0.0 collective-permute-done.1.bot_ref
  57.3 2.7 %collective-permute-start.2 = (bf16[384,512]{1,0:T(8,128)(2,1)S(1)}, bf16[384,512]{1,0:T(8,128)(2,1)S(1)}, u32[]{:S(2)}, u32[]{:S(2)}) collective-permute-start(bf16[384,512]{1,0:T(8,128)(2,1)S(1)} %pad_maximum_fusion), channel_id=1, source_target_pairs={{0,15},{1,0},{2,1},{3,2},{4,3},{5,4},{6,5},{7,6},{8,7},{9,8},{10,9... | collective-permute-start | bytes 1179656 | tf_op jit(solution)/shard_map/ppermute | solution.py:465
  60.0 0.3 collective-permute-start.3
  60.3 0.0 copy-done.1
  60.3 8.6 %own.1 = (f32[768,1024]{1,0:T(8,128)S(1)}, bf16[768,1024]{1,0:T(8,128)(2,1)S(1)}, bf16[768,2048]{1,0:T(8,128)(2,1)S(1)}, bf16[320,1024]{1,0:T(8,128)(2,1)S(1)}) custom-call(s32[4]{0:T(128)S(1)} %pad_add_fusion.place_ref, bf16[512,512]{1,0:T(8,128)(2,1)S(1)} %get-tuple-element.19.x_ref, bf16[128,512]{1,0:T(8,128)(2,1)S(1)} %collective-permute-done.top_ref, ...), custom_call_target="tpu_custom_call" | custom-call | flops 4831838208 | bytes 12582912 | tf_op jit(solution)/shard_map/own/pallas_call | solution.py:289
  68.9 0.0 collective-permute-done.2.right_ref
  68.9 3.5 %collective-permute-done.3.left_ref = bf16[384,512]{1,0:T(8,128)(2,1)S(1)} collective-permute-done((bf16[384,512]{1,0:T(8,128)(2,1)S(1)}, bf16[384,512]{1,0:T(8,128)(2,1)S(1)}, u32[]{:S(2)}, u32[]{:S(2)}) %collective-permute-start.3) | collective-permute-done | bytes 393248 | tf_op jit(solution)/shard_map/ppermute | solution.py:465
  72.5 23.4 %rest.1 = bf16[512,1024]{1,0:T(8,128)(2,1)} custom-call(s32[4]{0:T(128)S(1)} %pad_add_fusion.place_ref, bf16[384,512]{1,0:T(8,128)(2,1)S(1)} %collective-permute-done.2.right_ref, bf16[384,512]{1,0:T(8,128)(2,1)S(1)} %collective-permute-done.3.left_ref, f32[768,1024]{1,0:T(8,128)S(1)} %get-tuple-element.23.stream_ref, ...), custom_call_target="tpu_custom_call" | custom-call | tf_op jit(solution)/shard_map/rest/pallas_call | solution.py:438
  (6 shorter events, 0.1 us)
Async XLA Ops:
  4.8 11.2 %copy-start.2 = (bf16[512,1024]{1,0:T(8,128)(2,1)S(1)}, bf16[512,1024]{1,0:T(8,128)(2,1)}, u32[]{:S(2)}) copy-start(bf16[512,1024]{1,0:T(8,128)(2,1)} %param.14) | copy-start | bytes 3145732
  4.8 43.7 %copy-start = (f32[16,4,128]{2,1,0:T(4,128)S(1)}, f32[16,4,128]{2,1,0:T(4,128)}, u32[]{:S(2)}) copy-start(f32[16,4,128]{2,1,0:T(4,128)} %prof_ref.1) | copy-start | bytes 98308
  4.8 43.6 %all-to-all-start = ((bf16[128,8,1152]{2,1,0:T(8,128)(2,1)}), bf16[128,8,1152]{2,1,0:T(8,128)(2,1)S(1)}, u32[]{:S(2)}, u32[]{:S(2)}) async-start(bf16[128,8,1152]{2,1,0:T(8,128)(2,1)} %bitcast.4), calls=%async_computation | async-start | bytes 4718592 | tf_op jit(solution)/shard_map/all_to_all | solution.py:492
  51.6 8.7 %copy-start.1 = (f32[2,1024]{1,0:T(2,128)S(1)}, f32[2,1024]{1,0:T(2,128)}, u32[]{:S(2)}) copy-start(f32[2,1024]{1,0:T(2,128)} %gain_ref.3) | copy-start | bytes 24580
  51.6 5.6 %collective-permute-start = (bf16[128,512]{1,0:T(8,128)(2,1)S(1)}, bf16[128,512]{1,0:T(8,128)(2,1)S(1)}, u32[]{:S(2)}, u32[]{:S(2)}) collective-permute-start(bf16[128,512]{1,0:T(8,128)(2,1)S(1)} %get-tuple-element.18), channel_id=1, source_target_pairs={{0,16},{16,32},{32,48},{48,64},{64,80},{80,96},{96,112},{112,0},{1... | collective-permute-start | bytes 393224 | tf_op jit(solution)/shard_map/ppermute | solution.py:465
  51.6 5.6 %collective-permute-start.1 = (bf16[128,512]{1,0:T(8,128)(2,1)S(1)}, bf16[128,512]{1,0:T(8,128)(2,1)S(1)}, u32[]{:S(2)}, u32[]{:S(2)}) collective-permute-start(bf16[128,512]{1,0:T(8,128)(2,1)S(1)} %get-tuple-element.20), channel_id=1, source_target_pairs={{0,112},{16,0},{32,16},{48,32},{64,48},{80,64},{96,80},{112,96},{1... | collective-permute-start | bytes 393224 | tf_op jit(solution)/shard_map/ppermute | solution.py:465
  57.3 11.6 %collective-permute-start.2 = (bf16[384,512]{1,0:T(8,128)(2,1)S(1)}, bf16[384,512]{1,0:T(8,128)(2,1)S(1)}, u32[]{:S(2)}, u32[]{:S(2)}) collective-permute-start(bf16[384,512]{1,0:T(8,128)(2,1)S(1)} %pad_maximum_fusion), channel_id=1, source_target_pairs={{0,15},{1,0},{2,1},{3,2},{4,3},{5,4},{6,5},{7,6},{8,7},{9,8},{10,9... | collective-permute-start | bytes 1179656 | tf_op jit(solution)/shard_map/ppermute | solution.py:465
  60.0 12.4 %collective-permute-start.3 = (bf16[384,512]{1,0:T(8,128)(2,1)S(1)}, bf16[384,512]{1,0:T(8,128)(2,1)S(1)}, u32[]{:S(2)}, u32[]{:S(2)}) collective-permute-start(bf16[384,512]{1,0:T(8,128)(2,1)S(1)} %pad_maximum_fusion.1), channel_id=1, source_target_pairs={{0,1},{1,2},{2,3},{3,4},{4,5},{5,6},{6,7},{7,8},{8,9},{9,10},{10,1... | collective-permute-start | bytes 1179656 | tf_op jit(solution)/shard_map/ppermute | solution.py:465

commit v5 on v4

--- a/solution.py
+++ b/solution.py
@@ -22,8 +22,8 @@
 EDGE = 4 * HALO
 META = 128
 CHUNKS = 4
-VMEM_BYTES = 20 * 1024 * 1024
-LARGE_BYTES = 30 * 1024 * 1024
+VMEM_BYTES = 16 * 1024 * 1024
+LARGE_BYTES = 22 * 1024 * 1024
 
 f32 = jnp.float32
 bf16 = jnp.bfloat16
@@ -248,9 +248,16 @@
 
 
 def own_kernel(
-    place_ref, x_ref, top_ref, bot_ref, embed_ref, gain_ref, w_ref,
-    stream_ref, q_ref, kv_ref, att_ref, inp_ref,
+    place_ref, x_ref, top_ref, bot_ref, embed_ref, gain_ref, w_ref, w_hbm, o_hbm,
+    stream_ref, q_ref, kv_ref, mid_ref, later_q_ref, later_kv_ref, o_ref, next_ref,
+    inp_ref, att_ref, sem,
 ):
+    copies = [
+        pltpu.make_async_copy(o_hbm.at[0], o_ref, sem.at[0]),
+        pltpu.make_async_copy(w_hbm.at[1], next_ref, sem.at[1]),
+    ]
+    for copy in copies:
+        copy.start()
     for g in range(4):
         edge = slice(g * HALO, (g + 1) * HALO)
         tokens = jnp.concatenate(
@@ -271,6 +278,16 @@
         place_ref[1] - 8,
         (place_ref[2], place_ref[3]),
     )
+    for copy in copies:
+        copy.wait()
+    for n in range(2):
+        rows = slice(n * MID, (n + 1) * MID)
+        before = stream_ref[(n + 1) * WIDE + 16 : (n + 1) * WIDE + 16 + MID, :]
+        stream = before + dot(att_ref[rows, :], o_ref[...])
+        mid_ref[n * GRP : (n + 1) * GRP, :] = stream[16 : 16 + GRP, :]
+        inp_ref[rows, :] = normed(stream, gain_ref[1:2, :])
+    inputs = inp_ref[: 2 * MID, :]
+    project(inputs, inputs, next_ref, later_q_ref, later_kv_ref)
 
 
 def project(query_inputs, inputs, w_ref, q_ref, kv_ref):
@@ -283,7 +300,8 @@
         kv_ref[: part.shape[0], m : m + step] = part
 
 
-def own_part(place, x, top, bottom, embed, gain, w):
+def own_part(place, x, top, bottom, embed, gain, w, qkv_weight, out_weight):
+    hbm = pl.BlockSpec(memory_space=pltpu.HBM)
     vmem = pl.BlockSpec(memory_space=pltpu.VMEM)
     smem = pl.BlockSpec(memory_space=pltpu.SMEM)
     return pl.pallas_call(
@@ -292,16 +310,27 @@
             jax.ShapeDtypeStruct((4 * WIDE, MODEL), f32),
             jax.ShapeDtypeStruct((4 * WIDE, MODEL), bf16),
             jax.ShapeDtypeStruct((4 * WIDE, 2 * MODEL), bf16),
+            jax.ShapeDtypeStruct((2 * GRP, MODEL), f32),
             jax.ShapeDtypeStruct((2 * MID, MODEL), bf16),
+            jax.ShapeDtypeStruct((2 * MID, 2 * MODEL), bf16),
+            pltpu.VMEM((MODEL, MODEL), bf16),
+            pltpu.VMEM((MODEL, 3 * MODEL), bf16),
         ],
-        in_specs=[smem] + [vmem] * 6,
-        scratch_shapes=[pltpu.VMEM((4 * WIDE, MODEL), bf16)],
+        in_specs=[smem] + [vmem] * 6 + [hbm] * 2,
+        scratch_shapes=[
+            pltpu.VMEM((4 * WIDE, MODEL), bf16),
+            pltpu.VMEM((2 * MID, MODEL), bf16),
+            pltpu.SemaphoreType.DMA((2,)),
+        ],
         compiler_params=pltpu.CompilerParams(vmem_limit_bytes=VMEM_BYTES),
         cost_estimate=pl.CostEstimate(
             flops=2 * 4 * WIDE * MODEL * 3 * MODEL, bytes_accessed=12 << 20, transcendentals=0
         ),
         name="own",
-    )(place, x, top, bottom, in_vmem(embed), gain, in_vmem(w))
+    )(
+        place, x, top, bottom, in_vmem(embed), gain, in_vmem(w),
+        in_hbm(qkv_weight), in_hbm(out_weight),
+    )
 
 
 def attention(broad, tall, q_of, kv_of, a_of, row, col, ends):
@@ -351,17 +380,12 @@
 
 
 def rest_kernel(
-    place_ref, right_ref, left_ref, stream_ref, oq_ref, okv_ref, oatt_ref, gain_ref, embed_ref,
-    w_ref, w_hbm, o_hbm, out_ref,
-    next_ref, o_ref, side_ref, sq_ref, skv_ref, q_ref, kv_ref, mid_ref, att_ref, inp_ref, sem,
+    place_ref, right_ref, left_ref, stream_ref, oq_ref, okv_ref, omid_ref, mq_ref, mkv_ref, o_ref,
+    next_ref, gain_ref, embed_ref, w_ref, o_hbm, out_ref,
+    last_ref, side_ref, sq_ref, skv_ref, q_ref, kv_ref, mid_ref, att_ref, inp_ref, sem,
 ):
-    copies = [
-        pltpu.make_async_copy(o_hbm.at[0], o_ref.at[0], sem.at[0]),
-        pltpu.make_async_copy(w_hbm.at[1], next_ref, sem.at[1]),
-        pltpu.make_async_copy(o_hbm.at[1], o_ref.at[1], sem.at[2]),
-    ]
-    for copy in copies:
-        copy.start()
+    copy = pltpu.make_async_copy(o_hbm.at[1], last_ref, sem)
+    copy.start()
 
     for n in range(4):
         ref, g = (left_ref, right_ref)[n // 2], n % 2
@@ -394,36 +418,46 @@
     attention(
         [0, 2], 5, q_of, kv_of, lambda g: (att_ref, g * MID), place_ref[0] - 8, place_ref[1] - 8, ends
     )
-    copies[0].wait()
-    for g in range(6):
-        rows = slice(g * MID, (g + 1) * MID)
+    for n, g in enumerate((0, 1, 4, 5)):
+        rows = slice(n * MID, (n + 1) * MID)
         if g in (0, 5):
             before = side_ref[(g // 5) * WIDE + 16 : (g // 5) * WIDE + 16 + MID, :]
         else:
             before = stream_ref[(g - 1) * WIDE + 16 : (g - 1) * WIDE + 16 + MID, :]
-        mixed = oatt_ref[(g - 2) * MID : (g - 1) * MID, :] if g in (2, 3) else att_ref[rows, :]
-        stream = before + dot(mixed, o_ref[0])
-        if g not in (0, 5):
-            mid_ref[(g - 1) * GRP : g * GRP, :] = stream[16 : 16 + GRP, :]
+        stream = before + dot(att_ref[g * MID : (g + 1) * MID, :], o_ref[...])
+        if n in (1, 2):
+            mid_ref[(n - 1) * GRP : n * GRP, :] = stream[16 : 16 + GRP, :]
         inp_ref[rows, :] = normed(stream, gain_ref[1:2, :])
 
-    copies[1].wait()
-    project(inp_ref[MID : 5 * MID, :], inp_ref[...], next_ref, q_ref, kv_ref)
+    project(inp_ref[MID : 3 * MID, :], inp_ref[: 4 * MID, :], next_ref, q_ref, kv_ref)
+
+    def later_q_of(g):
+        if g in (0, 3):
+            return q_ref, (g // 3) * MID + 16
+        return mq_ref, (g - 1) * MID + 16
+
+    def later_kv_of(g):
+        if g in (2, 3):
+            return mkv_ref, (g - 2) * MID
+        return kv_ref, (g if g < 2 else g - 2) * MID
+
     attention(
         [0, 1],
         4,
-        lambda g: (q_ref, g * MID + 16),
-        lambda g: (kv_ref, g * MID),
+        later_q_of,
+        later_kv_of,
         lambda g: (att_ref, g * GRP),
         place_ref[0] - 4,
         place_ref[1] - 4,
         ends,
     )
-    copies[2].wait()
+    copy.wait()
     for g in range(4):
         rows = slice(g * GRP, (g + 1) * GRP)
-        stream = mid_ref[rows, :] + dot(att_ref[rows, :], o_ref[1])
-        inp_ref[rows, :] = stream.astype(bf16)
+        before = omid_ref[(g - 1) * GRP : g * GRP, :] if g in (1, 2) else mid_ref[
+            (g // 3) * GRP : (g // 3 + 1) * GRP, :
+        ]
+        inp_ref[rows, :] = (before + dot(att_ref[rows, :], last_ref[...])).astype(bf16)
     for r in range(0, 4 * GRP, GRP):
         to = iota((GRP, 4 * GRP), 0) + r
         source = iota((GRP, 4 * GRP), 1)
@@ -431,32 +465,32 @@
         out_ref[r : r + GRP, :] = dot(onehot(source == wanted), inp_ref[: 4 * GRP, :]).astype(bf16)
 
 
-def rest(place, left, right, own, gain, embed, w, qkv_weight, out_weight):
+def rest(place, left, right, own, gain, embed, w, out_weight):
     hbm = pl.BlockSpec(memory_space=pltpu.HBM)
     vmem = pl.BlockSpec(memory_space=pltpu.VMEM)
     smem = pl.BlockSpec(memory_space=pltpu.SMEM)
+    *own, o, later = own
     return pl.pallas_call(
         rest_kernel,
         out_shape=jax.ShapeDtypeStruct((4 * GRP, MODEL), bf16),
-        in_specs=[smem] + [vmem] * 9 + [hbm] * 2,
+        in_specs=[smem] + [vmem] * 13 + [hbm],
         scratch_shapes=[
-            pltpu.VMEM((MODEL, 3 * MODEL), bf16),
-            pltpu.VMEM((2, MODEL, MODEL), bf16),
+            pltpu.VMEM((MODEL, MODEL), bf16),
             pltpu.VMEM((2 * WIDE, MODEL), f32),
             pltpu.VMEM((2 * WIDE, MODEL), bf16),
             pltpu.VMEM((4 * WIDE, 2 * MODEL), bf16),
-            pltpu.VMEM((4 * MID, MODEL), bf16),
-            pltpu.VMEM((6 * MID, 2 * MODEL), bf16),
-            pltpu.VMEM((4 * GRP, MODEL), f32),
+            pltpu.VMEM((2 * MID, MODEL), bf16),
+            pltpu.VMEM((4 * MID, 2 * MODEL), bf16),
+            pltpu.VMEM((2 * GRP, MODEL), f32),
             pltpu.VMEM((6 * MID, MODEL), bf16),
-            pltpu.VMEM((6 * MID, MODEL), bf16),
-            pltpu.SemaphoreType.DMA((3,)),
+            pltpu.VMEM((4 * WIDE, MODEL), bf16),
+            pltpu.SemaphoreType.DMA,
         ],
         compiler_params=pltpu.CompilerParams(vmem_limit_bytes=LARGE_BYTES),
         name="rest",
     )(
-        place, right, left, *own, gain, in_vmem(embed), in_vmem(w),
-        in_hbm(qkv_weight), in_hbm(out_weight),
+        place, right, left, *own, in_vmem(o), in_vmem(later), gain, in_vmem(embed), in_vmem(w),
+        in_hbm(out_weight),
     )
 
 
@@ -493,8 +527,8 @@
     payload, place = lax.optimization_barrier((payload, place))
     x, first, last, embed, w = merge(payload, profiles, embed, qkv_weight)
     top, bottom, left, right = around(x, first, last)
-    own = own_part(place, x, top, bottom, embed, attn_gain, w)
-    tokens = rest(place, left, right, own, attn_gain, embed, w, qkv_weight, out_weight)
+    own = own_part(place, x, top, bottom, embed, attn_gain, w, qkv_weight, out_weight)
+    tokens = rest(place, left, right, own, attn_gain, embed, w, out_weight)
     return tokens.reshape(TOK_H, TOK_W, MODEL)
 
 

time: 96.2 us -> 94.8 us (0.985)
  waiting for transfers between devices: 37.5 us -> 33.9 us
  Pallas kernels: 40 us -> 41.9 us
    pallas_call x1, Pallas kernels: 8.64 us -> 12.4 us  [own_part(): pl.pallas_call(own_kernel, out_shape=[jax.ShapeDtypeStruct((4 * WIDE, MOD...]
    ppermute x4, waiting for transfers between devices: 6.13 us -> 2.62 us  [shifted(): lax.ppermute(cells, axis, [(i, (i + by) % count) for i in range(count)])]
    pallas_call x1, Pallas kernels: 23.4 us -> 21.6 us  [rest(): pl.pallas_call(rest_kernel, out_shape=jax.ShapeDtypeStruct((4 * GRP, MODE...]
  transfers between devices with their start and end apart: 5 -> 5, of which waited for: 3 -> 2; matrix products, arithmetic and copies ran while one was open for 1% -> 1% of each run, Pallas kernels for 9% -> 13%
where the time goes in v5:
time: 94.8 us; the launch traced here: 94.5 us
  Pallas kernels  41.9 us (44%)
  waiting for transfers between devices  33.9 us (36%)
  starting transfers between devices  17.1 us (18%)
  local copies, waits for them, and re-layouts  1.14 us (1%)
    all_to_all x1, waiting for transfers between devices, per_device(): lax.all_to_all(payload, ('row', 'col'), split_axis=0, concat_axis=0, tile...  31.3 us
    pallas_call x1, Pallas kernels, rest(): pl.pallas_call(rest_kernel, out_shape=jax.ShapeDtypeStruct((4 * GRP, MODE...  21.6 us
    pallas_call x1, Pallas kernels, own_part(): pl.pallas_call(own_kernel, out_shape=[jax.ShapeDtypeStruct((4 * WIDE, MOD...  12.4 us
    all_to_all x1, starting transfers between devices, per_device(): lax.all_to_all(payload, ('row', 'col'), split_axis=0, concat_axis=0, tile...  11.1 us
    ppermute x4, starting transfers between devices, shifted(): lax.ppermute(cells, axis, [(i, (i + by) % count) for i in range(count)])  5.91 us
    pallas_call x1, Pallas kernels, pack(): pl.pallas_call(pack_kernel, out_shape=jax.ShapeDtypeStruct((rows, CH * 12...  4.75 us
    pallas_call x1, Pallas kernels, merge(): pl.pallas_call(merge_kernel, out_shape=[jax.ShapeDtypeStruct((4 * GRP, PA...  3.15 us
    ppermute x4, waiting for transfers between devices, shifted(): lax.ppermute(cells, axis, [(i, (i + by) % count) for i in range(count)])  2.62 us
  transfers between devices with their start and end apart: 5, of which 2 were waited for; matrix products, arithmetic and copies ran while one was open for 1% of the time, Pallas kernels for 13%

profile of v5, /device:TPU:0, one launch (start us, length us, event | category | flops | bytes accessed | tf_op | source)
XLA Modules:
  0.0 94.5 jit_solution(11643358018525739507)
XLA Ops:
  0.0 4.8 %pack.1 = bf16[1024,1152]{1,0:T(8,128)(2,1)} custom-call(s32[1,128]{1,0:T(1,128)} %bitcast.17, s32[1,128]{1,0:T(1,128)} %bitcast.18, s32[1,128]{1,0:T(1,128)} %bitcast.19, f32[16,4,128]{2,1,0:T(4,128)} %prof_ref.1, f32[4096,128]{1,0:T(8,128)} %bitcast.15), custom_call_target="tpu_custom_call" | custom-call | tf_op jit(solution)/shard_map/pack/pallas_call | solution.py:121
  4.8 0.0 copy-start.2
  4.8 0.0 copy-start
  4.8 11.1 %all-to-all-start = ((bf16[128,8,1152]{2,1,0:T(8,128)(2,1)}), bf16[128,8,1152]{2,1,0:T(8,128)(2,1)S(1)}, u32[]{:S(2)}, u32[]{:S(2)}) async-start(bf16[128,8,1152]{2,1,0:T(8,128)(2,1)} %bitcast.4), calls=%async_computation | async-start | bytes 4718592 | tf_op jit(solution)/shard_map/all_to_all | solution.py:526
  15.9 0.0 copy-done.2
  16.0 1.1 %copy.10 = bf16[8,8,8,1024]{3,2,0,1:T(8,128)(2,1)} copy(bf16[8,8,8,1024]{3,2,1,0:T(8,128)(2,1)S(1)} %bitcast.16) | data formatting | bytes 2097152 | tf_op jit(solution)/shard_map/reshape | solution.py:524
  17.0 0.1 pad_add_fusion.place_ref
  17.1 31.3 %all-to-all-done = bf16[128,8,1152]{2,1,0:T(8,128)(2,1)S(1)} async-done(((bf16[128,8,1152]{2,1,0:T(8,128)(2,1)}), bf16[128,8,1152]{2,1,0:T(8,128)(2,1)S(1)}, u32[]{:S(2)}, u32[]{:S(2)}) %all-to-all-start) | async-done | bytes 2359328 | tf_op jit(solution)/shard_map/all_to_all | solution.py:526
  48.4 0.0 copy-done
  48.4 3.2 %merge.1 = (bf16[512,512]{1,0:T(8,128)(2,1)S(1)}, bf16[128,512]{1,0:T(8,128)(2,1)S(1)}, bf16[128,512]{1,0:T(8,128)(2,1)S(1)}, bf16[512,1024]{1,0:T(8,128)(2,1)S(1)}, bf16[1024,3072]{1,0:T(8,128)(2,1)S(1)}) custom-call(bf16[1024,1152]{1,0:T(8,128)(2,1)S(1)} %bitcast.13, f32[16,4,128]{2,1,0:T(4,128)S(1)} %copy-done, bf16[512,1024]{1,0:T(8,128)(2,1)} %bitcast.14, ...), custom_call_target="tpu_custom_call" | custom-call | tf_op jit(solution)/shard_map/merge/pallas_call | solution.py:222
  51.6 0.0 copy-start.1
  51.6 0.0 collective-permute-start
  51.6 2.9 %collective-permute-start.1 = (bf16[128,512]{1,0:T(8,128)(2,1)S(1)}, bf16[128,512]{1,0:T(8,128)(2,1)S(1)}, u32[]{:S(2)}, u32[]{:S(2)}) collective-permute-start(bf16[128,512]{1,0:T(8,128)(2,1)S(1)} %get-tuple-element.24), channel_id=1, source_target_pairs={{0,112},{16,0},{32,16},{48,32},{64,48},{80,64},{96,80},{112,96},{1... | collective-permute-start | bytes 393224 | tf_op jit(solution)/shard_map/ppermute | solution.py:499
  54.6 2.6 %collective-permute-done.top_ref = bf16[128,512]{1,0:T(8,128)(2,1)S(1)} collective-permute-done((bf16[128,512]{1,0:T(8,128)(2,1)S(1)}, bf16[128,512]{1,0:T(8,128)(2,1)S(1)}, u32[]{:S(2)}, u32[]{:S(2)}) %collective-permute-start) | collective-permute-done | bytes 131104 | tf_op jit(solution)/shard_map/ppermute | solution.py:499
  57.2 0.0 collective-permute-done.1.bot_ref
  57.3 2.7 %collective-permute-start.2 = (bf16[384,512]{1,0:T(8,128)(2,1)S(1)}, bf16[384,512]{1,0:T(8,128)(2,1)S(1)}, u32[]{:S(2)}, u32[]{:S(2)}) collective-permute-start(bf16[384,512]{1,0:T(8,128)(2,1)S(1)} %pad_maximum_fusion), channel_id=1, source_target_pairs={{0,15},{1,0},{2,1},{3,2},{4,3},{5,4},{6,5},{7,6},{8,7},{9,8},{10,9... | collective-permute-start | bytes 1179656 | tf_op jit(solution)/shard_map/ppermute | solution.py:499
  60.0 0.3 collective-permute-start.3
  60.3 0.0 copy-done.1
  60.3 12.4 %own.1 = (f32[768,1024]{1,0:T(8,128)S(1)}, bf16[768,1024]{1,0:T(8,128)(2,1)S(1)}, bf16[768,2048]{1,0:T(8,128)(2,1)S(1)}, f32[256,1024]{1,0:T(8,128)S(1)}, bf16[3...) custom-call(s32[4]{0:T(128)S(1)} %pad_add_fusion.place_ref, ...), custom_call_target="tpu_custom_call" | custom-call | flops 4831838208 | bytes 12582912 | tf_op jit(solution)/shard_map/own/pallas_call | solution.py:307
  72.7 0.0 collective-permute-done.2.right_ref
  72.7 0.0 collective-permute-done.3.left_ref
  72.7 21.6 %rest.1 = bf16[512,1024]{1,0:T(8,128)(2,1)} custom-call(s32[4]{0:T(128)S(1)} %pad_add_fusion.place_ref, bf16[384,512]{1,0:T(8,128)(2,1)S(1)} %collective-permute-done.2.right_ref, bf16[384,512]{1,0:T(8,128)(2,1)S(1)} %collective-permute-done.3.left_ref, f32[768,1024]{1,0:T(8,128)S(1)} %get-tuple-element.27.stream_ref, ...), custom_call_target="tpu_custom_call" | custom-call | tf_op jit(solution)/shard_map/rest/pallas_call | solution.py:473
  (6 shorter events, 0.1 us)
Async XLA Ops:
  4.8 11.2 %copy-start.2 = (bf16[512,1024]{1,0:T(8,128)(2,1)S(1)}, bf16[512,1024]{1,0:T(8,128)(2,1)}, u32[]{:S(2)}) copy-start(bf16[512,1024]{1,0:T(8,128)(2,1)} %param.14) | copy-start | bytes 3145732
  4.8 43.7 %copy-start = (f32[16,4,128]{2,1,0:T(4,128)S(1)}, f32[16,4,128]{2,1,0:T(4,128)}, u32[]{:S(2)}) copy-start(f32[16,4,128]{2,1,0:T(4,128)} %prof_ref.1) | copy-start | bytes 98308
  4.8 43.6 %all-to-all-start = ((bf16[128,8,1152]{2,1,0:T(8,128)(2,1)}), bf16[128,8,1152]{2,1,0:T(8,128)(2,1)S(1)}, u32[]{:S(2)}, u32[]{:S(2)}) async-start(bf16[128,8,1152]{2,1,0:T(8,128)(2,1)} %bitcast.4), calls=%async_computation | async-start | bytes 4718592 | tf_op jit(solution)/shard_map/all_to_all | solution.py:526
  51.6 8.7 %copy-start.1 = (f32[2,1024]{1,0:T(2,128)S(1)}, f32[2,1024]{1,0:T(2,128)}, u32[]{:S(2)}) copy-start(f32[2,1024]{1,0:T(2,128)} %gain_ref.3) | copy-start | bytes 24580
  51.6 5.6 %collective-permute-start = (bf16[128,512]{1,0:T(8,128)(2,1)S(1)}, bf16[128,512]{1,0:T(8,128)(2,1)S(1)}, u32[]{:S(2)}, u32[]{:S(2)}) collective-permute-start(bf16[128,512]{1,0:T(8,128)(2,1)S(1)} %get-tuple-element.22), channel_id=1, source_target_pairs={{0,16},{16,32},{32,48},{48,64},{64,80},{80,96},{96,112},{112,0},{1... | collective-permute-start | bytes 393224 | tf_op jit(solution)/shard_map/ppermute | solution.py:499
  51.6 5.6 %collective-permute-start.1 = (bf16[128,512]{1,0:T(8,128)(2,1)S(1)}, bf16[128,512]{1,0:T(8,128)(2,1)S(1)}, u32[]{:S(2)}, u32[]{:S(2)}) collective-permute-start(bf16[128,512]{1,0:T(8,128)(2,1)S(1)} %get-tuple-element.24), channel_id=1, source_target_pairs={{0,112},{16,0},{32,16},{48,32},{64,48},{80,64},{96,80},{112,96},{1... | collective-permute-start | bytes 393224 | tf_op jit(solution)/shard_map/ppermute | solution.py:499
  57.3 15.4 %collective-permute-start.2 = (bf16[384,512]{1,0:T(8,128)(2,1)S(1)}, bf16[384,512]{1,0:T(8,128)(2,1)S(1)}, u32[]{:S(2)}, u32[]{:S(2)}) collective-permute-start(bf16[384,512]{1,0:T(8,128)(2,1)S(1)} %pad_maximum_fusion), channel_id=1, source_target_pairs={{0,15},{1,0},{2,1},{3,2},{4,3},{5,4},{6,5},{7,6},{8,7},{9,8},{10,9... | collective-permute-start | bytes 1179656 | tf_op jit(solution)/shard_map/ppermute | solution.py:499
  60.0 12.7 %collective-permute-start.3 = (bf16[384,512]{1,0:T(8,128)(2,1)S(1)}, bf16[384,512]{1,0:T(8,128)(2,1)S(1)}, u32[]{:S(2)}, u32[]{:S(2)}) collective-permute-start(bf16[384,512]{1,0:T(8,128)(2,1)S(1)} %pad_maximum_fusion.1), channel_id=1, source_target_pairs={{0,1},{1,2},{2,3},{3,4},{4,5},{5,6},{6,7},{7,8},{8,9},{9,10},{10,1... | collective-permute-start | bytes 1179656 | tf_op jit(solution)/shard_map/ppermute | solution.py:499

commit v6 on v5

--- a/solution.py
+++ b/solution.py
@@ -5,12 +5,14 @@
 from jax import lax
 from jax.experimental import pallas as pl
 from jax.experimental.pallas import tpu as pltpu
+from jax.sharding import Mesh
 from jax.sharding import PartitionSpec as P
 
 HEADS = 16
 RADIUS = 4
 TOK_H = 32
 TOK_W = 16
+N_COL = 16
 BR = 4
 CH = 8
 MODEL = 1024
@@ -24,6 +26,8 @@
 CHUNKS = 4
 VMEM_BYTES = 16 * 1024 * 1024
 LARGE_BYTES = 22 * 1024 * 1024
+
+ROW = ("z", "core")
 
 f32 = jnp.float32
 bf16 = jnp.bfloat16
@@ -74,7 +78,10 @@
     for copy in small:
         copy.wait()
     eye = iota((count, count), 0) == iota((count, count), 1)
-    dest_row = dest_ref[...].astype(f32)
+    tile = dest_ref[...]
+    depth = count // (2 * N_COL)
+    place = (tile // N_COL % 2 * depth + tile // (2 * N_COL)) * N_COL + tile % N_COL
+    dest_row = place.astype(f32)
     dest_col = jnp.sum(jnp.where(eye, dest_row, 0.0), axis=1, keepdims=True)
     before = iota((count, count), 0) < iota((count, count), 1)
     same = (dest_col == dest_row) & before
@@ -154,13 +161,13 @@
 
 
 def merge_kernel(
-    pay_ref, prof_ref, embed_hbm, w_hbm, x_ref, top_ref, bot_ref, embed_ref, w_ref,
+    pay_ref, prof_ref, embed_hbm, w_hbm, x_ref, top_ref, bot_ref, embed_ref, wq_ref,
     mg_ref, y_ref, xg_ref, sem,
 ):
     rows = pay_ref.shape[0]
     copies = [
         pltpu.make_async_copy(embed_hbm, embed_ref, sem.at[0]),
-        pltpu.make_async_copy(w_hbm.at[0], w_ref, sem.at[1]),
+        pltpu.make_async_copy(w_hbm.at[0, :, pl.ds(0, MODEL)], wq_ref, sem.at[1]),
     ]
     for copy in copies:
         copy.start()
@@ -226,7 +233,7 @@
             jax.ShapeDtypeStruct((EDGE, PATCH), bf16),
             jax.ShapeDtypeStruct((EDGE, PATCH), bf16),
             pltpu.VMEM((PATCH, MODEL), bf16),
-            pltpu.VMEM((MODEL, 3 * MODEL), bf16),
+            pltpu.VMEM((MODEL, MODEL), bf16),
         ],
         in_specs=[vmem, vmem, hbm, hbm],
         scratch_shapes=[
@@ -248,13 +255,14 @@
 
 
 def own_kernel(
-    place_ref, x_ref, top_ref, bot_ref, embed_ref, gain_ref, w_ref, w_hbm, o_hbm,
-    stream_ref, q_ref, kv_ref, mid_ref, later_q_ref, later_kv_ref, o_ref, next_ref,
+    place_ref, x_ref, top_ref, bot_ref, embed_ref, gain_ref, wq_ref, w_hbm, o_hbm,
+    stream_ref, q_ref, kv_ref, mid_ref, later_q_ref, later_kv_ref, wkv_ref, o_ref, next_ref,
     inp_ref, att_ref, sem,
 ):
     copies = [
-        pltpu.make_async_copy(o_hbm.at[0], o_ref, sem.at[0]),
-        pltpu.make_async_copy(w_hbm.at[1], next_ref, sem.at[1]),
+        pltpu.make_async_copy(w_hbm.at[0, :, pl.ds(MODEL, 2 * MODEL)], wkv_ref, sem.at[0]),
+        pltpu.make_async_copy(o_hbm.at[0], o_ref, sem.at[1]),
+        pltpu.make_async_copy(w_hbm.at[1], next_ref, sem.at[2]),
     ]
     for copy in copies:
         copy.start()
@@ -267,7 +275,9 @@
         rows = slice(g * WIDE, (g + 1) * WIDE)
         stream_ref[rows, :] = stream
         inp_ref[rows, :] = normed(stream, gain_ref[0:1, :])
-    project(inp_ref[...], inp_ref[...], w_ref, q_ref, kv_ref)
+    project_queries(inp_ref[...], wq_ref, q_ref)
+    copies[0].wait()
+    project_keys(inp_ref[...], wkv_ref, 0, kv_ref)
     attention(
         [1],
         5,
@@ -278,7 +288,7 @@
         place_ref[1] - 8,
         (place_ref[2], place_ref[3]),
     )
-    for copy in copies:
+    for copy in copies[1:]:
         copy.wait()
     for n in range(2):
         rows = slice(n * MID, (n + 1) * MID)
@@ -290,14 +300,23 @@
     project(inputs, inputs, next_ref, later_q_ref, later_kv_ref)
 
 
-def project(query_inputs, inputs, w_ref, q_ref, kv_ref):
+def project_queries(inputs, w_ref, q_ref):
     step = 256
     for m in range(0, MODEL, step):
-        part = dot(query_inputs, w_ref[:, m : m + step]).astype(bf16)
+        part = dot(inputs, w_ref[:, m : m + step]).astype(bf16)
         q_ref[: part.shape[0], m : m + step] = part * jnp.asarray(0.125, bf16)
+
+
+def project_keys(inputs, w_ref, start, kv_ref):
+    step = 256
     for m in range(0, 2 * MODEL, step):
-        part = dot(inputs, w_ref[:, MODEL + m : MODEL + m + step]).astype(bf16)
+        part = dot(inputs, w_ref[:, start + m : start + m + step]).astype(bf16)
         kv_ref[: part.shape[0], m : m + step] = part
+
+
+def project(query_inputs, inputs, w_ref, q_ref, kv_ref):
+    project_queries(query_inputs, w_ref, q_ref)
+    project_keys(inputs, w_ref, MODEL, kv_ref)
 
 
 def own_part(place, x, top, bottom, embed, gain, w, qkv_weight, out_weight):
@@ -313,6 +332,7 @@
             jax.ShapeDtypeStruct((2 * GRP, MODEL), f32),
             jax.ShapeDtypeStruct((2 * MID, MODEL), bf16),
             jax.ShapeDtypeStruct((2 * MID, 2 * MODEL), bf16),
+            pltpu.VMEM((MODEL, 2 * MODEL), bf16),
             pltpu.VMEM((MODEL, MODEL), bf16),
             pltpu.VMEM((MODEL, 3 * MODEL), bf16),
         ],
@@ -320,7 +340,7 @@
         scratch_shapes=[
             pltpu.VMEM((4 * WIDE, MODEL), bf16),
             pltpu.VMEM((2 * MID, MODEL), bf16),
-            pltpu.SemaphoreType.DMA((2,)),
+            pltpu.SemaphoreType.DMA((3,)),
         ],
         compiler_params=pltpu.CompilerParams(vmem_limit_bytes=VMEM_BYTES),
         cost_estimate=pl.CostEstimate(
@@ -380,8 +400,8 @@
 
 
 def rest_kernel(
-    place_ref, right_ref, left_ref, stream_ref, oq_ref, okv_ref, omid_ref, mq_ref, mkv_ref, o_ref,
-    next_ref, gain_ref, embed_ref, w_ref, o_hbm, out_ref,
+    place_ref, right_ref, left_ref, stream_ref, oq_ref, okv_ref, omid_ref, mq_ref, mkv_ref, wkv_ref,
+    o_ref, next_ref, gain_ref, embed_ref, wq_ref, o_hbm, out_ref,
     last_ref, side_ref, sq_ref, skv_ref, q_ref, kv_ref, mid_ref, att_ref, inp_ref, sem,
 ):
     copy = pltpu.make_async_copy(o_hbm.at[1], last_ref, sem)
@@ -402,7 +422,8 @@
         inp_ref[n * WIDE : (n + 1) * WIDE, :] = normed(stream, gain_ref[0:1, :])
         if n in (1, 2):
             side_ref[(n - 1) * WIDE : n * WIDE, :] = stream
-    project(inp_ref[WIDE : 3 * WIDE, :], inp_ref[: 4 * WIDE, :], w_ref, sq_ref, skv_ref)
+    project_queries(inp_ref[WIDE : 3 * WIDE, :], wq_ref, sq_ref)
+    project_keys(inp_ref[: 4 * WIDE, :], wkv_ref, 0, skv_ref)
 
     def q_of(g):
         if g in (0, 5):
@@ -469,11 +490,11 @@
     hbm = pl.BlockSpec(memory_space=pltpu.HBM)
     vmem = pl.BlockSpec(memory_space=pltpu.VMEM)
     smem = pl.BlockSpec(memory_space=pltpu.SMEM)
-    *own, o, later = own
+    *own, wkv, o, later = own
     return pl.pallas_call(
         rest_kernel,
         out_shape=jax.ShapeDtypeStruct((4 * GRP, MODEL), bf16),
-        in_specs=[smem] + [vmem] * 13 + [hbm],
+        in_specs=[smem] + [vmem] * 14 + [hbm],
         scratch_shapes=[
             pltpu.VMEM((MODEL, MODEL), bf16),
             pltpu.VMEM((2 * WIDE, MODEL), f32),
@@ -489,8 +510,8 @@
         compiler_params=pltpu.CompilerParams(vmem_limit_bytes=LARGE_BYTES),
         name="rest",
     )(
-        place, right, left, *own, in_vmem(o), in_vmem(later), gain, in_vmem(embed), in_vmem(w),
-        in_hbm(out_weight),
+        place, right, left, *own, in_vmem(wkv), in_vmem(o), in_vmem(later), gain, in_vmem(embed),
+        in_vmem(w), in_hbm(out_weight),
     )
 
 
@@ -500,8 +521,8 @@
 
 
 def around(x, first, last):
-    top = shifted(last, "row", 1)
-    bottom = shifted(first, "row", -1)
+    top = shifted(last, ROW, 1)
+    bottom = shifted(first, ROW, -1)
     two = 2 * HALO
     right_edge = jnp.concatenate([top[two:], x[2 * GRP :], bottom[two:]], axis=0)
     left_edge = jnp.concatenate([top[:two], x[: 2 * GRP], bottom[:two]], axis=0)
@@ -515,15 +536,17 @@
 ):
     place = jnp.stack(
         [
-            lax.axis_index("row") * TOK_H,
+            lax.axis_index(ROW) * TOK_H,
             lax.axis_index("col") * TOK_W,
-            jnp.asarray(lax.axis_size("row") * TOK_H, i32),
+            jnp.asarray(lax.axis_size(ROW) * TOK_H, i32),
             jnp.asarray(lax.axis_size("col") * TOK_W, i32),
         ]
     ).astype(i32)
     embed = embed_weight.reshape(CH, 8, 8, MODEL).transpose(1, 0, 2, 3).reshape(PATCH, MODEL)
     payload = pack(dest, offsets, profile_index, profiles, scans)
-    payload = lax.all_to_all(payload, ("row", "col"), split_axis=0, concat_axis=0, tiled=True)
+    payload = lax.all_to_all(
+        payload, ("core", "z", "col"), split_axis=0, concat_axis=0, tiled=True
+    )
     payload, place = lax.optimization_barrier((payload, place))
     x, first, last, embed, w = merge(payload, profiles, embed, qkv_weight)
     top, bottom, left, right = around(x, first, last)
@@ -533,17 +556,10 @@
 
 
 def solution(mesh):
-    placed = (
-        P(("row", "col"), None, None, None),
-        P(("row", "col"), None),
-        P(("row", "col")),
-        P(("row", "col")),
-        P(),
-        P(),
-        P(),
-        P(),
-        P(),
-    )
+    rows, cols = mesh.shape["row"], mesh.shape["col"]
+    chips = Mesh(mesh.devices.reshape(rows // 2, 2, cols), (*ROW, "col"))
+    every = (*ROW, "col")
+    placed = (P(every, None, None, None), P(every, None), P(every), P(every), P(), P(), P(), P(), P())
     return jax.shard_map(
-        per_device, mesh=mesh, in_specs=placed, out_specs=P("row", "col", None), check_vma=False
-    )
+        per_device, mesh=chips, in_specs=placed, out_specs=P(ROW, "col", None), check_vma=False
+    )

time: 94.8 us -> 95.6 us (level)
    ppermute x4, waiting for transfers between devices: 2.62 us -> 4.36 us  [shifted(): lax.ppermute(cells, axis, [(i, (i + by) % count) for i in range(count)])]
    all_to_all x1, waiting for transfers between devices: 31.3 us -> 30.1 us  [per_device(): lax.all_to_all(payload, ('core', 'z', 'col'), split_axis=0, concat_axis=0...]
  transfers between devices with their start and end apart: 5 -> 5, of which waited for: 2 -> 3; matrix products, arithmetic and copies ran while one was open for 1% -> 1% of each run, Pallas kernels for 13% -> 13%
where the time goes in v6:
time: 95.6 us; the launch traced here: 95.4 us
  Pallas kernels  41.5 us (43%)
  waiting for transfers between devices  34.5 us (36%)
  starting transfers between devices  17.8 us (19%)
  local copies, waits for them, and re-layouts  1.14 us (1%)
    all_to_all x1, waiting for transfers between devices, per_device(): lax.all_to_all(payload, ('core', 'z', 'col'), split_axis=0, concat_axis=0...  30.1 us
    pallas_call x1, Pallas kernels, rest(): pl.pallas_call(rest_kernel, out_shape=jax.ShapeDtypeStruct((4 * GRP, MODE...  21.6 us
    pallas_call x1, Pallas kernels, own_part(): pl.pallas_call(own_kernel, out_shape=[jax.ShapeDtypeStruct((4 * WIDE, MOD...  12.3 us
    all_to_all x1, starting transfers between devices, per_device(): lax.all_to_all(payload, ('core', 'z', 'col'), split_axis=0, concat_axis=0...  11.1 us
    ppermute x4, starting transfers between devices, shifted(): lax.ppermute(cells, axis, [(i, (i + by) % count) for i in range(count)])  6.64 us
    pallas_call x1, Pallas kernels, pack(): pl.pallas_call(pack_kernel, out_shape=jax.ShapeDtypeStruct((rows, CH * 12...  4.76 us
    ppermute x4, waiting for transfers between devices, shifted(): lax.ppermute(cells, axis, [(i, (i + by) % count) for i in range(count)])  4.36 us
    pallas_call x1, Pallas kernels, merge(): pl.pallas_call(merge_kernel, out_shape=[jax.ShapeDtypeStruct((4 * GRP, PA...  2.88 us
  transfers between devices with their start and end apart: 5, of which 3 were waited for; matrix products, arithmetic and copies ran while one was open for 1% of the time, Pallas kernels for 13%

profile of v6, /device:TPU:0, one launch (start us, length us, event | category | flops | bytes accessed | tf_op | source)
XLA Modules:
  0.0 95.4 jit_solution(8146291252561971980)
XLA Ops:
  0.0 4.8 %pack.1 = bf16[1024,1152]{1,0:T(8,128)(2,1)} custom-call(s32[1,128]{1,0:T(1,128)} %bitcast.17, s32[1,128]{1,0:T(1,128)} %bitcast.18, s32[1,128]{1,0:T(1,128)} %bitcast.19, f32[16,4,128]{2,1,0:T(4,128)} %prof_ref.1, f32[4096,128]{1,0:T(8,128)} %bitcast.15), custom_call_target="tpu_custom_call" | custom-call | tf_op jit(solution)/shard_map/pack/pallas_call | solution.py:128
  4.8 0.0 copy-start.2
  4.8 0.0 copy-start
  4.8 11.1 %all-to-all-start = ((bf16[128,8,1152]{2,1,0:T(8,128)(2,1)}), bf16[128,8,1152]{2,1,0:T(8,128)(2,1)S(1)}, u32[]{:S(2)}, u32[]{:S(2)}) async-start(bf16[128,8,1152]{2,1,0:T(8,128)(2,1)} %bitcast.4), calls=%async_computation | async-start | bytes 4718592 | tf_op jit(solution)/shard_map/all_to_all | solution.py:547
  15.9 0.0 copy-done.2
  16.0 1.1 %copy.10 = bf16[8,8,8,1024]{3,2,0,1:T(8,128)(2,1)} copy(bf16[8,8,8,1024]{3,2,1,0:T(8,128)(2,1)S(1)} %bitcast.16) | data formatting | bytes 2097152 | tf_op jit(solution)/shard_map/reshape | solution.py:545
  17.0 0.1 pad_add_fusion.place_ref
  17.1 30.1 %all-to-all-done = bf16[128,8,1152]{2,1,0:T(8,128)(2,1)S(1)} async-done(((bf16[128,8,1152]{2,1,0:T(8,128)(2,1)}), bf16[128,8,1152]{2,1,0:T(8,128)(2,1)S(1)}, u32[]{:S(2)}, u32[]{:S(2)}) %all-to-all-start) | async-done | bytes 2359328 | tf_op jit(solution)/shard_map/all_to_all | solution.py:547
  47.2 0.0 copy-done
  47.2 2.9 %merge.1 = (bf16[512,512]{1,0:T(8,128)(2,1)S(1)}, bf16[128,512]{1,0:T(8,128)(2,1)S(1)}, bf16[128,512]{1,0:T(8,128)(2,1)S(1)}, bf16[512,1024]{1,0:T(8,128)(2,1)S(1)}, bf16[1024,1024]{1,0:T(8,128)(2,1)S(1)}) custom-call(bf16[1024,1152]{1,0:T(8,128)(2,1)S(1)} %bitcast.13, f32[16,4,128]{2,1,0:T(4,128)S(1)} %copy-done, bf16[512,1024]{1,0:T(8,128)(2,1)} %bitcast.14, ...), custom_call_target="tpu_custom_call" | custom-call | tf_op jit(solution)/shard_map/merge/pallas_call | solution.py:229
  50.1 0.0 copy-start.1
  50.1 0.0 collective-permute-start
  50.2 2.9 %collective-permute-start.1 = (bf16[128,512]{1,0:T(8,128)(2,1)S(1)}, bf16[128,512]{1,0:T(8,128)(2,1)S(1)}, u32[]{:S(2)}, u32[]{:S(2)}) collective-permute-start(bf16[128,512]{1,0:T(8,128)(2,1)S(1)} %get-tuple-element.25), channel_id=1, source_target_pairs={{0,112},{16,0},{32,16},{48,32},{64,48},{80,64},{96,80},{112,96},{1... | collective-permute-start | bytes 393224 | tf_op jit(solution)/shard_map/ppermute | solution.py:520
  53.2 2.6 %collective-permute-done.top_ref = bf16[128,512]{1,0:T(8,128)(2,1)S(1)} collective-permute-done((bf16[128,512]{1,0:T(8,128)(2,1)S(1)}, bf16[128,512]{1,0:T(8,128)(2,1)S(1)}, u32[]{:S(2)}, u32[]{:S(2)}) %collective-permute-start) | collective-permute-done | bytes 131104 | tf_op jit(solution)/shard_map/ppermute | solution.py:520
  55.8 0.0 collective-permute-done.1.bot_ref
  55.8 3.4 %collective-permute-start.2 = (bf16[384,512]{1,0:T(8,128)(2,1)S(1)}, bf16[384,512]{1,0:T(8,128)(2,1)S(1)}, u32[]{:S(2)}, u32[]{:S(2)}) collective-permute-start(bf16[384,512]{1,0:T(8,128)(2,1)S(1)} %pad_maximum_fusion), channel_id=1, source_target_pairs={{0,15},{1,0},{2,1},{3,2},{4,3},{5,4},{6,5},{7,6},{8,7},{9,8},{10,9... | collective-permute-start | bytes 1179656 | tf_op jit(solution)/shard_map/ppermute | solution.py:520
  59.3 0.3 collective-permute-start.3
  59.6 0.0 copy-done.1
  59.6 12.3 %own.1 = (f32[768,1024]{1,0:T(8,128)S(1)}, bf16[768,1024]{1,0:T(8,128)(2,1)S(1)}, bf16[768,2048]{1,0:T(8,128)(2,1)S(1)}, f32[256,1024]{1,0:T(8,128)S(1)}, bf16[3...) custom-call(s32[4]{0:T(128)S(1)} %pad_add_fusion.place_ref, ...), custom_call_target="tpu_custom_call" | custom-call | flops 4831838208 | bytes 12582912 | tf_op jit(solution)/shard_map/own/pallas_call | solution.py:326
  71.9 0.0 collective-permute-done.2.right_ref
  71.9 1.7 %collective-permute-done.3.left_ref = bf16[384,512]{1,0:T(8,128)(2,1)S(1)} collective-permute-done((bf16[384,512]{1,0:T(8,128)(2,1)S(1)}, bf16[384,512]{1,0:T(8,128)(2,1)S(1)}, u32[]{:S(2)}, u32[]{:S(2)}) %collective-permute-start.3) | collective-permute-done | bytes 393248 | tf_op jit(solution)/shard_map/ppermute | solution.py:520
  73.6 21.6 %rest.1 = bf16[512,1024]{1,0:T(8,128)(2,1)} custom-call(s32[4]{0:T(128)S(1)} %pad_add_fusion.place_ref, bf16[384,512]{1,0:T(8,128)(2,1)S(1)} %collective-permute-done.2.right_ref, bf16[384,512]{1,0:T(8,128)(2,1)S(1)} %collective-permute-done.3.left_ref, f32[768,1024]{1,0:T(8,128)S(1)} %get-tuple-element.28.stream_ref, ...), custom_call_target="tpu_custom_call" | custom-call | tf_op jit(solution)/shard_map/rest/pallas_call | solution.py:494
  (6 shorter events, 0.1 us)
Async XLA Ops:
  4.8 11.2 %copy-start.2 = (bf16[512,1024]{1,0:T(8,128)(2,1)S(1)}, bf16[512,1024]{1,0:T(8,128)(2,1)}, u32[]{:S(2)}) copy-start(bf16[512,1024]{1,0:T(8,128)(2,1)} %param.14) | copy-start | bytes 3145732
  4.8 42.5 %copy-start = (f32[16,4,128]{2,1,0:T(4,128)S(1)}, f32[16,4,128]{2,1,0:T(4,128)}, u32[]{:S(2)}) copy-start(f32[16,4,128]{2,1,0:T(4,128)} %prof_ref.1) | copy-start | bytes 98308
  4.8 42.5 %all-to-all-start = ((bf16[128,8,1152]{2,1,0:T(8,128)(2,1)}), bf16[128,8,1152]{2,1,0:T(8,128)(2,1)S(1)}, u32[]{:S(2)}, u32[]{:S(2)}) async-start(bf16[128,8,1152]{2,1,0:T(8,128)(2,1)} %bitcast.4), calls=%async_computation | async-start | bytes 4718592 | tf_op jit(solution)/shard_map/all_to_all | solution.py:547
  50.1 9.4 %copy-start.1 = (f32[2,1024]{1,0:T(2,128)S(1)}, f32[2,1024]{1,0:T(2,128)}, u32[]{:S(2)}) copy-start(f32[2,1024]{1,0:T(2,128)} %gain_ref.3) | copy-start | bytes 24580
  50.1 5.6 %collective-permute-start = (bf16[128,512]{1,0:T(8,128)(2,1)S(1)}, bf16[128,512]{1,0:T(8,128)(2,1)S(1)}, u32[]{:S(2)}, u32[]{:S(2)}) collective-permute-start(bf16[128,512]{1,0:T(8,128)(2,1)S(1)} %get-tuple-element.23), channel_id=1, source_target_pairs={{0,16},{16,32},{32,48},{48,64},{64,80},{80,96},{96,112},{112,0},{1... | collective-permute-start | bytes 393224 | tf_op jit(solution)/shard_map/ppermute | solution.py:520
  50.2 5.6 %collective-permute-start.1 = (bf16[128,512]{1,0:T(8,128)(2,1)S(1)}, bf16[128,512]{1,0:T(8,128)(2,1)S(1)}, u32[]{:S(2)}, u32[]{:S(2)}) collective-permute-start(bf16[128,512]{1,0:T(8,128)(2,1)S(1)} %get-tuple-element.25), channel_id=1, source_target_pairs={{0,112},{16,0},{32,16},{48,32},{64,48},{80,64},{96,80},{112,96},{1... | collective-permute-start | bytes 393224 | tf_op jit(solution)/shard_map/ppermute | solution.py:520
  55.8 16.0 %collective-permute-start.2 = (bf16[384,512]{1,0:T(8,128)(2,1)S(1)}, bf16[384,512]{1,0:T(8,128)(2,1)S(1)}, u32[]{:S(2)}, u32[]{:S(2)}) collective-permute-start(bf16[384,512]{1,0:T(8,128)(2,1)S(1)} %pad_maximum_fusion), channel_id=1, source_target_pairs={{0,15},{1,0},{2,1},{3,2},{4,3},{5,4},{6,5},{7,6},{8,7},{9,8},{10,9... | collective-permute-start | bytes 1179656 | tf_op jit(solution)/shard_map/ppermute | solution.py:520
  59.3 14.3 %collective-permute-start.3 = (bf16[384,512]{1,0:T(8,128)(2,1)S(1)}, bf16[384,512]{1,0:T(8,128)(2,1)S(1)}, u32[]{:S(2)}, u32[]{:S(2)}) collective-permute-start(bf16[384,512]{1,0:T(8,128)(2,1)S(1)} %pad_maximum_fusion.1), channel_id=1, source_target_pairs={{0,1},{1,2},{2,3},{3,4},{4,5},{5,6},{6,7},{7,8},{8,9},{9,10},{10,1... | collective-permute-start | bytes 1179656 | tf_op jit(solution)/shard_map/ppermute | solution.py:520

commit v7 on v6

--- a/solution.py
+++ b/solution.py
@@ -5,14 +5,12 @@
 from jax import lax
 from jax.experimental import pallas as pl
 from jax.experimental.pallas import tpu as pltpu
-from jax.sharding import Mesh
 from jax.sharding import PartitionSpec as P
 
 HEADS = 16
 RADIUS = 4
 TOK_H = 32
 TOK_W = 16
-N_COL = 16
 BR = 4
 CH = 8
 MODEL = 1024
@@ -27,8 +25,6 @@
 VMEM_BYTES = 16 * 1024 * 1024
 LARGE_BYTES = 22 * 1024 * 1024
 
-ROW = ("z", "core")
-
 f32 = jnp.float32
 bf16 = jnp.bfloat16
 i32 = jnp.int32
@@ -78,10 +74,7 @@
     for copy in small:
         copy.wait()
     eye = iota((count, count), 0) == iota((count, count), 1)
-    tile = dest_ref[...]
-    depth = count // (2 * N_COL)
-    place = (tile // N_COL % 2 * depth + tile // (2 * N_COL)) * N_COL + tile % N_COL
-    dest_row = place.astype(f32)
+    dest_row = dest_ref[...].astype(f32)
     dest_col = jnp.sum(jnp.where(eye, dest_row, 0.0), axis=1, keepdims=True)
     before = iota((count, count), 0) < iota((count, count), 1)
     same = (dest_col == dest_row) & before
@@ -401,8 +394,8 @@
 
 def rest_kernel(
     place_ref, right_ref, left_ref, stream_ref, oq_ref, okv_ref, omid_ref, mq_ref, mkv_ref, wkv_ref,
-    o_ref, next_ref, gain_ref, embed_ref, wq_ref, o_hbm, out_ref,
-    last_ref, side_ref, sq_ref, skv_ref, q_ref, kv_ref, mid_ref, att_ref, inp_ref, sem,
+    o_ref, next_ref, gain_ref, embed_ref, wq_ref, o_hbm, out_hbm,
+    last_ref, side_ref, sq_ref, skv_ref, q_ref, kv_ref, mid_ref, att_ref, inp_ref, sem, out_sem,
 ):
     copy = pltpu.make_async_copy(o_hbm.at[1], last_ref, sem)
     copy.start()
@@ -479,11 +472,23 @@
             (g // 3) * GRP : (g // 3 + 1) * GRP, :
         ]
         inp_ref[rows, :] = (before + dot(att_ref[rows, :], last_ref[...])).astype(bf16)
-    for r in range(0, 4 * GRP, GRP):
-        to = iota((GRP, 4 * GRP), 0) + r
-        source = iota((GRP, 4 * GRP), 1)
-        wanted = (to // 4 % 4) * GRP + (to // 16) * 4 + to % 4
-        out_ref[r : r + GRP, :] = dot(onehot(source == wanted), inp_ref[: 4 * GRP, :]).astype(bf16)
+    to = iota((GRP, GRP), 0)
+    wanted = (to // 4 % 4) * 32 + (to // 16) * 4 + to % 4
+    reorder = onehot(iota((GRP, GRP), 1) == wanted)
+    outs = []
+    for n in range(4):
+        rows = slice(n * GRP, (n + 1) * GRP)
+        tokens = jnp.concatenate(
+            [inp_ref[g * GRP + n * 32 : g * GRP + (n + 1) * 32, :] for g in range(4)], axis=0
+        )
+        att_ref[rows, :] = dot(reorder, tokens).astype(bf16)
+        span = pl.ds(n * GRP, GRP)
+        outs.append(
+            pltpu.make_async_copy(att_ref.at[span, :], out_hbm.at[span, :], out_sem.at[n])
+        )
+        outs[-1].start()
+    for out in outs:
+        out.wait()
 
 
 def rest(place, left, right, own, gain, embed, w, out_weight):
@@ -495,6 +500,7 @@
         rest_kernel,
         out_shape=jax.ShapeDtypeStruct((4 * GRP, MODEL), bf16),
         in_specs=[smem] + [vmem] * 14 + [hbm],
+        out_specs=hbm,
         scratch_shapes=[
             pltpu.VMEM((MODEL, MODEL), bf16),
             pltpu.VMEM((2 * WIDE, MODEL), f32),
@@ -506,6 +512,7 @@
             pltpu.VMEM((6 * MID, MODEL), bf16),
             pltpu.VMEM((4 * WIDE, MODEL), bf16),
             pltpu.SemaphoreType.DMA,
+            pltpu.SemaphoreType.DMA((4,)),
         ],
         compiler_params=pltpu.CompilerParams(vmem_limit_bytes=LARGE_BYTES),
         name="rest",
@@ -521,8 +528,8 @@
 
 
 def around(x, first, last):
-    top = shifted(last, ROW, 1)
-    bottom = shifted(first, ROW, -1)
+    top = shifted(last, "row", 1)
+    bottom = shifted(first, "row", -1)
     two = 2 * HALO
     right_edge = jnp.concatenate([top[two:], x[2 * GRP :], bottom[two:]], axis=0)
     left_edge = jnp.concatenate([top[:two], x[: 2 * GRP], bottom[:two]], axis=0)
@@ -536,17 +543,15 @@
 ):
     place = jnp.stack(
         [
-            lax.axis_index(ROW) * TOK_H,
+            lax.axis_index("row") * TOK_H,
             lax.axis_index("col") * TOK_W,
-            jnp.asarray(lax.axis_size(ROW) * TOK_H, i32),
+            jnp.asarray(lax.axis_size("row") * TOK_H, i32),
             jnp.asarray(lax.axis_size("col") * TOK_W, i32),
         ]
     ).astype(i32)
     embed = embed_weight.reshape(CH, 8, 8, MODEL).transpose(1, 0, 2, 3).reshape(PATCH, MODEL)
     payload = pack(dest, offsets, profile_index, profiles, scans)
-    payload = lax.all_to_all(
-        payload, ("core", "z", "col"), split_axis=0, concat_axis=0, tiled=True
-    )
+    payload = lax.all_to_all(payload, ("row", "col"), split_axis=0, concat_axis=0, tiled=True)
     payload, place = lax.optimization_barrier((payload, place))
     x, first, last, embed, w = merge(payload, profiles, embed, qkv_weight)
     top, bottom, left, right = around(x, first, last)
@@ -556,10 +561,17 @@
 
 
 def solution(mesh):
-    rows, cols = mesh.shape["row"], mesh.shape["col"]
-    chips = Mesh(mesh.devices.reshape(rows // 2, 2, cols), (*ROW, "col"))
-    every = (*ROW, "col")
-    placed = (P(every, None, None, None), P(every, None), P(every), P(every), P(), P(), P(), P(), P())
+    placed = (
+        P(("row", "col"), None, None, None),
+        P(("row", "col"), None),
+        P(("row", "col")),
+        P(("row", "col")),
+        P(),
+        P(),
+        P(),
+        P(),
+        P(),
+    )
     return jax.shard_map(
-        per_device, mesh=chips, in_specs=placed, out_specs=P(ROW, "col", None), check_vma=False
-    )
+        per_device, mesh=mesh, in_specs=placed, out_specs=P("row", "col", None), check_vma=False
+    )

time: 95.6 us -> 94 us (0.983)
    ppermute x4, waiting for transfers between devices: 4.36 us -> 2.62 us  [shifted(): lax.ppermute(cells, axis, [(i, (i + by) % count) for i in range(count)])]
    all_to_all x1, waiting for transfers between devices: 30.1 us -> 31.3 us  [per_device(): lax.all_to_all(payload, ('row', 'col'), split_axis=0, concat_axis=0, tile...]
  transfers between devices with their start and end apart: 5 -> 5, of which waited for: 3 -> 2; matrix products, arithmetic and copies ran while one was open for 1% -> 1% of each run, Pallas kernels for 13% -> 13%
where the time goes in v7:
time: 94 us; the launch traced here: 93.7 us
  Pallas kernels  41.1 us (44%)
  waiting for transfers between devices  33.9 us (36%)
  starting transfers between devices  17 us (18%)
  local copies, waits for them, and re-layouts  1.14 us (1%)
    all_to_all x1, waiting for transfers between devices, per_device(): lax.all_to_all(payload, ('row', 'col'), split_axis=0, concat_axis=0, tile...  31.3 us
    pallas_call x1, Pallas kernels, rest(): pl.pallas_call(rest_kernel, out_shape=jax.ShapeDtypeStruct((4 * GRP, MODE...  21.2 us
    pallas_call x1, Pallas kernels, own_part(): pl.pallas_call(own_kernel, out_shape=[jax.ShapeDtypeStruct((4 * WIDE, MOD...  12.3 us
    all_to_all x1, starting transfers between devices, per_device(): lax.all_to_all(payload, ('row', 'col'), split_axis=0, concat_axis=0, tile...  11.1 us
    ppermute x4, starting transfers between devices, shifted(): lax.ppermute(cells, axis, [(i, (i + by) % count) for i in range(count)])  5.91 us
    pallas_call x1, Pallas kernels, pack(): pl.pallas_call(pack_kernel, out_shape=jax.ShapeDtypeStruct((rows, CH * 12...  4.75 us
    pallas_call x1, Pallas kernels, merge(): pl.pallas_call(merge_kernel, out_shape=[jax.ShapeDtypeStruct((4 * GRP, PA...  2.88 us
    ppermute x4, waiting for transfers between devices, shifted(): lax.ppermute(cells, axis, [(i, (i + by) % count) for i in range(count)])  2.62 us
  transfers between devices with their start and end apart: 5, of which 2 were waited for; matrix products, arithmetic and copies ran while one was open for 1% of the time, Pallas kernels for 13%

profile of v7, /device:TPU:0, one launch (start us, length us, event | category | flops | bytes accessed | tf_op | source)
XLA Modules:
  0.0 93.7 jit_solution(752378442045819902)
XLA Ops:
  0.0 4.8 %pack.1 = bf16[1024,1152]{1,0:T(8,128)(2,1)} custom-call(s32[1,128]{1,0:T(1,128)} %bitcast.17, s32[1,128]{1,0:T(1,128)} %bitcast.18, s32[1,128]{1,0:T(1,128)} %bitcast.19, f32[16,4,128]{2,1,0:T(4,128)} %prof_ref.1, f32[4096,128]{1,0:T(8,128)} %bitcast.15), custom_call_target="tpu_custom_call" | custom-call | tf_op jit(solution)/shard_map/pack/pallas_call | solution.py:121
  4.8 0.0 copy-start.2
  4.8 0.0 copy-start
  4.8 11.1 %all-to-all-start = ((bf16[128,8,1152]{2,1,0:T(8,128)(2,1)}), bf16[128,8,1152]{2,1,0:T(8,128)(2,1)S(1)}, u32[]{:S(2)}, u32[]{:S(2)}) async-start(bf16[128,8,1152]{2,1,0:T(8,128)(2,1)} %bitcast.4), calls=%async_computation | async-start | bytes 4718592 | tf_op jit(solution)/shard_map/all_to_all | solution.py:554
  15.9 0.0 copy-done.2
  16.0 1.1 %copy.10 = bf16[8,8,8,1024]{3,2,0,1:T(8,128)(2,1)} copy(bf16[8,8,8,1024]{3,2,1,0:T(8,128)(2,1)S(1)} %bitcast.16) | data formatting | bytes 2097152 | tf_op jit(solution)/shard_map/reshape | solution.py:552
  17.0 0.1 pad_add_fusion.place_ref
  17.1 31.3 %all-to-all-done = bf16[128,8,1152]{2,1,0:T(8,128)(2,1)S(1)} async-done(((bf16[128,8,1152]{2,1,0:T(8,128)(2,1)}), bf16[128,8,1152]{2,1,0:T(8,128)(2,1)S(1)}, u32[]{:S(2)}, u32[]{:S(2)}) %all-to-all-start) | async-done | bytes 2359328 | tf_op jit(solution)/shard_map/all_to_all | solution.py:554
  48.4 0.0 copy-done
  48.4 2.9 %merge.1 = (bf16[512,512]{1,0:T(8,128)(2,1)S(1)}, bf16[128,512]{1,0:T(8,128)(2,1)S(1)}, bf16[128,512]{1,0:T(8,128)(2,1)S(1)}, bf16[512,1024]{1,0:T(8,128)(2,1)S(1)}, bf16[1024,1024]{1,0:T(8,128)(2,1)S(1)}) custom-call(bf16[1024,1152]{1,0:T(8,128)(2,1)S(1)} %bitcast.13, f32[16,4,128]{2,1,0:T(4,128)S(1)} %copy-done, bf16[512,1024]{1,0:T(8,128)(2,1)} %bitcast.14, ...), custom_call_target="tpu_custom_call" | custom-call | tf_op jit(solution)/shard_map/merge/pallas_call | solution.py:222
  51.3 0.0 copy-start.1
  51.3 0.0 collective-permute-start
  51.4 2.9 %collective-permute-start.1 = (bf16[128,512]{1,0:T(8,128)(2,1)S(1)}, bf16[128,512]{1,0:T(8,128)(2,1)S(1)}, u32[]{:S(2)}, u32[]{:S(2)}) collective-permute-start(bf16[128,512]{1,0:T(8,128)(2,1)S(1)} %get-tuple-element.25), channel_id=1, source_target_pairs={{0,112},{16,0},{32,16},{48,32},{64,48},{80,64},{96,80},{112,96},{1... | collective-permute-start | bytes 393224 | tf_op jit(solution)/shard_map/ppermute | solution.py:527
  54.3 2.6 %collective-permute-done.top_ref = bf16[128,512]{1,0:T(8,128)(2,1)S(1)} collective-permute-done((bf16[128,512]{1,0:T(8,128)(2,1)S(1)}, bf16[128,512]{1,0:T(8,128)(2,1)S(1)}, u32[]{:S(2)}, u32[]{:S(2)}) %collective-permute-start) | collective-permute-done | bytes 131104 | tf_op jit(solution)/shard_map/ppermute | solution.py:527
  57.0 0.0 collective-permute-done.1.bot_ref
  57.0 2.7 %collective-permute-start.2 = (bf16[384,512]{1,0:T(8,128)(2,1)S(1)}, bf16[384,512]{1,0:T(8,128)(2,1)S(1)}, u32[]{:S(2)}, u32[]{:S(2)}) collective-permute-start(bf16[384,512]{1,0:T(8,128)(2,1)S(1)} %pad_maximum_fusion), channel_id=1, source_target_pairs={{0,15},{1,0},{2,1},{3,2},{4,3},{5,4},{6,5},{7,6},{8,7},{9,8},{10,9... | collective-permute-start | bytes 1179656 | tf_op jit(solution)/shard_map/ppermute | solution.py:527
  59.7 0.3 collective-permute-start.3
  60.0 0.0 copy-done.1
  60.0 12.3 %own.1 = (f32[768,1024]{1,0:T(8,128)S(1)}, bf16[768,1024]{1,0:T(8,128)(2,1)S(1)}, bf16[768,2048]{1,0:T(8,128)(2,1)S(1)}, f32[256,1024]{1,0:T(8,128)S(1)}, bf16[3...) custom-call(s32[4]{0:T(128)S(1)} %pad_add_fusion.place_ref, ...), custom_call_target="tpu_custom_call" | custom-call | flops 4831838208 | bytes 12582912 | tf_op jit(solution)/shard_map/own/pallas_call | solution.py:319
  72.3 0.0 collective-permute-done.2.right_ref
  72.3 0.0 collective-permute-done.3.left_ref
  72.3 21.2 %rest.1 = bf16[512,1024]{1,0:T(8,128)(2,1)} custom-call(s32[4]{0:T(128)S(1)} %pad_add_fusion.place_ref, bf16[384,512]{1,0:T(8,128)(2,1)S(1)} %collective-permute-done.2.right_ref, bf16[384,512]{1,0:T(8,128)(2,1)S(1)} %collective-permute-done.3.left_ref, f32[768,1024]{1,0:T(8,128)S(1)} %get-tuple-element.28.stream_ref, ...), custom_call_target="tpu_custom_call" | custom-call | tf_op jit(solution)/shard_map/rest/pallas_call | solution.py:499
  (6 shorter events, 0.1 us)
Async XLA Ops:
  4.8 11.2 %copy-start.2 = (bf16[512,1024]{1,0:T(8,128)(2,1)S(1)}, bf16[512,1024]{1,0:T(8,128)(2,1)}, u32[]{:S(2)}) copy-start(bf16[512,1024]{1,0:T(8,128)(2,1)} %param.14) | copy-start | bytes 3145732
  4.8 43.7 %copy-start = (f32[16,4,128]{2,1,0:T(4,128)S(1)}, f32[16,4,128]{2,1,0:T(4,128)}, u32[]{:S(2)}) copy-start(f32[16,4,128]{2,1,0:T(4,128)} %prof_ref.1) | copy-start | bytes 98308
  4.8 43.6 %all-to-all-start = ((bf16[128,8,1152]{2,1,0:T(8,128)(2,1)}), bf16[128,8,1152]{2,1,0:T(8,128)(2,1)S(1)}, u32[]{:S(2)}, u32[]{:S(2)}) async-start(bf16[128,8,1152]{2,1,0:T(8,128)(2,1)} %bitcast.4), calls=%async_computation | async-start | bytes 4718592 | tf_op jit(solution)/shard_map/all_to_all | solution.py:554
  51.3 8.7 %copy-start.1 = (f32[2,1024]{1,0:T(2,128)S(1)}, f32[2,1024]{1,0:T(2,128)}, u32[]{:S(2)}) copy-start(f32[2,1024]{1,0:T(2,128)} %gain_ref.3) | copy-start | bytes 24580
  51.3 5.6 %collective-permute-start = (bf16[128,512]{1,0:T(8,128)(2,1)S(1)}, bf16[128,512]{1,0:T(8,128)(2,1)S(1)}, u32[]{:S(2)}, u32[]{:S(2)}) collective-permute-start(bf16[128,512]{1,0:T(8,128)(2,1)S(1)} %get-tuple-element.23), channel_id=1, source_target_pairs={{0,16},{16,32},{32,48},{48,64},{64,80},{80,96},{96,112},{112,0},{1... | collective-permute-start | bytes 393224 | tf_op jit(solution)/shard_map/ppermute | solution.py:527
  51.4 5.6 %collective-permute-start.1 = (bf16[128,512]{1,0:T(8,128)(2,1)S(1)}, bf16[128,512]{1,0:T(8,128)(2,1)S(1)}, u32[]{:S(2)}, u32[]{:S(2)}) collective-permute-start(bf16[128,512]{1,0:T(8,128)(2,1)S(1)} %get-tuple-element.25), channel_id=1, source_target_pairs={{0,112},{16,0},{32,16},{48,32},{64,48},{80,64},{96,80},{112,96},{1... | collective-permute-start | bytes 393224 | tf_op jit(solution)/shard_map/ppermute | solution.py:527
  57.0 15.3 %collective-permute-start.2 = (bf16[384,512]{1,0:T(8,128)(2,1)S(1)}, bf16[384,512]{1,0:T(8,128)(2,1)S(1)}, u32[]{:S(2)}, u32[]{:S(2)}) collective-permute-start(bf16[384,512]{1,0:T(8,128)(2,1)S(1)} %pad_maximum_fusion), channel_id=1, source_target_pairs={{0,15},{1,0},{2,1},{3,2},{4,3},{5,4},{6,5},{7,6},{8,7},{9,8},{10,9... | collective-permute-start | bytes 1179656 | tf_op jit(solution)/shard_map/ppermute | solution.py:527
  59.7 12.6 %collective-permute-start.3 = (bf16[384,512]{1,0:T(8,128)(2,1)S(1)}, bf16[384,512]{1,0:T(8,128)(2,1)S(1)}, u32[]{:S(2)}, u32[]{:S(2)}) collective-permute-start(bf16[384,512]{1,0:T(8,128)(2,1)S(1)} %pad_maximum_fusion.1), channel_id=1, source_target_pairs={{0,1},{1,2},{2,3},{3,4},{4,5},{5,6},{6,7},{7,8},{8,9},{9,10},{10,1... | collective-permute-start | bytes 1179656 | tf_op jit(solution)/shard_map/ppermute | solution.py:527

commit v8 on v7

--- a/solution.py
+++ b/solution.py
@@ -268,13 +268,14 @@
         rows = slice(g * WIDE, (g + 1) * WIDE)
         stream_ref[rows, :] = stream
         inp_ref[rows, :] = normed(stream, gain_ref[0:1, :])
-    project_queries(inp_ref[...], wq_ref, q_ref)
+    queries = [inp_ref[g * WIDE + 16 : g * WIDE + 16 + MID, :] for g in range(4)]
+    project_queries(jnp.concatenate(queries, axis=0), wq_ref, q_ref)
     copies[0].wait()
     project_keys(inp_ref[...], wkv_ref, 0, kv_ref)
     attention(
         [1],
         5,
-        lambda g: (q_ref, (g - 1) * WIDE + 16),
+        lambda g: (q_ref, (g - 1) * MID),
         lambda g: (kv_ref, (g - 2) * WIDE),
         lambda g: (att_ref, (g - 2) * MID),
         place_ref[0] - 8,
@@ -289,8 +290,9 @@
         stream = before + dot(att_ref[rows, :], o_ref[...])
         mid_ref[n * GRP : (n + 1) * GRP, :] = stream[16 : 16 + GRP, :]
         inp_ref[rows, :] = normed(stream, gain_ref[1:2, :])
-    inputs = inp_ref[: 2 * MID, :]
-    project(inputs, inputs, next_ref, later_q_ref, later_kv_ref)
+    queries = [inp_ref[n * MID + 16 : n * MID + 16 + GRP, :] for n in range(2)]
+    queries = jnp.concatenate(queries, axis=0)
+    project(queries, inp_ref[: 2 * MID, :], next_ref, later_q_ref, later_kv_ref)
 
 
 def project_queries(inputs, w_ref, q_ref):
@@ -320,10 +322,10 @@
         own_kernel,
         out_shape=[
             jax.ShapeDtypeStruct((4 * WIDE, MODEL), f32),
-            jax.ShapeDtypeStruct((4 * WIDE, MODEL), bf16),
+            jax.ShapeDtypeStruct((4 * MID, MODEL), bf16),
             jax.ShapeDtypeStruct((4 * WIDE, 2 * MODEL), bf16),
             jax.ShapeDtypeStruct((2 * GRP, MODEL), f32),
-            jax.ShapeDtypeStruct((2 * MID, MODEL), bf16),
+            jax.ShapeDtypeStruct((2 * GRP, MODEL), bf16),
             jax.ShapeDtypeStruct((2 * MID, 2 * MODEL), bf16),
             pltpu.VMEM((MODEL, 2 * MODEL), bf16),
             pltpu.VMEM((MODEL, MODEL), bf16),
@@ -415,13 +417,14 @@
         inp_ref[n * WIDE : (n + 1) * WIDE, :] = normed(stream, gain_ref[0:1, :])
         if n in (1, 2):
             side_ref[(n - 1) * WIDE : n * WIDE, :] = stream
-    project_queries(inp_ref[WIDE : 3 * WIDE, :], wq_ref, sq_ref)
+    queries = [inp_ref[g * WIDE + 16 : g * WIDE + 16 + MID, :] for g in (1, 2)]
+    project_queries(jnp.concatenate(queries, axis=0), wq_ref, sq_ref)
     project_keys(inp_ref[: 4 * WIDE, :], wkv_ref, 0, skv_ref)
 
     def q_of(g):
         if g in (0, 5):
-            return sq_ref, (g // 5) * WIDE + 16
-        return oq_ref, (g - 1) * WIDE + 16
+            return sq_ref, (g // 5) * MID
+        return oq_ref, (g - 1) * MID
 
     def kv_of(g):
         if g in (0, 1, 6, 7):
@@ -443,12 +446,14 @@
             mid_ref[(n - 1) * GRP : n * GRP, :] = stream[16 : 16 + GRP, :]
         inp_ref[rows, :] = normed(stream, gain_ref[1:2, :])
 
-    project(inp_ref[MID : 3 * MID, :], inp_ref[: 4 * MID, :], next_ref, q_ref, kv_ref)
+    queries = [inp_ref[n * MID + 16 : n * MID + 16 + GRP, :] for n in (1, 2)]
+    queries = jnp.concatenate(queries, axis=0)
+    project(queries, inp_ref[: 4 * MID, :], next_ref, q_ref, kv_ref)
 
     def later_q_of(g):
         if g in (0, 3):
-            return q_ref, (g // 3) * MID + 16
-        return mq_ref, (g - 1) * MID + 16
+            return q_ref, (g // 3) * GRP
+        return mq_ref, (g - 1) * GRP
 
     def later_kv_of(g):
         if g in (2, 3):
@@ -504,7 +509,7 @@
         scratch_shapes=[
             pltpu.VMEM((MODEL, MODEL), bf16),
             pltpu.VMEM((2 * WIDE, MODEL), f32),
-            pltpu.VMEM((2 * WIDE, MODEL), bf16),
+            pltpu.VMEM((2 * MID, MODEL), bf16),
             pltpu.VMEM((4 * WIDE, 2 * MODEL), bf16),
             pltpu.VMEM((2 * MID, MODEL), bf16),
             pltpu.VMEM((4 * MID, 2 * MODEL), bf16),

time: 94 us -> 92.3 us (0.982)
  Pallas kernels: 41.1 us -> 39.5 us
    pallas_call x1, Pallas kernels: 21.2 us -> 19.8 us  [rest(): pl.pallas_call(rest_kernel, out_shape=jax.ShapeDtypeStruct((4 * GRP, MODE...]
where the time goes in v8:
time: 92.3 us; the launch traced here: 92.1 us
  Pallas kernels  39.5 us (43%)
  waiting for transfers between devices  33.9 us (37%)
  starting transfers between devices  17 us (18%)
  local copies, waits for them, and re-layouts  1.14 us (1%)
    all_to_all x1, waiting for transfers between devices, per_device(): lax.all_to_all(payload, ('row', 'col'), split_axis=0, concat_axis=0, tile...  31.3 us
    pallas_call x1, Pallas kernels, rest(): pl.pallas_call(rest_kernel, out_shape=jax.ShapeDtypeStruct((4 * GRP, MODE...  19.8 us
    pallas_call x1, Pallas kernels, own_part(): pl.pallas_call(own_kernel, out_shape=[jax.ShapeDtypeStruct((4 * WIDE, MOD...  12.1 us
    all_to_all x1, starting transfers between devices, per_device(): lax.all_to_all(payload, ('row', 'col'), split_axis=0, concat_axis=0, tile...  11.1 us
    ppermute x4, starting transfers between devices, shifted(): lax.ppermute(cells, axis, [(i, (i + by) % count) for i in range(count)])  5.91 us
    pallas_call x1, Pallas kernels, pack(): pl.pallas_call(pack_kernel, out_shape=jax.ShapeDtypeStruct((rows, CH * 12...  4.75 us
    pallas_call x1, Pallas kernels, merge(): pl.pallas_call(merge_kernel, out_shape=[jax.ShapeDtypeStruct((4 * GRP, PA...  2.88 us
    ppermute x4, waiting for transfers between devices, shifted(): lax.ppermute(cells, axis, [(i, (i + by) % count) for i in range(count)])  2.62 us
  transfers between devices with their start and end apart: 5, of which 2 were waited for; matrix products, arithmetic and copies ran while one was open for 1% of the time, Pallas kernels for 13%

profile of v8, /device:TPU:0, one launch (start us, length us, event | category | flops | bytes accessed | tf_op | source)
XLA Modules:
  0.0 92.1 jit_solution(9351863663401766162)
XLA Ops:
  0.0 4.8 %pack.1 = bf16[1024,1152]{1,0:T(8,128)(2,1)} custom-call(s32[1,128]{1,0:T(1,128)} %bitcast.17, s32[1,128]{1,0:T(1,128)} %bitcast.18, s32[1,128]{1,0:T(1,128)} %bitcast.19, f32[16,4,128]{2,1,0:T(4,128)} %prof_ref.1, f32[4096,128]{1,0:T(8,128)} %bitcast.15), custom_call_target="tpu_custom_call" | custom-call | tf_op jit(solution)/shard_map/pack/pallas_call | solution.py:121
  4.8 0.0 copy-start.2
  4.8 0.0 copy-start
  4.8 11.1 %all-to-all-start = ((bf16[128,8,1152]{2,1,0:T(8,128)(2,1)}), bf16[128,8,1152]{2,1,0:T(8,128)(2,1)S(1)}, u32[]{:S(2)}, u32[]{:S(2)}) async-start(bf16[128,8,1152]{2,1,0:T(8,128)(2,1)} %bitcast.4), calls=%async_computation | async-start | bytes 4718592 | tf_op jit(solution)/shard_map/all_to_all | solution.py:559
  15.9 0.0 copy-done.2
  16.0 1.1 %copy.10 = bf16[8,8,8,1024]{3,2,0,1:T(8,128)(2,1)} copy(bf16[8,8,8,1024]{3,2,1,0:T(8,128)(2,1)S(1)} %bitcast.16) | data formatting | bytes 2097152 | tf_op jit(solution)/shard_map/reshape | solution.py:557
  17.0 0.1 pad_add_fusion.place_ref
  17.1 31.3 %all-to-all-done = bf16[128,8,1152]{2,1,0:T(8,128)(2,1)S(1)} async-done(((bf16[128,8,1152]{2,1,0:T(8,128)(2,1)}), bf16[128,8,1152]{2,1,0:T(8,128)(2,1)S(1)}, u32[]{:S(2)}, u32[]{:S(2)}) %all-to-all-start) | async-done | bytes 2359328 | tf_op jit(solution)/shard_map/all_to_all | solution.py:559
  48.4 0.0 copy-done
  48.4 2.9 %merge.1 = (bf16[512,512]{1,0:T(8,128)(2,1)S(1)}, bf16[128,512]{1,0:T(8,128)(2,1)S(1)}, bf16[128,512]{1,0:T(8,128)(2,1)S(1)}, bf16[512,1024]{1,0:T(8,128)(2,1)S(1)}, bf16[1024,1024]{1,0:T(8,128)(2,1)S(1)}) custom-call(bf16[1024,1152]{1,0:T(8,128)(2,1)S(1)} %bitcast.13, f32[16,4,128]{2,1,0:T(4,128)S(1)} %copy-done, bf16[512,1024]{1,0:T(8,128)(2,1)} %bitcast.14, ...), custom_call_target="tpu_custom_call" | custom-call | tf_op jit(solution)/shard_map/merge/pallas_call | solution.py:222
  51.3 0.0 copy-start.1
  51.3 0.0 collective-permute-start
  51.4 2.9 %collective-permute-start.1 = (bf16[128,512]{1,0:T(8,128)(2,1)S(1)}, bf16[128,512]{1,0:T(8,128)(2,1)S(1)}, u32[]{:S(2)}, u32[]{:S(2)}) collective-permute-start(bf16[128,512]{1,0:T(8,128)(2,1)S(1)} %get-tuple-element.25), channel_id=1, source_target_pairs={{0,112},{16,0},{32,16},{48,32},{64,48},{80,64},{96,80},{112,96},{1... | collective-permute-start | bytes 393224 | tf_op jit(solution)/shard_map/ppermute | solution.py:532
  54.3 2.6 %collective-permute-done.top_ref = bf16[128,512]{1,0:T(8,128)(2,1)S(1)} collective-permute-done((bf16[128,512]{1,0:T(8,128)(2,1)S(1)}, bf16[128,512]{1,0:T(8,128)(2,1)S(1)}, u32[]{:S(2)}, u32[]{:S(2)}) %collective-permute-start) | collective-permute-done | bytes 131104 | tf_op jit(solution)/shard_map/ppermute | solution.py:532
  57.0 0.0 collective-permute-done.1.bot_ref
  57.0 2.7 %collective-permute-start.2 = (bf16[384,512]{1,0:T(8,128)(2,1)S(1)}, bf16[384,512]{1,0:T(8,128)(2,1)S(1)}, u32[]{:S(2)}, u32[]{:S(2)}) collective-permute-start(bf16[384,512]{1,0:T(8,128)(2,1)S(1)} %pad_maximum_fusion), channel_id=1, source_target_pairs={{0,15},{1,0},{2,1},{3,2},{4,3},{5,4},{6,5},{7,6},{8,7},{9,8},{10,9... | collective-permute-start | bytes 1179656 | tf_op jit(solution)/shard_map/ppermute | solution.py:532
  59.7 0.3 collective-permute-start.3
  60.0 0.0 copy-done.1
  60.0 12.1 %own.1 = (f32[768,1024]{1,0:T(8,128)S(1)}, bf16[640,1024]{1,0:T(8,128)(2,1)S(1)}, bf16[768,2048]{1,0:T(8,128)(2,1)S(1)}, f32[256,1024]{1,0:T(8,128)S(1)}, bf16[2...) custom-call(s32[4]{0:T(128)S(1)} %pad_add_fusion.place_ref, ...), custom_call_target="tpu_custom_call" | custom-call | flops 4831838208 | bytes 12582912 | tf_op jit(solution)/shard_map/own/pallas_call | solution.py:321
  72.2 0.0 collective-permute-done.2.right_ref
  72.2 0.0 collective-permute-done.3.left_ref
  72.2 19.8 %rest.1 = bf16[512,1024]{1,0:T(8,128)(2,1)} custom-call(s32[4]{0:T(128)S(1)} %pad_add_fusion.place_ref, bf16[384,512]{1,0:T(8,128)(2,1)S(1)} %collective-permute-done.2.right_ref, bf16[384,512]{1,0:T(8,128)(2,1)S(1)} %collective-permute-done.3.left_ref, f32[768,1024]{1,0:T(8,128)S(1)} %get-tuple-element.28.stream_ref, ...), custom_call_target="tpu_custom_call" | custom-call | tf_op jit(solution)/shard_map/rest/pallas_call | solution.py:504
  (6 shorter events, 0.1 us)
Async XLA Ops:
  4.8 11.2 %copy-start.2 = (bf16[512,1024]{1,0:T(8,128)(2,1)S(1)}, bf16[512,1024]{1,0:T(8,128)(2,1)}, u32[]{:S(2)}) copy-start(bf16[512,1024]{1,0:T(8,128)(2,1)} %param.14) | copy-start | bytes 3145732
  4.8 43.7 %copy-start = (f32[16,4,128]{2,1,0:T(4,128)S(1)}, f32[16,4,128]{2,1,0:T(4,128)}, u32[]{:S(2)}) copy-start(f32[16,4,128]{2,1,0:T(4,128)} %prof_ref.1) | copy-start | bytes 98308
  4.8 43.6 %all-to-all-start = ((bf16[128,8,1152]{2,1,0:T(8,128)(2,1)}), bf16[128,8,1152]{2,1,0:T(8,128)(2,1)S(1)}, u32[]{:S(2)}, u32[]{:S(2)}) async-start(bf16[128,8,1152]{2,1,0:T(8,128)(2,1)} %bitcast.4), calls=%async_computation | async-start | bytes 4718592 | tf_op jit(solution)/shard_map/all_to_all | solution.py:559
  51.3 8.7 %copy-start.1 = (f32[2,1024]{1,0:T(2,128)S(1)}, f32[2,1024]{1,0:T(2,128)}, u32[]{:S(2)}) copy-start(f32[2,1024]{1,0:T(2,128)} %gain_ref.3) | copy-start | bytes 24580
  51.3 5.6 %collective-permute-start = (bf16[128,512]{1,0:T(8,128)(2,1)S(1)}, bf16[128,512]{1,0:T(8,128)(2,1)S(1)}, u32[]{:S(2)}, u32[]{:S(2)}) collective-permute-start(bf16[128,512]{1,0:T(8,128)(2,1)S(1)} %get-tuple-element.23), channel_id=1, source_target_pairs={{0,16},{16,32},{32,48},{48,64},{64,80},{80,96},{96,112},{112,0},{1... | collective-permute-start | bytes 393224 | tf_op jit(solution)/shard_map/ppermute | solution.py:532
  51.4 5.6 %collective-permute-start.1 = (bf16[128,512]{1,0:T(8,128)(2,1)S(1)}, bf16[128,512]{1,0:T(8,128)(2,1)S(1)}, u32[]{:S(2)}, u32[]{:S(2)}) collective-permute-start(bf16[128,512]{1,0:T(8,128)(2,1)S(1)} %get-tuple-element.25), channel_id=1, source_target_pairs={{0,112},{16,0},{32,16},{48,32},{64,48},{80,64},{96,80},{112,96},{1... | collective-permute-start | bytes 393224 | tf_op jit(solution)/shard_map/ppermute | solution.py:532
  57.0 15.1 %collective-permute-start.2 = (bf16[384,512]{1,0:T(8,128)(2,1)S(1)}, bf16[384,512]{1,0:T(8,128)(2,1)S(1)}, u32[]{:S(2)}, u32[]{:S(2)}) collective-permute-start(bf16[384,512]{1,0:T(8,128)(2,1)S(1)} %pad_maximum_fusion), channel_id=1, source_target_pairs={{0,15},{1,0},{2,1},{3,2},{4,3},{5,4},{6,5},{7,6},{8,7},{9,8},{10,9... | collective-permute-start | bytes 1179656 | tf_op jit(solution)/shard_map/ppermute | solution.py:532
  59.7 12.4 %collective-permute-start.3 = (bf16[384,512]{1,0:T(8,128)(2,1)S(1)}, bf16[384,512]{1,0:T(8,128)(2,1)S(1)}, u32[]{:S(2)}, u32[]{:S(2)}) collective-permute-start(bf16[384,512]{1,0:T(8,128)(2,1)S(1)} %pad_maximum_fusion.1), channel_id=1, source_target_pairs={{0,1},{1,2},{2,3},{3,4},{4,5},{5,6},{6,7},{7,8},{8,9},{9,10},{10,1... | collective-permute-start | bytes 1179656 | tf_op jit(solution)/shard_map/ppermute | solution.py:532
